TPU v7x, 32 devices: a whole 2x2x4 slice. The times are simulated.
32 devices in a mesh: groups: 2 (over x), tensor: 8 (over z, y), seq: 2 (over core).
Axes of the slice: x: 2, y: 2, z: 4, core: 2. Of those that a mesh axis runs over, the one named last changes fastest.
Arguments:
- token_input_rows: bfloat16 [1024, 8192], P(('groups', 'tensor', 'seq')), parts along dimension 0, may hold values from -6 to 6
- base_projection_weight: bfloat16 [8192, 16384], P(None, 'tensor'), may hold values from -0.0625 to 0.0625
- adapter_down_maps: bfloat16 [8, 8192, 64], P('tensor'), may hold values from -0.0625 to 0.0625
- adapter_up_maps: bfloat16 [8, 64, 16384], P('tensor'), may hold values from -0.75 to 0.75
- token_adapter_index: int32 [1024], P(('groups', 'tensor', 'seq')), parts along dimension 0, may hold values from 0 to 7, as said below
- adapter_slot_table: int32 [8], replicated, may hold values from 0 to 7, each once
Outputs:
- projected: bfloat16 [1024, 16384], P(('groups', 'tensor', 'seq')), parts along dimension 0
There are 2 independent parts, one for each index of `groups`. A program takes and returns all parts, laid end to end along the dimension named above; an argument that names none is the same for every part. Nothing has to cross between parts.
Inputs may be any that keep to these rules, and one draw needn't show every extreme that they name: `token_adapter_index`: in each aligned block of 32 tokens (the tokens of one device) every adapter is named at most 5 times; one adapter, the same in every block, is named exactly 5 times in every block. `adapter_slot_table`: each slot is named by exactly one adapter.
All inputs are finite; a program needn't handle non-finite values.
Results may differ from a plain program's by a relative error of at most 0.0057.
Values may be sent and summed in bfloat16 or wider, within the bound.
No kernel may reach another device: no remote copies, remote signals or barrier semaphores. Data moves between devices by JAX's collectives and lax.ppermute only.
A program may use at most 128 MiB of HBM per device.

v0:
```python
import jax
import jax.numpy as jnp
from jax import lax
from jax.sharding import PartitionSpec as P


def body(
    token_input_rows,
    base_projection_weight,
    adapter_down_maps,
    adapter_up_maps,
    token_adapter_index,
    adapter_slot_table,
):
    row_count = token_input_rows.shape[0]
    width = token_input_rows.shape[1]
    tensor_count = lax.axis_size("tensor")
    capacity = max(2, (row_count + tensor_count - 1) // tensor_count + 1)
    partial_rows = jnp.dot(
        lax.all_gather(token_input_rows, "tensor", axis=0, tiled=True),
        base_projection_weight,
        preferred_element_type=jnp.float32,
    ).astype(jnp.bfloat16)
    matches = token_adapter_index[:, None] == jnp.arange(tensor_count, dtype=jnp.int32)[None, :]
    target = jnp.sum(jnp.where(matches, adapter_slot_table[None, :], 0), axis=1)
    token_order = jnp.arange(row_count, dtype=jnp.int32)
    same_target = target[:, None] == target[None, :]
    earlier = token_order[None, :] < token_order[:, None]
    position = jnp.sum(jnp.where(same_target & earlier, 1, 0), axis=1)
    slot_index = target * capacity + position
    placing = (
        slot_index[None, :] == jnp.arange(tensor_count * capacity, dtype=jnp.int32)[:, None]
    ).astype(jnp.bfloat16)
    outgoing = jnp.dot(placing, token_input_rows, preferred_element_type=jnp.float32).astype(
        jnp.bfloat16
    )
    outgoing = outgoing.reshape(tensor_count, capacity, width)
    base_output = lax.all_to_all(partial_rows, "tensor", split_axis=0, concat_axis=1, tiled=True)
    received_rows = lax.all_to_all(outgoing, "tensor", split_axis=0, concat_axis=0, tiled=True)
    flat_rows = received_rows.reshape(-1, width)
    rank_activations = jnp.dot(
        flat_rows, adapter_down_maps[0], preferred_element_type=jnp.float32
    ).astype(jnp.bfloat16)
    adapter_update = jnp.dot(
        rank_activations, adapter_up_maps[0], preferred_element_type=jnp.float32
    ).astype(jnp.bfloat16)
    returned = lax.all_to_all(
        adapter_update.reshape(received_rows.shape[0], received_rows.shape[1], -1),
        "tensor",
        split_axis=0,
        concat_axis=0,
        tiled=True,
    )
    returned = returned.reshape(tensor_count * capacity, -1)
    token_delta = jnp.einsum("st,sf->tf", placing, returned, preferred_element_type=jnp.float32)
    return (base_output.astype(jnp.float32) + token_delta).astype(jnp.bfloat16)


def solution(mesh):
    placed = (
        P(("groups", "tensor", "seq"), None),
        P(None, "tensor"),
        P("tensor", None, None),
        P("tensor", None, None),
        P(("groups", "tensor", "seq")),
        P(),
    )
    return jax.shard_map(
        body,
        mesh=mesh,
        in_specs=placed,
        out_specs=P(("groups", "tensor", "seq"), None),
        check_vma=False,
    )
```

profile of v0, /device:TPU:0, one launch (start us, length us, event | category | flops | bytes accessed | tf_op | source)
XLA Modules:
  0.0 195.4 jit_solution(1013380845442240755)
XLA Ops:
  6.5 0.0 copy-start
  6.5 0.0 all-gather.2.cloned.1.call-start
  6.5 0.7 all-gather.2.cloned.1.call-update
  7.3 0.8 select_reduce_fusion.1
  8.0 0.2 select_reduce_fusion
  8.2 2.2 %convolution_convert_fusion.1 = bf16[40,8192]{1,0:T(8,128)(2,1)} fusion(bf16[32,8192]{1,0:T(8,128)(2,1)} %param.6, s32[32]{0:T(128)S(1)} %multiply_add_fusion), kind=kOutput, calls=%fused_computation.3 | convolution fusion | flops 21300480 | bytes 1179776 | tf_op jit(solution)/shard_map/dot_general | solution.py:34
  10.4 1.4 reshape.27
  11.8 49.8 %all_to_all.23 = bf16[8,5,8192]{2,1,0:T(8,128)(2,1)} all-to-all(bf16[8,5,8192]{2,1,0:T(8,128)(2,1)S(1)} %reshape.27), channel_id=1, replica_groups=mesh['groups'=2,'tensor'=8,'seq'=2] {'tensor'}, dimensions={0} | all-to-all | bytes 1310720 | tf_op jit(solution)/shard_map/all_to_all | solution.py:39
  61.6 2.4 %reshape.28 = bf16[40,8192]{1,0:T(8,128)(2,1)} reshape(bf16[8,5,8192]{2,1,0:T(8,128)(2,1)} %all_to_all.23) | data formatting | bytes 1310720 | tf_op jit(solution)/shard_map/reshape | solution.py:40
  64.0 0.0 copy-done
  64.0 3.1 %convolution_convert_fusion = bf16[40,16384]{1,0:T(8,128)(2,1)S(1)} fusion(bf16[1,64,16384]{2,1,0:T(8,128)(2,1)S(1)} %copy-done, bf16[40,8192]{1,0:T(8,128)(2,1)} %reshape.28, bf16[1,8192,64]{1,2,0:T(8,128)(2,1)} %param.8), kind=kOutput, calls=%fused_computation.1 | convolution fusion | flops 126487040 | bytes 5111808 | tf_op jit(solution)/shard_map/dot_general | solution.py:44
  67.1 1.9 reshape.29
  69.0 4.3 %all-to-all-start.2 = ((bf16[8,5,16384]{2,1,0:T(8,128)(2,1)}), bf16[8,5,16384]{2,1,0:T(8,128)(2,1)}, u32[]{:S(2)}, u32[]{:S(2)}) async-start(bf16[8,5,16384]{2,1,0:T(8,128)(2,1)} %reshape.29), calls=%async_computation.2 | async-start | bytes 4194304 | tf_op jit(solution)/shard_map/all_to_all | solution.py:47
  73.4 64.5 %all-gather.2.cloned.1.call-done = bf16[256,8192]{1,0:T(8,128)(2,1)} async-done(((bf16[32,8192]{1,0:T(8,128)(2,1)}), bf16[256,8192]{1,0:T(8,128)(2,1)}) %all-gather.2.cloned.1.call-update) | async-done | bytes 4194320 | tf_op jit(solution)/shard_map/all_gather | solution.py:20
  137.9 17.0 %convolution_convert_fusion.2 = bf16[256,2048]{1,0:T(8,128)(2,1)} fusion(bf16[256,8192]{1,0:T(8,128)(2,1)} %all-gather.2.cloned.1.call-done, bf16[8192,2048]{1,0:T(8,128)(2,1)} %param.7), kind=kOutput, calls=%fused_computation.4 | convolution fusion | flops 8590458880 | bytes 38797312 | tf_op jit(solution)/shard_map/dot_general | solution.py:19
  154.9 0.0 all-to-all-done.2
  154.9 4.2 %all-to-all-start = ((bf16[8,32,2048]{2,1,0:T(8,128)(2,1)}), bf16[8,32,2048]{2,1,0:T(8,128)(2,1)}, u32[]{:S(2)}, u32[]{:S(2)}) async-start(bf16[8,32,2048]{2,1,0:T(8,128)(2,1)} %bitcast), calls=%async_computation | async-start | bytes 2097152 | tf_op jit(solution)/shard_map/all_to_all | solution.py:38
  159.2 2.2 %reshape.30 = bf16[40,16384]{1,0:T(8,128)(2,1)S(1)} reshape(bf16[8,5,16384]{2,1,0:T(8,128)(2,1)} %all-to-all-done.2) | data formatting | bytes 2621440 | tf_op jit(solution)/shard_map/reshape | solution.py:54
  161.4 24.0 %all-to-all-done = bf16[8,32,2048]{2,1,0:T(8,128)(2,1)} async-done(((bf16[8,32,2048]{2,1,0:T(8,128)(2,1)}), bf16[8,32,2048]{2,1,0:T(8,128)(2,1)}, u32[]{:S(2)}, u32[]{:S(2)}) %all-to-all-start) | async-done | bytes 1048608 | tf_op jit(solution)/shard_map/all_to_all | solution.py:38
  185.3 1.5 convert_bitcast_fusion
  186.8 0.2 copy.10
  187.0 1.5 fusion
  (1 shorter events, 0.0 us)
Async XLA Ops:
  6.5 57.5 %copy-start = (bf16[1,64,16384]{2,1,0:T(8,128)(2,1)S(1)}, bf16[1,64,16384]{2,1,0:T(8,128)(2,1)}, u32[]{:S(2)}) copy-start(bf16[1,64,16384]{2,1,0:T(8,128)(2,1)} %param.9) | copy-start | bytes 6291460
  6.5 131.4 %all-gather.2.cloned.1.call-start = ((), (), s32[]{:S(2)}) async-start(), calls=%async_computation.3 | async-start | bytes 4718592 | tf_op jit(solution)/shard_map/all_gather | solution.py:20
  69.0 85.9 %all-to-all-start.2 = ((bf16[8,5,16384]{2,1,0:T(8,128)(2,1)}), bf16[8,5,16384]{2,1,0:T(8,128)(2,1)}, u32[]{:S(2)}, u32[]{:S(2)}) async-start(bf16[8,5,16384]{2,1,0:T(8,128)(2,1)} %reshape.29), calls=%async_computation.2 | async-start | bytes 4194304 | tf_op jit(solution)/shard_map/all_to_all | solution.py:47
  154.9 30.4 %all-to-all-start = ((bf16[8,32,2048]{2,1,0:T(8,128)(2,1)}), bf16[8,32,2048]{2,1,0:T(8,128)(2,1)}, u32[]{:S(2)}, u32[]{:S(2)}) async-start(bf16[8,32,2048]{2,1,0:T(8,128)(2,1)} %bitcast), calls=%async_computation | async-start | bytes 2097152 | tf_op jit(solution)/shard_map/all_to_all | solution.py:38
Sparse Core Ops, SparseCore 0:
  9.5 128.3 all-gather.1
where the time goes:
time: 196 us; the launch traced here: 195 us
  waiting for transfers between devices  89.2 us (46%)
  blocking collectives  49.8 us (25%)
  matrix products  23.8 us (12%)
  between operations  13.4 us (7%)
  starting transfers between devices  8.58 us (4%)
  local copies, waits for them, and re-layouts  8.14 us (4%)
  other arithmetic  2.4 us (1%)
    all_gather x1, waiting for transfers between devices, body(): lax.all_gather(token_input_rows, 'tensor', axis=0, tiled=True)  64.5 us
    all_to_all x1, blocking collectives, body(): lax.all_to_all(outgoing, 'tensor', split_axis=0, concat_axis=0, tiled=True)  49.8 us
    all_to_all x1, waiting for transfers between devices, body(): lax.all_to_all(partial_rows, 'tensor', split_axis=0, concat_axis=1, tiled...  24 us
    dot_general x1, matrix products, body(): jnp.dot(lax.all_gather(token_input_rows, 'tensor', axis=0, tiled=True), b...  17 us
    all_to_all x1, starting transfers between devices, body(): lax.all_to_all(adapter_update.reshape(received_rows.shape[0], received_ro...  4.34 us
    all_to_all x1, starting transfers between devices, body(): lax.all_to_all(partial_rows, 'tensor', split_axis=0, concat_axis=1, tiled...  4.24 us
  transfers between devices with their start and end apart: 3, of which 2 were waited for; matrix products, arithmetic and copies ran while one was open for 16% of the time, Pallas kernels for 0%

commit v1 on v0

v1 whole, which is shorter than its diff:
```python
import functools

import jax
import jax.numpy as jnp
from jax import lax
from jax.experimental import pallas as pl
from jax.experimental.pallas import tpu as pltpu
from jax.sharding import PartitionSpec as P

BF16 = jnp.bfloat16
F32 = jnp.float32
ANY = pl.BlockSpec(memory_space=pl.ANY)
VMEM = pl.BlockSpec(memory_space=pltpu.VMEM)
SMEM = pl.BlockSpec(memory_space=pltpu.SMEM)


def ring_order(count):
    if count % 2 or count > 8:
        return list(range(count))
    return list(range(0, count, 2)) + list(range(1, count, 2))[::-1]


def fetch_rows(units, place, rows, held, sem):
    return [
        pltpu.make_async_copy(
            unit, held.at[pl.ds(pl.multiple_of(place[j] * rows, rows), rows)], sem.at[j]
        )
        for j, unit in enumerate(units)
    ]


def rank_kernel(count, rows, *refs):
    place, mine = refs[:2]
    units = refs[2 : 2 + count]
    down, slots, out, held, sem = refs[2 + count :]
    copies = fetch_rows(units, place, rows, held, sem)
    for copy in copies:
        copy.start()
    for copy in copies:
        copy.wait()
    low = jnp.dot(held[...], down[...], preferred_element_type=F32)
    out[...] = jnp.where(slots[...] == mine[0], low, 0.0).astype(BF16)


def rank_rows(units, place, mine, down, slots):
    count, rows = len(units), units[0].shape[0]
    width, rank = down.shape
    return pl.pallas_call(
        functools.partial(rank_kernel, count, rows),
        in_specs=[SMEM, SMEM] + [ANY] * count + [VMEM, VMEM],
        out_specs=VMEM,
        out_shape=jax.ShapeDtypeStruct((count * rows, rank), BF16),
        scratch_shapes=[
            pltpu.VMEM((count * rows, width), BF16),
            pltpu.SemaphoreType.DMA((count,)),
        ],
        compiler_params=pltpu.CompilerParams(vmem_limit_bytes=28 << 20),
        cost_estimate=pl.CostEstimate(
            flops=2 * count * rows * width * rank,
            bytes_accessed=2 * width * (count * rows + rank),
            transcendentals=0,
        ),
    )(place, mine, *units, down, slots)


def project_kernel(count, rows, quarters, *refs):
    place, quarter_of = refs[:2]
    units = refs[2 : 2 + count]
    weight = refs[2 + count]
    ups = refs[3 + count : 3 + count + quarters]
    low, slots, out, held, w_held, u_held, x_sem, w_sem, u_sem = refs[3 + count + quarters :]
    columns = weight.shape[1]
    pieces = w_sem.shape[0]
    step = columns // pieces
    rank = low.shape[1]
    per = u_held.shape[0] // quarters
    sub = rank // quarters

    def weight_copy(i):
        at = pl.ds(i * step, step)
        return pltpu.make_async_copy(weight.at[:, at], w_held.at[i], w_sem.at[i])

    x_copies = fetch_rows(units, place, rows, held, x_sem)
    for copy in x_copies:
        copy.start()
    for i in range(pieces):
        weight_copy(i).start()
    u_copies = [
        pltpu.make_async_copy(
            up, u_held.at[pl.ds(pl.multiple_of(quarter_of[j] * per, per), per)], u_sem.at[j]
        )
        for j, up in enumerate(ups)
    ]
    for copy in u_copies:
        copy.start()
    depth = u_held.shape[0]
    at = lax.broadcasted_iota(jnp.int32, (rank, depth), 1)
    entry = lax.broadcasted_iota(jnp.int32, (rank, depth), 0)
    spread = jnp.where(entry == at // per * sub + at % sub, 1.0, 0.0).astype(BF16)
    wide = jnp.dot(low[...], spread, preferred_element_type=F32)
    owner = lax.broadcasted_iota(jnp.int32, wide.shape, 1) % per // sub
    wide = jnp.where(owner == slots[...], wide, 0.0).astype(BF16)
    for copy in x_copies:
        copy.wait()
    for copy in u_copies:
        copy.wait()
    for i in range(pieces):
        cols = slice(i * step, (i + 1) * step)
        weight_copy(i).wait()
        base = jnp.dot(held[...], w_held[i], preferred_element_type=F32).astype(BF16)
        delta = jnp.dot(wide, u_held[:, cols], preferred_element_type=F32).astype(BF16)
        out[:, cols] = (base.astype(F32) + delta.astype(F32)).astype(BF16)


def project(units, place, weight, ups, quarter_of, low, slots):
    count, rows = len(units), units[0].shape[0]
    width, columns = weight.shape
    quarters = len(ups)
    depth = sum(u.shape[0] for u in ups)
    pieces = max(1, columns // 256)
    total = count * rows
    return pl.pallas_call(
        functools.partial(project_kernel, count, rows, quarters),
        in_specs=[SMEM, SMEM] + [ANY] * (count + 1 + quarters) + [VMEM, VMEM],
        out_specs=VMEM,
        out_shape=jax.ShapeDtypeStruct((total, columns), BF16),
        scratch_shapes=[
            pltpu.VMEM((total, width), BF16),
            pltpu.VMEM((pieces, width, columns // pieces), BF16),
            pltpu.VMEM((depth, columns), BF16),
            pltpu.SemaphoreType.DMA((count,)),
            pltpu.SemaphoreType.DMA((pieces,)),
            pltpu.SemaphoreType.DMA((quarters,)),
        ],
        compiler_params=pltpu.CompilerParams(vmem_limit_bytes=48 << 20),
        cost_estimate=pl.CostEstimate(
            flops=2 * total * width * columns,
            bytes_accessed=2 * width * (columns + total),
            transcendentals=0,
        ),
    )(place, quarter_of, *units, weight, *ups, low, slots)


def body(
    token_input_rows,
    base_projection_weight,
    adapter_down_maps,
    adapter_up_maps,
    token_adapter_index,
    adapter_slot_table,
):
    count = lax.axis_size("tensor")
    groups, seqs = lax.axis_size("groups"), lax.axis_size("seq")
    me = lax.axis_index("tensor")
    replica = lax.axis_index("groups") * seqs + lax.axis_index("seq")
    rows, width = token_input_rows.shape
    half = rows // 2
    columns = base_projection_weight.shape[1]
    rank = adapter_up_maps.shape[1]

    order = ring_order(count)
    place_of = [order.index(t) for t in range(count)]
    ahead = [(order[p], order[(p + 1) % count]) for p in range(count)]
    behind = [(b, a) for a, b in ahead]

    far = count // 2
    first, second = token_input_rows[:half], token_input_rows[half:]
    chains = [[[first], [first]], [[second], [second]]]
    for k in range(1, far + 1):
        for h in range(2):
            for way, pairs in enumerate((ahead, behind)):
                if k < far or way == h:
                    chains[h][way].append(lax.ppermute(chains[h][way][-1], "tensor", pairs))
    units = []
    for h in range(2):
        held = [chains[h][0][0]]
        for k in range(1, far + 1):
            held += [chains[h][way][k] for way in range(2) if k < len(chains[h][way])]
        units.append(held)
    position = jnp.asarray(place_of, jnp.int32)[me]
    order_array = jnp.asarray(order, jnp.int32)

    def offsets(h):
        found = [0]
        for k in range(1, far + 1):
            found += [(-k, k)[way] for way in range(2) if k < len(chains[h][way])]
        return jnp.asarray(found, jnp.int32)

    places = [order_array[(position + offsets(h)) % count] for h in range(2)]

    replicas = groups * seqs
    sub = rank // replicas
    share = lax.dynamic_slice_in_dim(adapter_up_maps[0], replica * sub, sub, 0)
    share = share.reshape(sub, count, columns).transpose(1, 0, 2)
    share = lax.all_to_all(share, "tensor", split_axis=0, concat_axis=0, tiled=True)
    ups = [share.reshape(count * sub, columns)]
    bit = 1
    while bit < replicas:
        axis, size, flip = ("seq", seqs, bit) if bit < seqs else ("groups", groups, bit // seqs)
        pairs = [(i, i ^ flip) for i in range(size)]
        ups += [lax.ppermute(u, axis, pairs) for u in ups]
        bit *= 2
    quarter_of = replica ^ jnp.arange(replicas, dtype=jnp.int32)

    indices = lax.all_gather(token_adapter_index, "tensor", axis=0, tiled=False)
    matches = indices[:, :, None] == jnp.arange(count, dtype=jnp.int32)
    slots = jnp.sum(jnp.where(matches, adapter_slot_table, 0), axis=2)
    slots = [slots[:, :half].reshape(-1, 1), slots[:, half:].reshape(-1, 1)]

    parts = []
    for h in range(2):
        low = rank_rows(
            units[h], places[h], me.astype(jnp.int32)[None], adapter_down_maps[0], slots[h]
        )
        bit = 1
        while bit < count:
            low = low + lax.ppermute(low, "tensor", [(t, t ^ bit) for t in range(count)])
            bit *= 2
        result = project(
            units[h], places[h], base_projection_weight, ups, quarter_of, low, slots[h]
        )
        parts.append(
            lax.all_to_all(
                result.reshape(count, half, columns), "tensor", split_axis=0, concat_axis=0, tiled=True
            )
        )
    parts = [p.transpose(1, 0, 2).reshape(half, -1) for p in parts]
    return jnp.concatenate(parts, axis=0)


def solution(mesh):
    placed = (
        P(("groups", "tensor", "seq"), None),
        P(None, "tensor"),
        P("tensor", None, None),
        P("tensor", None, None),
        P(("groups", "tensor", "seq")),
        P(),
    )
    return jax.shard_map(
        body,
        mesh=mesh,
        in_specs=placed,
        out_specs=P(("groups", "tensor", "seq"), None),
        check_vma=False,
    )
```

time: 196 us -> 176 us (0.90)
  Pallas kernels: 0 us -> 50.6 us
  blocking collectives: 49.8 us -> 13.8 us
  waiting for transfers between devices: 89.2 us -> 53.6 us
  starting transfers between devices: 8.58 us -> 39.5 us
  matrix products: 23.8 us -> 0 us
  between operations: 13.4 us -> 0.98 us
  local copies, waits for them, and re-layouts: 8.14 us -> 15 us
    all_gather x1 -> x0, waiting for transfers between devices: 64.5 us -> none  [body(): lax.all_gather(token_input_rows, 'tensor', axis=0, tiled=True)]
    pallas_call x0 -> x4, Pallas kernels: none -> 50.6 us  [the longest x2 45.2 us: project(): pl.pallas_call(functools.partial(project_kernel, count, rows, quarters),...]
    all_to_all x1 -> x0, blocking collectives: 49.8 us -> none  [body(): lax.all_to_all(outgoing, 'tensor', split_axis=0, concat_axis=0, tiled=True)]
    ppermute x0 -> x23, waiting for transfers between devices: none -> 31.8 us  [the longest x6 19.2 us: body(): lax.ppermute(low, 'tensor', [(t, t ^ bit) for t in range(count)])]
    ppermute x0 -> x23, starting transfers between devices: none -> 23.9 us  [the longest x14 16.8 us: body(): chains[h][way].append(lax.ppermute(chains[h][way][-1], 'tensor', pairs))]
    dot_general x4 -> x0, matrix products: 23.8 us -> none  [the longest x1 17 us: body(): jnp.dot(lax.all_gather(token_input_rows, 'tensor', axis=0, tiled=True), b...]
    unnamed x0 -> x1, blocking collectives: none -> 13.8 us
    unnamed x2 -> x27, local copies, waits for them, and re-layouts: 0.01 us -> 9.49 us
  transfers between devices with their start and end apart: 3 -> 26, of which waited for: 2 -> 11; matrix products, arithmetic and copies ran while one was open for 16% -> 5% of each run, Pallas kernels for 0% -> 29%
where the time goes in v1:
time: 176 us; the launch traced here: 175 us
  waiting for transfers between devices  53.6 us (30%)
  Pallas kernels  50.6 us (29%)
  starting transfers between devices  39.5 us (22%)
  local copies, waits for them, and re-layouts  15 us (9%)
  blocking collectives  13.8 us (8%)
  other arithmetic  1.79 us (1%)
    pallas_call x2, Pallas kernels, project(): pl.pallas_call(functools.partial(project_kernel, count, rows, quarters),...  45.2 us
    ppermute x6, waiting for transfers between devices, body(): lax.ppermute(low, 'tensor', [(t, t ^ bit) for t in range(count)])  19.2 us
    ppermute x14, starting transfers between devices, body(): chains[h][way].append(lax.ppermute(chains[h][way][-1], 'tensor', pairs))  16.8 us
    unnamed x1, blocking collectives  13.8 us
    all_to_all x1, waiting for transfers between devices, body(): lax.all_to_all(share, 'tensor', split_axis=0, concat_axis=0, tiled=True)  12.7 us
    ppermute x14, waiting for transfers between devices, body(): chains[h][way].append(lax.ppermute(chains[h][way][-1], 'tensor', pairs))  12.5 us
    unnamed x27, local copies, waits for them, and re-layouts  9.49 us
    all_to_all x2, waiting for transfers between devices, body(): lax.all_to_all(result.reshape(count, half, columns), 'tensor', split_axis...  9.2 us
  transfers between devices with their start and end apart: 26, of which 11 were waited for; matrix products, arithmetic and copies ran while one was open for 5% of the time, Pallas kernels for 29%

profile of v1, /device:TPU:0, one launch (start us, length us, event | category | flops | bytes accessed | tf_op | source)
XLA Modules:
  0.0 175.3 jit_solution(8802604760999823753)
XLA Ops:
  0.0 1.6 copy-done
  1.7 0.3 copy.44
  2.0 1.1 copy.34
  3.1 7.3 %all-to-all-start = ((bf16[8,16,2048]{2,1,0:T(8,128)(2,1)}), bf16[8,16,2048]{2,1,0:T(8,128)(2,1)S(1)}, u32[]{:S(2)}, u32[]{:S(2)}) async-start(bf16[8,16,2048]{2,1,0:T(8,128)(2,1)} %copy.34), calls=%async_computation | async-start | bytes 1048576 | tf_op jit(solution)/shard_map/all_to_all | solution.py:195
  10.4 1.1 fusion.2
  11.5 2.1 %collective-permute-start = (bf16[16,8192]{1,0:T(8,128)(2,1)S(1)}, bf16[16,8192]{1,0:T(8,128)(2,1)}, u32[]{:S(2)}, u32[]{:S(2)}) collective-permute-start(bf16[16,8192]{1,0:T(8,128)(2,1)S(1)} %get-tuple-element.5.refs_2_), channel_id=1, source_target_pairs={{0,4},{4,8},{8,12},{12,14},{14,10},{10,6},{6,2},{2,0},{1,5},{5,9},... | collective-permute-start | bytes 786440 | tf_op jit(solution)/shard_map/ppermute | solution.py:173
  13.6 12.7 %all-to-all-done = bf16[8,16,2048]{2,1,0:T(8,128)(2,1)S(1)} async-done(((bf16[8,16,2048]{2,1,0:T(8,128)(2,1)}), bf16[8,16,2048]{2,1,0:T(8,128)(2,1)S(1)}, u32[]{:S(2)}, u32[]{:S(2)}) %all-to-all-start) | async-done | bytes 524320 | tf_op jit(solution)/shard_map/all_to_all | solution.py:195
  26.3 2.5 %collective-permute-start.2 = (bf16[16,8192]{1,0:T(8,128)(2,1)}, bf16[16,8192]{1,0:T(8,128)(2,1)}, u32[]{:S(2)}, u32[]{:S(2)}) collective-permute-start(bf16[16,8192]{1,0:T(8,128)(2,1)} %collective-permute-done.refs_3_), channel_id=1, source_target_pairs={{0,4},{4,8},{8,12},{12,14},{14,10},{10,6},{6,2},{2,0},{1,5},{5,9},... | collective-permute-start | bytes 786440 | tf_op jit(solution)/shard_map/ppermute | solution.py:173
  28.8 3.8 %collective-permute-start.14 = (bf16[16,8192]{1,0:T(8,128)(2,1)S(1)}, bf16[16,8192]{1,0:T(8,128)(2,1)S(1)}, u32[]{:S(2)}, u32[]{:S(2)}) collective-permute-start(bf16[16,8192]{1,0:T(8,128)(2,1)S(1)} %get-tuple-element.6.refs_2_), channel_id=1, source_target_pairs={{4,0},{8,4},{12,8},{14,12},{10,14},{6,10},{2,6},{0,2},{5,1},{9,5},... | collective-permute-start | bytes 786440 | tf_op jit(solution)/shard_map/ppermute | solution.py:173
  32.6 0.6 dynamic-slice.1
  34.1 13.8 %all-reduce = s32[256]{0:T(256)S(1)} all-reduce(s32[256]{0:T(256)S(1)} %dynamic-update-slice), channel_id=2, replica_groups=mesh['groups'=2,'tensor'=8,'seq'=2] {'tensor'}, use_global_device_ids=true, to_apply=%add | all-reduce | flops 256 | bytes 2048
  48.1 2.1 %collective-permute-start.5 = (bf16[16,8192]{1,0:T(8,128)(2,1)}, bf16[16,8192]{1,0:T(8,128)(2,1)}, u32[]{:S(2)}, u32[]{:S(2)}) collective-permute-start(bf16[16,8192]{1,0:T(8,128)(2,1)} %collective-permute-done.3.refs_6_), channel_id=1, source_target_pairs={{4,0},{8,4},{12,8},{14,12},{10,14},{6,10},{2,6},{0,2},{5,1},{9,5},... | collective-permute-start | bytes 786440 | tf_op jit(solution)/shard_map/ppermute | solution.py:173
  50.1 1.5 collective-permute-start.8
  51.6 0.5 collective-permute-start.9
  52.3 2.7 %copy.35 = bf16[1,8192,64]{2,1,0:T(8,128)(2,1)} copy(bf16[1,8192,64]{1,2,0:T(8,128)(2,1)} %param.12) | data formatting | bytes 2097152 | tf_op args[2]
  55.1 0.6 dynamic_slice.6
  55.7 0.6 compare_select_fusion
  56.3 0.3 collective-permute-start.13
  56.6 1.8 %collective-permute-start.16 = (bf16[16,8192]{1,0:T(8,128)(2,1)S(1)}, bf16[16,8192]{1,0:T(8,128)(2,1)}, u32[]{:S(2)}, u32[]{:S(2)}) collective-permute-start(bf16[16,8192]{1,0:T(8,128)(2,1)S(1)} %collective-permute-done.14.refs_4_), channel_id=1, source_target_pairs={{4,0},{8,4},{12,8},{14,12},{10,14},{6,10},{2,6},{0,2},{5,1},{9,5},... | collective-permute-start | bytes 786440 | tf_op jit(solution)/shard_map/ppermute | solution.py:173
  58.4 0.6 gather_fusion
  59.1 4.0 %collective-permute-done.6.refs_9_ = bf16[16,8192]{1,0:T(8,128)(2,1)} collective-permute-done((bf16[16,8192]{1,0:T(8,128)(2,1)}, bf16[16,8192]{1,0:T(8,128)(2,1)}, u32[]{:S(2)}, u32[]{:S(2)}) %collective-permute-start.6) | collective-permute-done | bytes 262176 | tf_op jit(solution)/shard_map/ppermute | solution.py:173
  63.1 1.6 copy-done.1
  64.7 2.8 %shard_map.100 = bf16[128,64]{1,0:T(8,128)(2,1)S(1)} custom-call(s32[8]{0:T(128)S(1)} %gather_fusion, s32[1]{0:T(128)} %bitcast.3.refs_1_, bf16[16,8192]{1,0:T(8,128)(2,1)S(1)} %get-tuple-element.5.refs_2_, bf16[16,8192]{1,0:T(8,128)(2,1)} %collective-permute-done.refs_3_, bf16[16,8192]{1,0:T(8,128)(2,1)} %collective-permute-done.1.refs_4_, ...), custom_call_target="tpu_custom_call" | custom-call | flops 134217728 | bytes 3145728 | tf_op jit(solution)/shard_map/pallas_call | solution.py:48
  67.5 3.9 %collective-permute-done.10 = bf16[128,64]{1,0:T(8,128)(2,1)S(1)} collective-permute-done((bf16[128,64]{1,0:T(8,128)(2,1)S(1)}, bf16[128,64]{1,0:T(8,128)(2,1)S(1)}, u32[]{:S(2)}, u32[]{:S(2)}) %collective-permute-start.10) | collective-permute-done | bytes 16416 | tf_op jit(solution)/shard_map/ppermute | solution.py:217
  71.5 4.3 %collective-permute-done.11 = bf16[128,64]{1,0:T(8,128)(2,1)S(1)} collective-permute-done((bf16[128,64]{1,0:T(8,128)(2,1)S(1)}, bf16[128,64]{1,0:T(8,128)(2,1)S(1)}, u32[]{:S(2)}, u32[]{:S(2)}) %collective-permute-start.11) | collective-permute-done | bytes 16416 | tf_op jit(solution)/shard_map/ppermute | solution.py:217
  76.0 1.6 collective-permute-start.15
  77.6 0.5 collective-permute-start.18
  78.0 2.7 %collective-permute-done.12 = bf16[128,64]{1,0:T(8,128)(2,1)S(1)} collective-permute-done((bf16[128,64]{1,0:T(8,128)(2,1)S(1)}, bf16[128,64]{1,0:T(8,128)(2,1)S(1)}, u32[]{:S(2)}, u32[]{:S(2)}) %collective-permute-start.12) | collective-permute-done | bytes 16416 | tf_op jit(solution)/shard_map/ppermute | solution.py:217
  80.8 22.3 %shard_map.101 = bf16[128,2048]{1,0:T(8,128)(2,1)S(1)} custom-call(s32[8]{0:T(128)S(1)} %gather_fusion, s32[4]{0:T(128)S(1)} %iota_xor_fusion.refs_1_, bf16[16,8192]{1,0:T(8,128)(2,1)S(1)} %get-tuple-element.5.refs_2_, bf16[16,8192]{1,0:T(8,128)(2,1)} %collective-permute-done.refs_3_, bf16[16,8192]{1,0:T(8,128)(2,1)} %collective-permute-done.1.refs_4_, ...), custom_call_target="tpu_custom_call" | custom-call | flops 4294967296 | bytes 35651584 | tf_op jit(solution)/shard_map/pallas_call | solution.py:122
  103.1 0.8 copy-done.3
  103.9 4.1 %all-to-all-start.1 = ((bf16[8,16,2048]{2,1,0:T(8,128)(2,1)}), bf16[8,16,2048]{2,1,0:T(8,128)(2,1)}, u32[]{:S(2)}, u32[]{:S(2)}) async-start(bf16[8,16,2048]{2,1,0:T(8,128)(2,1)} %bitcast.24), calls=%async_computation.1 | async-start | bytes 1048576 | tf_op jit(solution)/shard_map/all_to_all | solution.py:223
  108.0 1.9 %collective-permute-start.17 = (bf16[16,8192]{1,0:T(8,128)(2,1)}, bf16[16,8192]{1,0:T(8,128)(2,1)S(1)}, u32[]{:S(2)}, u32[]{:S(2)}) collective-permute-start(bf16[16,8192]{1,0:T(8,128)(2,1)} %collective-permute-done.15.refs_5_), channel_id=1, source_target_pairs={{0,4},{4,8},{8,12},{12,14},{14,10},{10,6},{6,2},{2,0},{1,5},{5,9},... | collective-permute-start | bytes 786440 | tf_op jit(solution)/shard_map/ppermute | solution.py:173
  110.2 0.6 gather_fusion.1
  110.9 5.7 %collective-permute-done.17.refs_7_ = bf16[16,8192]{1,0:T(8,128)(2,1)S(1)} collective-permute-done((bf16[16,8192]{1,0:T(8,128)(2,1)}, bf16[16,8192]{1,0:T(8,128)(2,1)S(1)}, u32[]{:S(2)}, u32[]{:S(2)}) %collective-permute-start.17) | collective-permute-done | bytes 262176 | tf_op jit(solution)/shard_map/ppermute | solution.py:173
  116.6 2.9 %collective-permute-done.19.refs_9_ = bf16[16,8192]{1,0:T(8,128)(2,1)} collective-permute-done((bf16[16,8192]{1,0:T(8,128)(2,1)}, bf16[16,8192]{1,0:T(8,128)(2,1)}, u32[]{:S(2)}, u32[]{:S(2)}) %collective-permute-start.19) | collective-permute-done | bytes 262176 | tf_op jit(solution)/shard_map/ppermute | solution.py:173
  119.4 1.6 copy-done.2
  121.0 2.6 %shard_map.102 = bf16[128,64]{1,0:T(8,128)(2,1)S(1)} custom-call(s32[8]{0:T(128)S(1)} %gather_fusion.1, s32[1]{0:T(128)} %bitcast.3.refs_1_, bf16[16,8192]{1,0:T(8,128)(2,1)S(1)} %get-tuple-element.6.refs_2_, bf16[16,8192]{1,0:T(8,128)(2,1)} %collective-permute-done.13.refs_3_, bf16[16,8192]{1,0:T(8,128)(2,1)S(1)} %collective-permute-done.14.refs_4_, ...), custom_call_target="tpu_custom_call" | custom-call | flops 134217728 | bytes 3145728 | tf_op jit(solution)/shard_map/pallas_call | solution.py:48
  123.7 0.8 collective-permute-start.20
  124.5 3.1 %collective-permute-done.20 = bf16[128,64]{1,0:T(8,128)(2,1)S(1)} collective-permute-done((bf16[128,64]{1,0:T(8,128)(2,1)S(1)}, bf16[128,64]{1,0:T(8,128)(2,1)S(1)}, u32[]{:S(2)}, u32[]{:S(2)}) %collective-permute-start.20) | collective-permute-done | bytes 16416 | tf_op jit(solution)/shard_map/ppermute | solution.py:217
  127.7 2.4 %collective-permute-start.21 = (bf16[128,64]{1,0:T(8,128)(2,1)S(1)}, bf16[128,64]{1,0:T(8,128)(2,1)S(1)}, u32[]{:S(2)}, u32[]{:S(2)}) collective-permute-start(bf16[128,64]{1,0:T(8,128)(2,1)S(1)} %add.66), channel_id=1, source_target_pairs={{0,4},{2,6},{4,0},{6,2},{8,12},{10,14},{12,8},{14,10},{1,5},{3,7},... | collective-permute-start | bytes 49160 | tf_op jit(solution)/shard_map/ppermute | solution.py:217
  130.0 1.9 %collective-permute-done.21 = bf16[128,64]{1,0:T(8,128)(2,1)S(1)} collective-permute-done((bf16[128,64]{1,0:T(8,128)(2,1)S(1)}, bf16[128,64]{1,0:T(8,128)(2,1)S(1)}, u32[]{:S(2)}, u32[]{:S(2)}) %collective-permute-start.21) | collective-permute-done | bytes 16416 | tf_op jit(solution)/shard_map/ppermute | solution.py:217
  131.9 1.6 collective-permute-start.22
  133.5 3.3 %collective-permute-done.22 = bf16[128,64]{1,0:T(8,128)(2,1)S(1)} collective-permute-done((bf16[128,64]{1,0:T(8,128)(2,1)S(1)}, bf16[128,64]{1,0:T(8,128)(2,1)S(1)}, u32[]{:S(2)}, u32[]{:S(2)}) %collective-permute-start.22) | collective-permute-done | bytes 16416 | tf_op jit(solution)/shard_map/ppermute | solution.py:217
  136.8 22.9 %shard_map.103 = bf16[128,2048]{1,0:T(8,128)(2,1)} custom-call(s32[8]{0:T(128)S(1)} %gather_fusion.1, s32[4]{0:T(128)S(1)} %iota_xor_fusion.refs_1_, bf16[16,8192]{1,0:T(8,128)(2,1)S(1)} %get-tuple-element.6.refs_2_, bf16[16,8192]{1,0:T(8,128)(2,1)} %collective-permute-done.13.refs_3_, bf16[16,8192]{1,0:T(8,128)(2,1)S(1)} %collective-permute-done.14.refs_4_, ...), custom_call_target="tpu_custom_call" | custom-call | flops 4294967296 | bytes 35651584 | tf_op jit(solution)/shard_map/pallas_call | solution.py:122
  159.8 4.2 %all-to-all-start.2 = ((bf16[8,16,2048]{2,1,0:T(8,128)(2,1)}), bf16[8,16,2048]{2,1,0:T(8,128)(2,1)S(1)}, u32[]{:S(2)}, u32[]{:S(2)}) async-start(bf16[8,16,2048]{2,1,0:T(8,128)(2,1)} %bitcast.8), calls=%async_computation.2 | async-start | bytes 1048576 | tf_op jit(solution)/shard_map/all_to_all | solution.py:223
  164.0 1.1 copy.42
  165.1 9.2 %all-to-all-done.2 = bf16[8,16,2048]{2,1,0:T(8,128)(2,1)S(1)} async-done(((bf16[8,16,2048]{2,1,0:T(8,128)(2,1)}), bf16[8,16,2048]{2,1,0:T(8,128)(2,1)S(1)}, u32[]{:S(2)}, u32[]{:S(2)}) %all-to-all-start.2) | async-done | bytes 524320 | tf_op jit(solution)/shard_map/all_to_all | solution.py:223
  174.3 1.0 pad_maximum_fusion
  (60 shorter events, 1.4 us)
Async XLA Ops:
  0.0 1.6 copy-start
  1.6 31.0 %copy-start.10 = (u32[32]{0:T(128)S(1)}, u32[32]{0:T(128)}, u32[]{:S(2)}) copy-start(u32[32]{0:T(128)} %constant.58) | copy-start | bytes 388
  1.6 32.2 %copy-start.8 = (s32[32]{0:T(128)S(1)}, s32[32]{0:T(128)}, u32[]{:S(2)}) copy-start(s32[32]{0:T(128)} %param.14) | copy-start | bytes 388
  1.7 46.3 %copy-start.5 = (s32[8]{0:T(128)S(1)}, s32[8]{0:T(128)}, u32[]{:S(2)}) copy-start(s32[8]{0:T(128)} %param.15) | copy-start | bytes 100
  3.1 23.2 %all-to-all-start = ((bf16[8,16,2048]{2,1,0:T(8,128)(2,1)}), bf16[8,16,2048]{2,1,0:T(8,128)(2,1)S(1)}, u32[]{:S(2)}, u32[]{:S(2)}) async-start(bf16[8,16,2048]{2,1,0:T(8,128)(2,1)} %copy.34), calls=%async_computation | async-start | bytes 1048576 | tf_op jit(solution)/shard_map/all_to_all | solution.py:195
  10.3 44.7 %copy-start.9 = (s32[8]{0:T(128)S(1)}, s32[8]{0:T(128)}, u32[]{:S(2)}) copy-start(s32[8]{0:T(128)} %constant.50.clone) | copy-start | bytes 100
  10.3 45.3 %copy-start.6 = (s32[8]{0:T(128)S(1)}, s32[8]{0:T(128)}, u32[]{:S(2)}) copy-start(s32[8]{0:T(128)} %constant.52.clone) | copy-start | bytes 100
  10.4 45.3 %copy-start.7 = (s32[8]{0:T(128)S(1)}, s32[8]{0:T(128)}, u32[]{:S(2)}) copy-start(s32[8]{0:T(128)} %constant.53.clone) | copy-start | bytes 100
  10.4 48.1 %copy-start.4 = (s32[8]{0:T(128)S(1)}, s32[8]{0:T(128)}, u32[]{:S(2)}) copy-start(s32[8]{0:T(128)} %constant.51.clone) | copy-start | bytes 100
  11.5 14.8 %collective-permute-start = (bf16[16,8192]{1,0:T(8,128)(2,1)S(1)}, bf16[16,8192]{1,0:T(8,128)(2,1)}, u32[]{:S(2)}, u32[]{:S(2)}) collective-permute-start(bf16[16,8192]{1,0:T(8,128)(2,1)S(1)} %get-tuple-element.5.refs_2_), channel_id=1, source_target_pairs={{0,4},{4,8},{8,12},{12,14},{14,10},{10,6},{6,2},{2,0},{1,5},{5,9},... | collective-permute-start | bytes 786440 | tf_op jit(solution)/shard_map/ppermute | solution.py:173
  13.5 15.3 %collective-permute-start.1 = (bf16[16,8192]{1,0:T(8,128)(2,1)S(1)}, bf16[16,8192]{1,0:T(8,128)(2,1)}, u32[]{:S(2)}, u32[]{:S(2)}) collective-permute-start(bf16[16,8192]{1,0:T(8,128)(2,1)S(1)} %get-tuple-element.5.refs_2_), channel_id=1, source_target_pairs={{4,0},{8,4},{12,8},{14,12},{10,14},{6,10},{2,6},{0,2},{5,1},{9,5},... | collective-permute-start | bytes 786440 | tf_op jit(solution)/shard_map/ppermute | solution.py:173
  26.3 25.3 %collective-permute-start.7 = (bf16[128,2048]{1,0:T(8,128)(2,1)S(1)}, bf16[128,2048]{1,0:T(8,128)(2,1)}, u32[]{:S(2)}, u32[]{:S(2)}) collective-permute-start(bf16[128,2048]{1,0:T(8,128)(2,1)S(1)} %bitcast.20), channel_id=1, source_target_pairs={{0,1},{1,0},{2,3},{3,2},{4,5},{5,4},{6,7},{7,6},{8,9},{9,8},{10,11... | collective-permute-start | bytes 1572872 | tf_op jit(solution)/shard_map/ppermute | solution.py:201
  26.3 21.7 %collective-permute-start.2 = (bf16[16,8192]{1,0:T(8,128)(2,1)}, bf16[16,8192]{1,0:T(8,128)(2,1)}, u32[]{:S(2)}, u32[]{:S(2)}) collective-permute-start(bf16[16,8192]{1,0:T(8,128)(2,1)} %collective-permute-done.refs_3_), channel_id=1, source_target_pairs={{0,4},{4,8},{8,12},{12,14},{14,10},{10,6},{6,2},{2,0},{1,5},{5,9},... | collective-permute-start | bytes 786440 | tf_op jit(solution)/shard_map/ppermute | solution.py:173
  28.8 19.2 %collective-permute-start.3 = (bf16[16,8192]{1,0:T(8,128)(2,1)}, bf16[16,8192]{1,0:T(8,128)(2,1)}, u32[]{:S(2)}, u32[]{:S(2)}) collective-permute-start(bf16[16,8192]{1,0:T(8,128)(2,1)} %collective-permute-done.1.refs_4_), channel_id=1, source_target_pairs={{4,0},{8,4},{12,8},{14,12},{10,14},{6,10},{2,6},{0,2},{5,1},{9,5},... | collective-permute-start | bytes 786440 | tf_op jit(solution)/shard_map/ppermute | solution.py:173
  28.8 27.5 %collective-permute-start.14 = (bf16[16,8192]{1,0:T(8,128)(2,1)S(1)}, bf16[16,8192]{1,0:T(8,128)(2,1)S(1)}, u32[]{:S(2)}, u32[]{:S(2)}) collective-permute-start(bf16[16,8192]{1,0:T(8,128)(2,1)S(1)} %get-tuple-element.6.refs_2_), channel_id=1, source_target_pairs={{4,0},{8,4},{12,8},{14,12},{10,14},{6,10},{2,6},{0,2},{5,1},{9,5},... | collective-permute-start | bytes 786440 | tf_op jit(solution)/shard_map/ppermute | solution.py:173
  48.0 7.7 %collective-permute-start.4 = (bf16[16,8192]{1,0:T(8,128)(2,1)}, bf16[16,8192]{1,0:T(8,128)(2,1)}, u32[]{:S(2)}, u32[]{:S(2)}) collective-permute-start(bf16[16,8192]{1,0:T(8,128)(2,1)} %collective-permute-done.2.refs_5_), channel_id=1, source_target_pairs={{0,4},{4,8},{8,12},{12,14},{14,10},{10,6},{6,2},{2,0},{1,5},{5,9},... | collective-permute-start | bytes 786440 | tf_op jit(solution)/shard_map/ppermute | solution.py:173
  48.1 8.5 %collective-permute-start.5 = (bf16[16,8192]{1,0:T(8,128)(2,1)}, bf16[16,8192]{1,0:T(8,128)(2,1)}, u32[]{:S(2)}, u32[]{:S(2)}) collective-permute-start(bf16[16,8192]{1,0:T(8,128)(2,1)} %collective-permute-done.3.refs_6_), channel_id=1, source_target_pairs={{4,0},{8,4},{12,8},{14,12},{10,14},{6,10},{2,6},{0,2},{5,1},{9,5},... | collective-permute-start | bytes 786440 | tf_op jit(solution)/shard_map/ppermute | solution.py:173
  50.1 30.6 %collective-permute-start.8 = (bf16[128,2048]{1,0:T(8,128)(2,1)S(1)}, bf16[128,2048]{1,0:T(8,128)(2,1)}, u32[]{:S(2)}, u32[]{:S(2)}) collective-permute-start(bf16[128,2048]{1,0:T(8,128)(2,1)S(1)} %bitcast.21), channel_id=1, source_target_pairs={{0,16},{16,0},{1,17},{17,1},{2,18},{18,2},{3,19},{19,3},{4,20},{20... | collective-permute-start | bytes 1572872 | tf_op jit(solution)/shard_map/ppermute | solution.py:201
  51.6 29.1 %collective-permute-start.9 = (bf16[128,2048]{1,0:T(8,128)(2,1)}, bf16[128,2048]{1,0:T(8,128)(2,1)}, u32[]{:S(2)}, u32[]{:S(2)}) collective-permute-start(bf16[128,2048]{1,0:T(8,128)(2,1)} %collective-permute-done.7.refs_12_), channel_id=1, source_target_pairs={{0,16},{16,0},{1,17},{17,1},{2,18},{18,2},{3,19},{19,3},{4,20},{20... | collective-permute-start | bytes 1572872 | tf_op jit(solution)/shard_map/ppermute | solution.py:201
  55.7 7.4 %collective-permute-start.6 = (bf16[16,8192]{1,0:T(8,128)(2,1)}, bf16[16,8192]{1,0:T(8,128)(2,1)}, u32[]{:S(2)}, u32[]{:S(2)}) collective-permute-start(bf16[16,8192]{1,0:T(8,128)(2,1)} %collective-permute-done.4.refs_7_), channel_id=1, source_target_pairs={{0,4},{4,8},{8,12},{12,14},{14,10},{10,6},{6,2},{2,0},{1,5},{5,9},... | collective-permute-start | bytes 786440 | tf_op jit(solution)/shard_map/ppermute | solution.py:173
  56.3 19.7 %collective-permute-start.13 = (bf16[16,8192]{1,0:T(8,128)(2,1)S(1)}, bf16[16,8192]{1,0:T(8,128)(2,1)}, u32[]{:S(2)}, u32[]{:S(2)}) collective-permute-start(bf16[16,8192]{1,0:T(8,128)(2,1)S(1)} %get-tuple-element.6.refs_2_), channel_id=1, source_target_pairs={{0,4},{4,8},{8,12},{12,14},{14,10},{10,6},{6,2},{2,0},{1,5},{5,9},... | collective-permute-start | bytes 786440 | tf_op jit(solution)/shard_map/ppermute | solution.py:173
  56.6 21.0 %collective-permute-start.16 = (bf16[16,8192]{1,0:T(8,128)(2,1)S(1)}, bf16[16,8192]{1,0:T(8,128)(2,1)}, u32[]{:S(2)}, u32[]{:S(2)}) collective-permute-start(bf16[16,8192]{1,0:T(8,128)(2,1)S(1)} %collective-permute-done.14.refs_4_), channel_id=1, source_target_pairs={{4,0},{8,4},{12,8},{14,12},{10,14},{6,10},{2,6},{0,2},{5,1},{9,5},... | collective-permute-start | bytes 786440 | tf_op jit(solution)/shard_map/ppermute | solution.py:173
  63.1 1.6 copy-start.1
  67.5 4.0 %collective-permute-start.10 = (bf16[128,64]{1,0:T(8,128)(2,1)S(1)}, bf16[128,64]{1,0:T(8,128)(2,1)S(1)}, u32[]{:S(2)}, u32[]{:S(2)}) collective-permute-start(bf16[128,64]{1,0:T(8,128)(2,1)S(1)} %shard_map.100), channel_id=1, source_target_pairs={{0,2},{2,0},{4,6},{6,4},{8,10},{10,8},{12,14},{14,12},{1,3},{3,1},... | collective-permute-start | bytes 49160 | tf_op jit(solution)/shard_map/ppermute | solution.py:217
  71.5 4.4 %collective-permute-start.11 = (bf16[128,64]{1,0:T(8,128)(2,1)S(1)}, bf16[128,64]{1,0:T(8,128)(2,1)S(1)}, u32[]{:S(2)}, u32[]{:S(2)}) collective-permute-start(bf16[128,64]{1,0:T(8,128)(2,1)S(1)} %add.60), channel_id=1, source_target_pairs={{0,4},{2,6},{4,0},{6,2},{8,12},{10,14},{12,8},{14,10},{1,5},{3,7},... | collective-permute-start | bytes 49160 | tf_op jit(solution)/shard_map/ppermute | solution.py:217
  75.9 4.9 %collective-permute-start.12 = (bf16[128,64]{1,0:T(8,128)(2,1)S(1)}, bf16[128,64]{1,0:T(8,128)(2,1)S(1)}, u32[]{:S(2)}, u32[]{:S(2)}) collective-permute-start(bf16[128,64]{1,0:T(8,128)(2,1)S(1)} %add.61), channel_id=1, source_target_pairs={{0,8},{2,10},{4,12},{6,14},{8,0},{10,2},{12,4},{14,6},{1,9},{3,11}... | collective-permute-start | bytes 49160 | tf_op jit(solution)/shard_map/ppermute | solution.py:217
  76.0 32.1 %collective-permute-start.15 = (bf16[16,8192]{1,0:T(8,128)(2,1)}, bf16[16,8192]{1,0:T(8,128)(2,1)}, u32[]{:S(2)}, u32[]{:S(2)}) collective-permute-start(bf16[16,8192]{1,0:T(8,128)(2,1)} %collective-permute-done.13.refs_3_), channel_id=1, source_target_pairs={{0,4},{4,8},{8,12},{12,14},{14,10},{10,6},{6,2},{2,0},{1,5},{5,9},... | collective-permute-start | bytes 786440 | tf_op jit(solution)/shard_map/ppermute | solution.py:173
  77.6 32.4 %collective-permute-start.18 = (bf16[16,8192]{1,0:T(8,128)(2,1)}, bf16[16,8192]{1,0:T(8,128)(2,1)}, u32[]{:S(2)}, u32[]{:S(2)}) collective-permute-start(bf16[16,8192]{1,0:T(8,128)(2,1)} %collective-permute-done.16.refs_6_), channel_id=1, source_target_pairs={{4,0},{8,4},{12,8},{14,12},{10,14},{6,10},{2,6},{0,2},{5,1},{9,5},... | collective-permute-start | bytes 786440 | tf_op jit(solution)/shard_map/ppermute | solution.py:173
  103.1 0.8 copy-start.3
  103.9 55.9 %all-to-all-start.1 = ((bf16[8,16,2048]{2,1,0:T(8,128)(2,1)}), bf16[8,16,2048]{2,1,0:T(8,128)(2,1)}, u32[]{:S(2)}, u32[]{:S(2)}) async-start(bf16[8,16,2048]{2,1,0:T(8,128)(2,1)} %bitcast.24), calls=%async_computation.1 | async-start | bytes 1048576 | tf_op jit(solution)/shard_map/all_to_all | solution.py:223
  108.0 8.5 %collective-permute-start.17 = (bf16[16,8192]{1,0:T(8,128)(2,1)}, bf16[16,8192]{1,0:T(8,128)(2,1)S(1)}, u32[]{:S(2)}, u32[]{:S(2)}) collective-permute-start(bf16[16,8192]{1,0:T(8,128)(2,1)} %collective-permute-done.15.refs_5_), channel_id=1, source_target_pairs={{0,4},{4,8},{8,12},{12,14},{14,10},{10,6},{6,2},{2,0},{1,5},{5,9},... | collective-permute-start | bytes 786440 | tf_op jit(solution)/shard_map/ppermute | solution.py:173
  109.9 9.5 %collective-permute-start.19 = (bf16[16,8192]{1,0:T(8,128)(2,1)}, bf16[16,8192]{1,0:T(8,128)(2,1)}, u32[]{:S(2)}, u32[]{:S(2)}) collective-permute-start(bf16[16,8192]{1,0:T(8,128)(2,1)} %collective-permute-done.18.refs_8_), channel_id=1, source_target_pairs={{4,0},{8,4},{12,8},{14,12},{10,14},{6,10},{2,6},{0,2},{5,1},{9,5},... | collective-permute-start | bytes 786440 | tf_op jit(solution)/shard_map/ppermute | solution.py:173
  119.4 1.6 copy-start.2
  123.7 4.0 %collective-permute-start.20 = (bf16[128,64]{1,0:T(8,128)(2,1)S(1)}, bf16[128,64]{1,0:T(8,128)(2,1)S(1)}, u32[]{:S(2)}, u32[]{:S(2)}) collective-permute-start(bf16[128,64]{1,0:T(8,128)(2,1)S(1)} %shard_map.102), channel_id=1, source_target_pairs={{0,2},{2,0},{4,6},{6,4},{8,10},{10,8},{12,14},{14,12},{1,3},{3,1},... | collective-permute-start | bytes 49160 | tf_op jit(solution)/shard_map/ppermute | solution.py:217
  127.7 4.3 %collective-permute-start.21 = (bf16[128,64]{1,0:T(8,128)(2,1)S(1)}, bf16[128,64]{1,0:T(8,128)(2,1)S(1)}, u32[]{:S(2)}, u32[]{:S(2)}) collective-permute-start(bf16[128,64]{1,0:T(8,128)(2,1)S(1)} %add.66), channel_id=1, source_target_pairs={{0,4},{2,6},{4,0},{6,2},{8,12},{10,14},{12,8},{14,10},{1,5},{3,7},... | collective-permute-start | bytes 49160 | tf_op jit(solution)/shard_map/ppermute | solution.py:217
  131.9 4.9 %collective-permute-start.22 = (bf16[128,64]{1,0:T(8,128)(2,1)S(1)}, bf16[128,64]{1,0:T(8,128)(2,1)S(1)}, u32[]{:S(2)}, u32[]{:S(2)}) collective-permute-start(bf16[128,64]{1,0:T(8,128)(2,1)S(1)} %add.67), channel_id=1, source_target_pairs={{0,8},{2,10},{4,12},{6,14},{8,0},{10,2},{12,4},{14,6},{1,9},{3,11}... | collective-permute-start | bytes 49160 | tf_op jit(solution)/shard_map/ppermute | solution.py:217
  159.8 14.5 %all-to-all-start.2 = ((bf16[8,16,2048]{2,1,0:T(8,128)(2,1)}), bf16[8,16,2048]{2,1,0:T(8,128)(2,1)S(1)}, u32[]{:S(2)}, u32[]{:S(2)}) async-start(bf16[8,16,2048]{2,1,0:T(8,128)(2,1)} %bitcast.8), calls=%async_computation.2 | async-start | bytes 1048576 | tf_op jit(solution)/shard_map/all_to_all | solution.py:223

commit v2 on v0

v2 whole, which is shorter than its diff:
```python
import functools

import jax
import jax.numpy as jnp
from jax import lax
from jax.experimental import pallas as pl
from jax.experimental.pallas import tpu as pltpu
from jax.sharding import PartitionSpec as P

BF16 = jnp.bfloat16
F32 = jnp.float32
HBM = pl.BlockSpec(memory_space=pltpu.HBM)
SMEM = pl.BlockSpec(memory_space=pltpu.SMEM)
LANES = 128


def walks_back(count):
    return count % 2 == 0 and count <= 8


def ring_order(count):
    if walks_back(count):
        return list(range(0, count, 2)) + list(range(1, count, 2))[::-1]
    return list(range(count))


def owner_at(me, offset, count):
    if not walks_back(count):
        return lax.rem(me + offset + count, count)
    place = jnp.where(me % 2 == 0, me // 2, count - 1 - me // 2)
    place = lax.rem(place + offset + count, count)
    return jnp.where(place < count // 2, 2 * place, 2 * (count - 1 - place) + 1)


def fetch_rows(units, held, sem):
    rows = units[0].shape[0]
    return [
        pltpu.make_async_copy(unit, held.at[pl.ds(j * rows, rows)], sem.at[j])
        for j, unit in enumerate(units)
    ]


def row_of(me, place, count, rows):
    offset, part, parts = place
    return pl.multiple_of((owner_at(me, offset, count) * parts + part) * rows, rows)


def start_all(copies):
    for copy in copies:
        copy.start()


def wait_all(copies):
    for copy in copies:
        copy.wait()


def call(kernel, outs, in_specs, scratch, flops, moved):
    return pl.pallas_call(
        kernel,
        in_specs=in_specs,
        out_specs=[HBM] * len(outs),
        out_shape=[jax.ShapeDtypeStruct(out, BF16) for out in outs],
        scratch_shapes=scratch,
        compiler_params=pltpu.CompilerParams(vmem_limit_bytes=60 << 20),
        cost_estimate=pl.CostEstimate(flops=flops, bytes_accessed=moved, transcendentals=0),
    )


def masked_ranks(me, held, d_held):
    width, rank = d_held.shape
    low = jnp.dot(held[:, :width], d_held[...], preferred_element_type=F32)
    low = jnp.where(held[:, width : width + rank].astype(F32) == me.astype(F32), low, 0.0)
    return jnp.concatenate([low, jnp.zeros_like(low)], axis=1).astype(BF16)


def early_rows(ids, units, weight, down):
    fetched, rows = len(units), units[0].shape[0]
    wide = units[0].shape[1]
    columns = weight.shape[1]
    width, rank = down.shape
    total = fetched * rows
    step = min(512, columns)
    pieces = columns // step

    def kernel(ids, *refs):
        units, refs = refs[:fetched], refs[fetched:]
        weight, down, out, low, held, w_held, d_held, o_held, l_held, sem, w_sem, d_sem, o_sem = refs
        copies = fetch_rows(units, held, sem) + [pltpu.make_async_copy(down, d_held, d_sem)]
        w_copies, o_copies = [], []
        for i in range(pieces):
            at = pl.ds(i * step, step)
            w_copies.append(pltpu.make_async_copy(weight.at[:, at], w_held.at[i], w_sem.at[i]))
            o_copies.append(pltpu.make_async_copy(o_held.at[:, at], out.at[:, at], o_sem.at[i]))
        o_copies.append(pltpu.make_async_copy(l_held, low, o_sem.at[pieces]))
        start_all(copies)
        start_all(w_copies)
        wait_all(copies)
        l_held[...] = masked_ranks(ids[0], held, d_held)
        o_copies[pieces].start()
        for i in range(pieces):
            w_copies[i].wait()
            o_held[:, i * step : (i + 1) * step] = jnp.dot(
                held[:, :width], w_held[i], preferred_element_type=F32
            ).astype(BF16)
            o_copies[i].start()
        wait_all(o_copies)

    return call(
        kernel,
        [(total, columns), (total, 2 * rank)],
        [SMEM] + [HBM] * (fetched + 2),
        [
            pltpu.VMEM((total, wide), BF16),
            pltpu.VMEM((pieces, width, step), BF16),
            pltpu.VMEM((width, rank), BF16),
            pltpu.VMEM((total, columns), BF16),
            pltpu.VMEM((total, 2 * rank), BF16),
            pltpu.SemaphoreType.DMA((fetched,)),
            pltpu.SemaphoreType.DMA((pieces,)),
            pltpu.SemaphoreType.DMA,
            pltpu.SemaphoreType.DMA((pieces + 1,)),
        ],
        2 * total * width * (columns + rank),
        2 * width * (columns + total + rank),
    )(ids, *units, weight, down)


def late_ranks(ids, units, places, down, early, early_places, count):
    fetched, rows = len(units), units[0].shape[0]
    wide = units[0].shape[1]
    width, rank = down.shape
    total = (len(places) + len(early_places)) * rows

    def kernel(ids, *refs):
        units, refs = refs[:fetched], refs[fetched:]
        down, early, out, held, d_held, o_held, sem, d_sem, e_sem, o_sem = refs
        copies = fetch_rows(units, held, sem) + [pltpu.make_async_copy(down, d_held, d_sem)]
        for j, place in enumerate(early_places):
            at = pl.ds(row_of(ids[0], place, count, rows), rows)
            part = early.at[pl.ds(j * rows, rows)]
            copies.append(pltpu.make_async_copy(part, o_held.at[at], e_sem.at[j]))
        start_all(copies)
        wait_all(copies)
        low = masked_ranks(ids[0], held, d_held)
        for j, place in enumerate(places):
            at = pl.ds(row_of(ids[0], place, count, rows), rows)
            o_held[at] = low[j * rows : (j + 1) * rows]
        copies = [pltpu.make_async_copy(o_held, out.at[i], o_sem.at[i]) for i in range(count)]
        start_all(copies)
        wait_all(copies)

    return call(
        kernel,
        [(count, total, 2 * rank)],
        [SMEM] + [HBM] * (fetched + 2),
        [
            pltpu.VMEM((fetched * rows, wide), BF16),
            pltpu.VMEM((width, rank), BF16),
            pltpu.VMEM((total, 2 * rank), BF16),
            pltpu.SemaphoreType.DMA((fetched,)),
            pltpu.SemaphoreType.DMA,
            pltpu.SemaphoreType.DMA((len(early_places),)),
            pltpu.SemaphoreType.DMA((count,)),
        ],
        2 * fetched * rows * width * rank,
        2 * width * (fetched * rows + rank),
    )(ids, *units, down, early)[0]


def base_rows(ids, units, weight):
    fetched, rows = len(units), units[0].shape[0]
    wide = units[0].shape[1]
    width, columns = weight.shape
    total = fetched * rows
    step = min(512, columns)
    pieces = columns // step

    def kernel(ids, *refs):
        units, refs = refs[:fetched], refs[fetched:]
        weight, out, held, w_held, o_held, sem, w_sem, o_sem = refs
        x_copies = fetch_rows(units, held, sem)
        w_copies, o_copies = [], []
        for i in range(pieces):
            at = pl.ds(i * step, step)
            w_copies.append(pltpu.make_async_copy(weight.at[:, at], w_held.at[i], w_sem.at[i]))
            o_copies.append(pltpu.make_async_copy(o_held.at[:, at], out.at[:, at], o_sem.at[i]))
        start_all(x_copies)
        start_all(w_copies)
        wait_all(x_copies)
        for i in range(pieces):
            w_copies[i].wait()
            o_held[:, i * step : (i + 1) * step] = jnp.dot(
                held[:, :width], w_held[i], preferred_element_type=F32
            ).astype(BF16)
            o_copies[i].start()
        wait_all(o_copies)

    return call(
        kernel,
        [(total, columns)],
        [SMEM] + [HBM] * (fetched + 1),
        [
            pltpu.VMEM((total, wide), BF16),
            pltpu.VMEM((pieces, width, step), BF16),
            pltpu.VMEM((total, columns), BF16),
            pltpu.SemaphoreType.DMA((fetched,)),
            pltpu.SemaphoreType.DMA((pieces,)),
            pltpu.SemaphoreType.DMA((pieces,)),
        ],
        2 * total * width * columns,
        2 * width * (columns + total),
    )(ids, *units, weight)[0]


def add_delta(ids, ups, crossed, bases, places, low):
    shares, parts = len(ups), len(bases)
    count, sub, columns = ups[0].shape
    rank = sub * shares
    total = low.shape[1]
    rows = total // len(places)
    own = total // count
    per = [base.shape[0] // rows for base in bases]

    def kernel(ids, *refs):
        ups, bases, low = refs[:shares], refs[shares : shares + parts], refs[shares + parts]
        outs = refs[shares + parts + 1 : shares + parts + 1 + count]
        u_held, b_held, o_held, l_held, sem, b_sem, l_sem, o_sem = refs[shares + parts + 1 + count :]
        l_copy = pltpu.make_async_copy(low, l_held, l_sem)
        l_copy.start()
        u_copies, b_copies = [], []
        for j, up in enumerate(ups):
            at = pl.multiple_of((ids[1] ^ crossed[j]) * sub, sub)
            u_copies.append(pltpu.make_async_copy(up, u_held.at[:, pl.ds(at, sub)], sem.at[j]))
        pieces = [(base, j) for base, units in zip(bases, per) for j in range(units)]
        for j, (base, k) in enumerate(pieces):
            at = pl.ds(row_of(ids[0], places[j], count, rows), rows)
            part = base.at[pl.ds(k * rows, rows)]
            b_copies.append(pltpu.make_async_copy(part, b_held.at[at], b_sem.at[j]))
        start_all(u_copies)
        start_all(b_copies)
        l_copy.wait()
        wide = jnp.concatenate([l_held[s][:, :rank] for s in range(count)], axis=1)
        wait_all(u_copies)
        ups_here = u_held[...].reshape(count * rank, columns)
        delta = jnp.dot(wide, ups_here, preferred_element_type=F32).astype(BF16)
        wait_all(b_copies)
        o_held[...] = (b_held[...].astype(F32) + delta.astype(F32)).astype(BF16)
        o_copies = []
        for i in range(count):
            at = pl.ds(pl.multiple_of((ids[0] ^ i) * own, own), own)
            o_copies.append(pltpu.make_async_copy(o_held.at[at], outs[i], o_sem.at[i]))
        start_all(o_copies)
        wait_all(o_copies)

    return call(
        kernel,
        [(own, columns)] * count,
        [SMEM] + [HBM] * (shares + parts + 1),
        [
            pltpu.VMEM((count, rank, columns), BF16),
            pltpu.VMEM((total, columns), BF16),
            pltpu.VMEM((total, columns), BF16),
            pltpu.VMEM(low.shape, BF16),
            pltpu.SemaphoreType.DMA((shares,)),
            pltpu.SemaphoreType.DMA((len(places),)),
            pltpu.SemaphoreType.DMA,
            pltpu.SemaphoreType.DMA((count,)),
        ],
        2 * total * count * rank * columns,
        2 * count * rank * columns,
    )(ids, *ups, *bases, low)


def split_share(ids, up, count, sub):
    columns = up.shape[1] // count

    def kernel(ids, up, out, held, sem, o_sem):
        at = pl.ds(pl.multiple_of(ids[1] * sub, sub), sub)
        copies, o_copies = [], []
        for t in range(count):
            cols = pl.ds(t * columns, columns)
            copies.append(pltpu.make_async_copy(up.at[at, cols], held.at[t], sem.at[t]))
            o_copies.append(pltpu.make_async_copy(held.at[t], out.at[t], o_sem.at[t]))
        start_all(copies)
        for t in range(count):
            copies[t].wait()
            o_copies[t].start()
        wait_all(o_copies)

    return call(
        kernel,
        [(count, sub, columns)],
        [SMEM, HBM],
        [
            pltpu.VMEM((count, sub, columns), BF16),
            pltpu.SemaphoreType.DMA((count,)),
            pltpu.SemaphoreType.DMA((count,)),
        ],
        0,
        4 * count * sub * columns,
    )(ids, up)[0]


def join_columns(ids, parts):
    count = len(parts)
    rows, columns = parts[0].shape

    def kernel(ids, *refs):
        parts, (out, held, sem, o_sem) = refs[:count], refs[count:]
        copies, o_copies = [], []
        for i, part in enumerate(parts):
            at = pl.ds(pl.multiple_of((ids[0] ^ i) * columns, columns), columns)
            copies.append(pltpu.make_async_copy(part, held.at[i], sem.at[i]))
            o_copies.append(pltpu.make_async_copy(held.at[i], out.at[:, at], o_sem.at[i]))
        start_all(copies)
        for i in range(count):
            copies[i].wait()
            o_copies[i].start()
        wait_all(o_copies)

    return call(
        kernel,
        [(rows, count * columns)],
        [SMEM] + [HBM] * count,
        [
            pltpu.VMEM((count, rows, columns), BF16),
            pltpu.SemaphoreType.DMA((count,)),
            pltpu.SemaphoreType.DMA((count,)),
        ],
        0,
        4 * rows * count * columns,
    )(ids, *parts)[0]


def after(value, *earlier):
    return lax.optimization_barrier((value, *earlier))[0]


def body(
    token_input_rows,
    base_projection_weight,
    adapter_down_maps,
    adapter_up_maps,
    token_adapter_index,
    adapter_slot_table,
):
    count = lax.axis_size("tensor")
    groups, seqs = lax.axis_size("groups"), lax.axis_size("seq")
    me = lax.axis_index("tensor")
    rows, width = token_input_rows.shape
    half = rows // 2
    rank = adapter_up_maps.shape[1]
    group_shares = max(1, min(groups, rank // (16 * seqs)))
    sub = rank // (group_shares * seqs)
    share_index = (lax.axis_index("groups") % group_shares) * seqs + lax.axis_index("seq")
    ids = jnp.stack([me, share_index]).astype(jnp.int32)

    order = ring_order(count)
    ahead = [(order[p], order[(p + 1) % count]) for p in range(count)]
    behind = [(b, a) for a, b in ahead]

    matches = token_adapter_index[:, None] == jnp.arange(count, dtype=jnp.int32)[None, :]
    slots = jnp.sum(jnp.where(matches, adapter_slot_table[None, :], 0), axis=1)
    slots = jnp.broadcast_to(slots[:, None], (rows, LANES)).astype(BF16)
    carried = jnp.concatenate([token_input_rows, slots], axis=1)

    far = count // 2
    first, second = carried[:half], carried[half:]
    chains = [[[first], [first]], [[second], [second]]]
    for k in range(1, far + 1):
        for h in range(2):
            for way, pairs in enumerate((ahead, behind)):
                if k < far or way == h:
                    chains[h][way].append(lax.ppermute(chains[h][way][-1], "tensor", pairs))
    units, places = [], []
    for k in range(far + 1):
        for h in range(2):
            for way in range(2 if k else 1):
                if k < len(chains[h][way]):
                    units.append(chains[h][way][k])
                    places.append(((-k, k)[way], h, 2))
    early = (units[:count], places[:count])
    late = (units[count:], places[count:])

    swapped = lax.ppermute(ids, "seq", [(i, (i + 1) % seqs) for i in range(seqs)])
    share = split_share(after(ids, swapped), adapter_up_maps[0], count, sub)
    ups = [lax.all_to_all(share, "tensor", split_axis=0, concat_axis=0, tiled=True)]
    crossed = [0]
    for axis, size, shared, stride in (("groups", groups, group_shares, seqs), ("seq", seqs, seqs, 1)):
        bit = 1
        while bit < shared:
            ups += [lax.ppermute(u, axis, [(i, i ^ bit) for i in range(size)]) for u in ups]
            crossed += [c ^ (bit * stride) for c in crossed]
            bit *= 2

    down = adapter_down_maps[0]
    early_base, early_low = early_rows(ids, early[0], base_projection_weight, down)
    low = late_ranks(ids, late[0], late[1], down, early_low, early[1], count)
    low_all = lax.all_to_all(low, "tensor", split_axis=0, concat_axis=0, tiled=True)
    late_base = base_rows(after(ids, low), late[0], base_projection_weight)
    results = add_delta(
        ids, ups, crossed, [early_base, late_base], early[1] + late[1], low_all
    )
    parts = [results[0]]
    for i in range(1, count):
        parts.append(lax.ppermute(results[i], "tensor", [(t, t ^ i) for t in range(count)]))
    return join_columns(ids, parts)


def solution(mesh):
    placed = (
        P(("groups", "tensor", "seq"), None),
        P(None, "tensor"),
        P("tensor", None, None),
        P("tensor", None, None),
        P(("groups", "tensor", "seq")),
        P(),
    )
    return jax.shard_map(
        body,
        mesh=mesh,
        in_specs=placed,
        out_specs=P(("groups", "tensor", "seq"), None),
        check_vma=False,
    )
```

time: 196 us -> 138 us (0.70)
  the two profiles are of different devices: /device:TPU:0 before, /device:TPU:16 now
where the time goes in v2:
time: 138 us; the launch traced here: 137 us
  waiting for transfers between devices  47.3 us (34%)
  Pallas kernels  46.9 us (34%)
  starting transfers between devices  37.2 us (27%)
  local copies, waits for them, and re-layouts  4.61 us (3%)
    ppermute x14, waiting for transfers between devices, body(): chains[h][way].append(lax.ppermute(chains[h][way][-1], 'tensor', pairs))  25.3 us
    ppermute x7, waiting for transfers between devices, body(): lax.ppermute(results[i], 'tensor', [(t, t ^ i) for t in range(count)])  22 us
    pallas_call x1, Pallas kernels, early_rows(): call(kernel, [(total, columns), (total, 2 * rank)], [SMEM] + [HBM] * (fet...  16.7 us
    ppermute x14, starting transfers between devices, body(): chains[h][way].append(lax.ppermute(chains[h][way][-1], 'tensor', pairs))  16.2 us
    pallas_call x1, Pallas kernels, base_rows(): call(kernel, [(total, columns)], [SMEM] + [HBM] * (fetched + 1), [pltpu.V...  15.2 us
    ppermute x7, starting transfers between devices, body(): lax.ppermute(results[i], 'tensor', [(t, t ^ i) for t in range(count)])  7.94 us
    all_to_all x1, starting transfers between devices, body(): lax.all_to_all(share, 'tensor', split_axis=0, concat_axis=0, tiled=True)  6.18 us
    pallas_call x1, Pallas kernels, add_delta(): call(kernel, [(own, columns)] * count, [SMEM] + [HBM] * (shares + parts +...  4.97 us
  transfers between devices with their start and end apart: 26, of which 11 were waited for; matrix products, arithmetic and copies ran while one was open for 1% of the time, Pallas kernels for 27%

profile of v2, /device:TPU:16, one launch (start us, length us, event | category | flops | bytes accessed | tf_op | source)
XLA Modules:
  0.0 137.3 jit_solution(10729758331706728011)
XLA Ops:
  0.0 0.6 pad_add_fusion.ids
  0.6 2.6 %shard_map.64 = bf16[8,16,2048]{2,1,0:T(8,128)(2,1)} custom-call(s32[2]{0:T(128)} %pad_add_fusion.ids, bf16[64,16384]{1,0:T(8,128)(2,1)} %bitcast.6), custom_call_target="tpu_custom_call" | custom-call | bytes 1048576 | tf_op jit(solution)/shard_map/pallas_call | solution.py:291
  3.3 6.2 %all-to-all-start = ((bf16[8,16,2048]{2,1,0:T(8,128)(2,1)}), bf16[8,16,2048]{2,1,0:T(8,128)(2,1)S(1)}, u32[]{:S(2)}, u32[]{:S(2)}) async-start(bf16[8,16,2048]{2,1,0:T(8,128)(2,1)} %shard_map.64), calls=%async_computation | async-start | bytes 1048576 | tf_op jit(solution)/shard_map/all_to_all | solution.py:388
  9.5 0.1 select_reduce_fusion
  9.6 0.1 broadcast_in_dim.23
  9.7 0.6 collective-permute-start.6
  10.3 1.5 %collective-permute-start.3 = (bf16[16,8320]{1,0:T(8,128)(2,1)S(1)}, bf16[16,8320]{1,0:T(8,128)(2,1)S(1)}, u32[]{:S(2)}, u32[]{:S(2)}) collective-permute-start(bf16[16,8320]{1,0:T(8,128)(2,1)S(1)} %get-tuple-element.28.refs_0_), channel_id=1, source_target_pairs={{0,4},{4,8},{8,12},{12,14},{14,10},{10,6},{6,2},{2,0},{1,5},{5,9},... | collective-permute-start | bytes 798728 | tf_op jit(solution)/shard_map/ppermute | solution.py:375
  11.8 1.5 %collective-permute-start.5 = (bf16[16,8320]{1,0:T(8,128)(2,1)S(1)}, bf16[16,8320]{1,0:T(8,128)(2,1)}, u32[]{:S(2)}, u32[]{:S(2)}) collective-permute-start(bf16[16,8320]{1,0:T(8,128)(2,1)S(1)} %get-tuple-element.27.refs_1_), channel_id=1, source_target_pairs={{0,4},{4,8},{8,12},{12,14},{14,10},{10,6},{6,2},{2,0},{1,5},{5,9},... | collective-permute-start | bytes 798728 | tf_op jit(solution)/shard_map/ppermute | solution.py:375
  13.2 0.6 collective-permute-start.4
  13.8 13.9 %collective-permute-done.6.refs_5_ = bf16[16,8320]{1,0:T(8,128)(2,1)S(1)} collective-permute-done((bf16[16,8320]{1,0:T(8,128)(2,1)S(1)}, bf16[16,8320]{1,0:T(8,128)(2,1)S(1)}, u32[]{:S(2)}, u32[]{:S(2)}) %collective-permute-start.6) | collective-permute-done | bytes 266272 | tf_op jit(solution)/shard_map/ppermute | solution.py:375
  27.7 2.5 %collective-permute-start.10 = (bf16[16,8320]{1,0:T(8,128)(2,1)S(1)}, bf16[16,8320]{1,0:T(8,128)(2,1)S(1)}, u32[]{:S(2)}, u32[]{:S(2)}) collective-permute-start(bf16[16,8320]{1,0:T(8,128)(2,1)S(1)} %collective-permute-done.6.refs_5_), channel_id=1, source_target_pairs={{4,0},{8,4},{12,8},{14,12},{10,14},{6,10},{2,6},{0,2},{5,1},{9,5},... | collective-permute-start | bytes 798728 | tf_op jit(solution)/shard_map/ppermute | solution.py:375
  30.2 3.3 %collective-permute-done.5.refs_4_ = bf16[16,8320]{1,0:T(8,128)(2,1)} collective-permute-done((bf16[16,8320]{1,0:T(8,128)(2,1)S(1)}, bf16[16,8320]{1,0:T(8,128)(2,1)}, u32[]{:S(2)}, u32[]{:S(2)}) %collective-permute-start.5) | collective-permute-done | bytes 266272 | tf_op jit(solution)/shard_map/ppermute | solution.py:375
  33.6 2.4 %collective-permute-start.8 = (bf16[16,8320]{1,0:T(8,128)(2,1)}, bf16[16,8320]{1,0:T(8,128)(2,1)}, u32[]{:S(2)}, u32[]{:S(2)}) collective-permute-start(bf16[16,8320]{1,0:T(8,128)(2,1)} %collective-permute-done.4.refs_3_), channel_id=1, source_target_pairs={{4,0},{8,4},{12,8},{14,12},{10,14},{6,10},{2,6},{0,2},{5,1},{9,5},... | collective-permute-start | bytes 798728 | tf_op jit(solution)/shard_map/ppermute | solution.py:375
  36.0 3.1 %collective-permute-done.10.refs_1_ = bf16[16,8320]{1,0:T(8,128)(2,1)S(1)} collective-permute-done((bf16[16,8320]{1,0:T(8,128)(2,1)S(1)}, bf16[16,8320]{1,0:T(8,128)(2,1)S(1)}, u32[]{:S(2)}, u32[]{:S(2)}) %collective-permute-start.10) | collective-permute-done | bytes 266272 | tf_op jit(solution)/shard_map/ppermute | solution.py:375
  39.1 2.5 %collective-permute-start.14 = (bf16[16,8320]{1,0:T(8,128)(2,1)S(1)}, bf16[16,8320]{1,0:T(8,128)(2,1)S(1)}, u32[]{:S(2)}, u32[]{:S(2)}) collective-permute-start(bf16[16,8320]{1,0:T(8,128)(2,1)S(1)} %collective-permute-done.10.refs_1_), channel_id=1, source_target_pairs={{4,0},{8,4},{12,8},{14,12},{10,14},{6,10},{2,6},{0,2},{5,1},{9,5},... | collective-permute-start | bytes 798728 | tf_op jit(solution)/shard_map/ppermute | solution.py:375
  41.7 1.8 %copy.8 = bf16[1,8192,64]{2,1,0:T(8,128)(2,1)} copy(bf16[1,8192,64]{1,2,0:T(8,128)(2,1)S(1)} %copy-done.12) | data formatting | bytes 2097152 | tf_op args[2]
  43.5 1.8 %collective-permute-done.9.refs_0_ = bf16[16,8320]{1,0:T(8,128)(2,1)S(1)} collective-permute-done((bf16[16,8320]{1,0:T(8,128)(2,1)}, bf16[16,8320]{1,0:T(8,128)(2,1)S(1)}, u32[]{:S(2)}, u32[]{:S(2)}) %collective-permute-start.9) | collective-permute-done | bytes 266272 | tf_op jit(solution)/shard_map/ppermute | solution.py:375
  45.3 2.2 %collective-permute-start.12 = (bf16[16,8320]{1,0:T(8,128)(2,1)}, bf16[16,8320]{1,0:T(8,128)(2,1)S(1)}, u32[]{:S(2)}, u32[]{:S(2)}) collective-permute-start(bf16[16,8320]{1,0:T(8,128)(2,1)} %collective-permute-done.8.refs_7_), channel_id=1, source_target_pairs={{4,0},{8,4},{12,8},{14,12},{10,14},{6,10},{2,6},{0,2},{5,1},{9,5},... | collective-permute-start | bytes 798728 | tf_op jit(solution)/shard_map/ppermute | solution.py:375
  47.4 3.1 %collective-permute-done.14.refs_5_ = bf16[16,8320]{1,0:T(8,128)(2,1)S(1)} collective-permute-done((bf16[16,8320]{1,0:T(8,128)(2,1)S(1)}, bf16[16,8320]{1,0:T(8,128)(2,1)S(1)}, u32[]{:S(2)}, u32[]{:S(2)}) %collective-permute-start.14) | collective-permute-done | bytes 266272 | tf_op jit(solution)/shard_map/ppermute | solution.py:375
  50.6 2.5 %collective-permute-start.16 = (bf16[16,8320]{1,0:T(8,128)(2,1)S(1)}, bf16[16,8320]{1,0:T(8,128)(2,1)S(1)}, u32[]{:S(2)}, u32[]{:S(2)}) collective-permute-start(bf16[16,8320]{1,0:T(8,128)(2,1)S(1)} %collective-permute-done.14.refs_5_), channel_id=1, source_target_pairs={{4,0},{8,4},{12,8},{14,12},{10,14},{6,10},{2,6},{0,2},{5,1},{9,5},... | collective-permute-start | bytes 798728 | tf_op jit(solution)/shard_map/ppermute | solution.py:375
  53.1 1.6 %collective-permute-start = (bf16[8,16,2048]{2,1,0:T(8,128)(2,1)S(1)}, bf16[8,16,2048]{2,1,0:T(8,128)(2,1)}, u32[]{:S(2)}, u32[]{:S(2)}) collective-permute-start(bf16[8,16,2048]{2,1,0:T(8,128)(2,1)S(1)} %all-to-all-done.refs_0_), channel_id=1, source_target_pairs={{0,16},{16,0},{1,17},{17,1},{2,18},{18,2},{3,19},{19,3},{4,20},{20... | collective-permute-start | bytes 1572872 | tf_op jit(solution)/shard_map/ppermute | solution.py:393
  54.6 16.7 %shard_map.65 = (bf16[128,2048]{1,0:T(8,128)(2,1)}, bf16[128,128]{1,0:T(8,128)(2,1)}) custom-call(s32[2]{0:T(128)} %pad_add_fusion.ids, bf16[16,8320]{1,0:T(8,128)(2,1)} %copy-done.11, bf16[16,8320]{1,0:T(8,128)(2,1)} %copy-done.10, bf16[16,8320]{1,0:T(8,128)(2,1)} %copy-done.17, bf16[16,8320]{1,0:T(8,128)(2,1)} %collective-permute-done.4.refs_3_, ...), custom_call_target="tpu_custom_call" | custom-call | flops 4429185024 | bytes 36700160 | tf_op jit(solution)/shard_map/pallas_call | solution.py:109
  71.4 0.6 copy-done.6
  72.1 0.1 copy-done.7
  72.2 0.1 copy-done.8
  72.3 0.1 copy-done.9
  72.4 4.7 %shard_map.66 = bf16[8,256,128]{2,1,0:T(8,128)(2,1)} custom-call(s32[2]{0:T(128)} %pad_add_fusion.ids, bf16[16,8320]{1,0:T(8,128)(2,1)} %copy-done.3, bf16[16,8320]{1,0:T(8,128)(2,1)} %copy-done.2, bf16[16,8320]{1,0:T(8,128)(2,1)} %copy-done.5, bf16[16,8320]{1,0:T(8,128)(2,1)} %copy-done.7, bf16[16,8320]{1,0:T(8,128)(2,1)} %copy-done.6, ...), custom_call_target="tpu_custom_call" | custom-call | flops 134217728 | bytes 3145728 | tf_op jit(solution)/shard_map/pallas_call | solution.py:153
  77.1 4.9 %all-to-all-start.1 = ((bf16[8,256,128]{2,1,0:T(8,128)(2,1)}), bf16[8,256,128]{2,1,0:T(8,128)(2,1)S(1)}, u32[]{:S(2)}, u32[]{:S(2)}) async-start(bf16[8,256,128]{2,1,0:T(8,128)(2,1)} %shard_map.66), calls=%async_computation.1 | async-start | bytes 1048576 | tf_op jit(solution)/shard_map/all_to_all | solution.py:400
  82.0 0.5 collective-permute-start.2
  82.5 15.2 %shard_map.67.refs_5_ = bf16[128,2048]{1,0:T(8,128)(2,1)} custom-call(s32[2]{0:T(128)} %pad_add_fusion.ids, bf16[16,8320]{1,0:T(8,128)(2,1)} %copy-done.3, bf16[16,8320]{1,0:T(8,128)(2,1)} %copy-done.2, bf16[16,8320]{1,0:T(8,128)(2,1)} %copy-done.5, bf16[16,8320]{1,0:T(8,128)(2,1)} %copy-done.7, bf16[16,8320]{1,0:T(8,128)(2,1)} %copy-done.6, ...), custom_call_target="tpu_custom_call" | custom-call | flops 4294967296 | bytes 35651584 | tf_op jit(solution)/shard_map/pallas_call | solution.py:199
  97.8 0.7 copy-done.14
  98.5 0.2 copy-done.15
  98.7 0.1 copy-done.1
  98.8 5.0 %shard_map.68 = (bf16[32,2048]{1,0:T(8,128)(2,1)}, bf16[32,2048]{1,0:T(8,128)(2,1)}, bf16[32,2048]{1,0:T(8,128)(2,1)}, bf16[32,2048]{1,0:T(8,128)(2,1)}, bf16[32...) custom-call(s32[2]{0:T(128)} %pad_add_fusion.ids, ...), custom_call_target="tpu_custom_call" | custom-call | flops 536870912 | bytes 2097152 | tf_op jit(solution)/shard_map/pallas_call | solution.py:256
  103.8 1.5 %collective-permute-start.17 = (bf16[32,2048]{1,0:T(8,128)(2,1)}, bf16[32,2048]{1,0:T(8,128)(2,1)S(1)}, u32[]{:S(2)}, u32[]{:S(2)}) collective-permute-start(bf16[32,2048]{1,0:T(8,128)(2,1)} %get-tuple-element.20), channel_id=1, source_target_pairs={{0,2},{2,0},{4,6},{6,4},{8,10},{10,8},{12,14},{14,12},{1,3},{3,1},... | collective-permute-start | bytes 393224 | tf_op jit(solution)/shard_map/ppermute | solution.py:407
  105.4 1.5 %collective-permute-start.18 = (bf16[32,2048]{1,0:T(8,128)(2,1)}, bf16[32,2048]{1,0:T(8,128)(2,1)S(1)}, u32[]{:S(2)}, u32[]{:S(2)}) collective-permute-start(bf16[32,2048]{1,0:T(8,128)(2,1)} %get-tuple-element.21), channel_id=1, source_target_pairs={{0,4},{2,6},{4,0},{6,2},{8,12},{10,14},{12,8},{14,10},{1,5},{3,7},... | collective-permute-start | bytes 393224 | tf_op jit(solution)/shard_map/ppermute | solution.py:407
  106.8 0.6 collective-permute-start.19
  107.4 0.3 collective-permute-start.20
  107.7 3.5 %collective-permute-start.21 = (bf16[32,2048]{1,0:T(8,128)(2,1)}, bf16[32,2048]{1,0:T(8,128)(2,1)S(1)}, u32[]{:S(2)}, u32[]{:S(2)}) collective-permute-start(bf16[32,2048]{1,0:T(8,128)(2,1)} %get-tuple-element.24), channel_id=1, source_target_pairs={{0,10},{2,8},{4,14},{6,12},{8,2},{10,0},{12,6},{14,4},{1,11},{3,9}... | collective-permute-start | bytes 393224 | tf_op jit(solution)/shard_map/ppermute | solution.py:407
  111.2 0.6 collective-permute-start.22
  111.8 2.4 %collective-permute-done.18.refs_2_ = bf16[32,2048]{1,0:T(8,128)(2,1)S(1)} collective-permute-done((bf16[32,2048]{1,0:T(8,128)(2,1)}, bf16[32,2048]{1,0:T(8,128)(2,1)S(1)}, u32[]{:S(2)}, u32[]{:S(2)}) %collective-permute-start.18) | collective-permute-done | bytes 131104 | tf_op jit(solution)/shard_map/ppermute | solution.py:407
  114.2 1.8 %collective-permute-done.19.refs_3_ = bf16[32,2048]{1,0:T(8,128)(2,1)S(1)} collective-permute-done((bf16[32,2048]{1,0:T(8,128)(2,1)}, bf16[32,2048]{1,0:T(8,128)(2,1)S(1)}, u32[]{:S(2)}, u32[]{:S(2)}) %collective-permute-start.19) | collective-permute-done | bytes 131104 | tf_op jit(solution)/shard_map/ppermute | solution.py:407
  116.0 1.7 %collective-permute-done.20.refs_4_ = bf16[32,2048]{1,0:T(8,128)(2,1)S(1)} collective-permute-done((bf16[32,2048]{1,0:T(8,128)(2,1)}, bf16[32,2048]{1,0:T(8,128)(2,1)S(1)}, u32[]{:S(2)}, u32[]{:S(2)}) %collective-permute-start.20) | collective-permute-done | bytes 131104 | tf_op jit(solution)/shard_map/ppermute | solution.py:407
  117.7 8.5 %collective-permute-done.21.refs_5_ = bf16[32,2048]{1,0:T(8,128)(2,1)S(1)} collective-permute-done((bf16[32,2048]{1,0:T(8,128)(2,1)}, bf16[32,2048]{1,0:T(8,128)(2,1)S(1)}, u32[]{:S(2)}, u32[]{:S(2)}) %collective-permute-start.21) | collective-permute-done | bytes 131104 | tf_op jit(solution)/shard_map/ppermute | solution.py:407
  126.2 5.3 %collective-permute-done.22.refs_6_ = bf16[32,2048]{1,0:T(8,128)(2,1)S(1)} collective-permute-done((bf16[32,2048]{1,0:T(8,128)(2,1)}, bf16[32,2048]{1,0:T(8,128)(2,1)S(1)}, u32[]{:S(2)}, u32[]{:S(2)}) %collective-permute-start.22) | collective-permute-done | bytes 131104 | tf_op jit(solution)/shard_map/ppermute | solution.py:407
  131.4 2.3 %collective-permute-done.23.refs_7_ = bf16[32,2048]{1,0:T(8,128)(2,1)S(1)} collective-permute-done((bf16[32,2048]{1,0:T(8,128)(2,1)}, bf16[32,2048]{1,0:T(8,128)(2,1)S(1)}, u32[]{:S(2)}, u32[]{:S(2)}) %collective-permute-start.23) | collective-permute-done | bytes 131104 | tf_op jit(solution)/shard_map/ppermute | solution.py:407
  133.8 0.6 copy-done.24
  134.4 2.7 %shard_map.69 = bf16[32,16384]{1,0:T(8,128)(2,1)} custom-call(s32[2]{0:T(128)} %pad_add_fusion.ids, bf16[32,2048]{1,0:T(8,128)(2,1)} %get-tuple-element.19.refs_0_, bf16[32,2048]{1,0:T(8,128)(2,1)} %copy-done.18, bf16[32,2048]{1,0:T(8,128)(2,1)} %copy-done.19, bf16[32,2048]{1,0:T(8,128)(2,1)} %copy-done.20, bf16[32,2048]{1,0:T(8,128)(2,1)} %copy-done.21, ...), custom_call_target="tpu_custom_call" | custom-call | bytes 2097152 | tf_op jit(solution)/shard_map/pallas_call | solution.py:322
  (70 shorter events, 0.2 us)
Async XLA Ops:
  0.0 9.5 %copy-start.26 = (s32[32]{0:T(128)S(1)}, s32[32]{0:T(128)}, u32[]{:S(2)}) copy-start(s32[32]{0:T(128)} %param.10) | copy-start | bytes 388
  0.0 9.5 %copy-start.25 = (s32[8]{0:T(128)S(1)}, s32[8]{0:T(128)}, u32[]{:S(2)}) copy-start(s32[8]{0:T(128)} %param.11) | copy-start | bytes 100
  0.0 9.6 %copy-start.13 = (bf16[32,8192]{1,0:T(8,128)(2,1)S(1)}, bf16[32,8192]{1,0:T(8,128)(2,1)}, u32[]{:S(2)}) copy-start(bf16[32,8192]{1,0:T(8,128)(2,1)} %param.6) | copy-start | bytes 1572868
  0.6 41.0 %copy-start.12 = (bf16[1,8192,64]{1,2,0:T(8,128)(2,1)S(1)}, bf16[1,8192,64]{1,2,0:T(8,128)(2,1)}, u32[]{:S(2)}) copy-start(bf16[1,8192,64]{1,2,0:T(8,128)(2,1)} %param.8) | copy-start | bytes 3145732
  3.3 49.8 %all-to-all-start = ((bf16[8,16,2048]{2,1,0:T(8,128)(2,1)}), bf16[8,16,2048]{2,1,0:T(8,128)(2,1)S(1)}, u32[]{:S(2)}, u32[]{:S(2)}) async-start(bf16[8,16,2048]{2,1,0:T(8,128)(2,1)} %shard_map.64), calls=%async_computation | async-start | bytes 1048576 | tf_op jit(solution)/shard_map/all_to_all | solution.py:388
  9.7 45.0 %copy-start.10 = (bf16[16,8320]{1,0:T(8,128)(2,1)}, bf16[16,8320]{1,0:T(8,128)(2,1)S(1)}, u32[]{:S(2)}) copy-start(bf16[16,8320]{1,0:T(8,128)(2,1)S(1)} %get-tuple-element.27.refs_1_) | copy-start | bytes 798724
  9.7 44.9 %copy-start.11 = (bf16[16,8320]{1,0:T(8,128)(2,1)}, bf16[16,8320]{1,0:T(8,128)(2,1)S(1)}, u32[]{:S(2)}) copy-start(bf16[16,8320]{1,0:T(8,128)(2,1)S(1)} %get-tuple-element.28.refs_0_) | copy-start | bytes 798724
  9.7 18.0 %collective-permute-start.6 = (bf16[16,8320]{1,0:T(8,128)(2,1)S(1)}, bf16[16,8320]{1,0:T(8,128)(2,1)S(1)}, u32[]{:S(2)}, u32[]{:S(2)}) collective-permute-start(bf16[16,8320]{1,0:T(8,128)(2,1)S(1)} %get-tuple-element.27.refs_1_), channel_id=1, source_target_pairs={{4,0},{8,4},{12,8},{14,12},{10,14},{6,10},{2,6},{0,2},{5,1},{9,5},... | collective-permute-start | bytes 798728 | tf_op jit(solution)/shard_map/ppermute | solution.py:375
  10.3 19.9 %collective-permute-start.3 = (bf16[16,8320]{1,0:T(8,128)(2,1)S(1)}, bf16[16,8320]{1,0:T(8,128)(2,1)S(1)}, u32[]{:S(2)}, u32[]{:S(2)}) collective-permute-start(bf16[16,8320]{1,0:T(8,128)(2,1)S(1)} %get-tuple-element.28.refs_0_), channel_id=1, source_target_pairs={{0,4},{4,8},{8,12},{12,14},{14,10},{10,6},{6,2},{2,0},{1,5},{5,9},... | collective-permute-start | bytes 798728 | tf_op jit(solution)/shard_map/ppermute | solution.py:375
  11.8 21.8 %collective-permute-start.5 = (bf16[16,8320]{1,0:T(8,128)(2,1)S(1)}, bf16[16,8320]{1,0:T(8,128)(2,1)}, u32[]{:S(2)}, u32[]{:S(2)}) collective-permute-start(bf16[16,8320]{1,0:T(8,128)(2,1)S(1)} %get-tuple-element.27.refs_1_), channel_id=1, source_target_pairs={{0,4},{4,8},{8,12},{12,14},{14,10},{10,6},{6,2},{2,0},{1,5},{5,9},... | collective-permute-start | bytes 798728 | tf_op jit(solution)/shard_map/ppermute | solution.py:375
  13.2 20.3 %collective-permute-start.4 = (bf16[16,8320]{1,0:T(8,128)(2,1)S(1)}, bf16[16,8320]{1,0:T(8,128)(2,1)}, u32[]{:S(2)}, u32[]{:S(2)}) collective-permute-start(bf16[16,8320]{1,0:T(8,128)(2,1)S(1)} %get-tuple-element.28.refs_0_), channel_id=1, source_target_pairs={{4,0},{8,4},{12,8},{14,12},{10,14},{6,10},{2,6},{0,2},{5,1},{9,5},... | collective-permute-start | bytes 798728 | tf_op jit(solution)/shard_map/ppermute | solution.py:375
  27.7 8.3 %copy-start.16 = (bf16[16,8320]{1,0:T(8,128)(2,1)}, bf16[16,8320]{1,0:T(8,128)(2,1)S(1)}, u32[]{:S(2)}) copy-start(bf16[16,8320]{1,0:T(8,128)(2,1)S(1)} %collective-permute-done.6.refs_5_) | copy-start | bytes 798724
  27.7 11.4 %collective-permute-start.10 = (bf16[16,8320]{1,0:T(8,128)(2,1)S(1)}, bf16[16,8320]{1,0:T(8,128)(2,1)S(1)}, u32[]{:S(2)}, u32[]{:S(2)}) collective-permute-start(bf16[16,8320]{1,0:T(8,128)(2,1)S(1)} %collective-permute-done.6.refs_5_), channel_id=1, source_target_pairs={{4,0},{8,4},{12,8},{14,12},{10,14},{6,10},{2,6},{0,2},{5,1},{9,5},... | collective-permute-start | bytes 798728 | tf_op jit(solution)/shard_map/ppermute | solution.py:375
  30.2 11.4 %copy-start.17 = (bf16[16,8320]{1,0:T(8,128)(2,1)}, bf16[16,8320]{1,0:T(8,128)(2,1)S(1)}, u32[]{:S(2)}) copy-start(bf16[16,8320]{1,0:T(8,128)(2,1)S(1)} %collective-permute-done.3.refs_2_) | copy-start | bytes 798724
  30.2 11.4 %collective-permute-start.7 = (bf16[16,8320]{1,0:T(8,128)(2,1)S(1)}, bf16[16,8320]{1,0:T(8,128)(2,1)}, u32[]{:S(2)}, u32[]{:S(2)}) collective-permute-start(bf16[16,8320]{1,0:T(8,128)(2,1)S(1)} %collective-permute-done.3.refs_2_), channel_id=1, source_target_pairs={{0,4},{4,8},{8,12},{12,14},{14,10},{10,6},{6,2},{2,0},{1,5},{5,9},... | collective-permute-start | bytes 798728 | tf_op jit(solution)/shard_map/ppermute | solution.py:375
  33.6 11.7 %collective-permute-start.9 = (bf16[16,8320]{1,0:T(8,128)(2,1)}, bf16[16,8320]{1,0:T(8,128)(2,1)S(1)}, u32[]{:S(2)}, u32[]{:S(2)}) collective-permute-start(bf16[16,8320]{1,0:T(8,128)(2,1)} %collective-permute-done.5.refs_4_), channel_id=1, source_target_pairs={{0,4},{4,8},{8,12},{12,14},{14,10},{10,6},{6,2},{2,0},{1,5},{5,9},... | collective-permute-start | bytes 798728 | tf_op jit(solution)/shard_map/ppermute | solution.py:375
  33.6 11.7 %collective-permute-start.8 = (bf16[16,8320]{1,0:T(8,128)(2,1)}, bf16[16,8320]{1,0:T(8,128)(2,1)}, u32[]{:S(2)}, u32[]{:S(2)}) collective-permute-start(bf16[16,8320]{1,0:T(8,128)(2,1)} %collective-permute-done.4.refs_3_), channel_id=1, source_target_pairs={{4,0},{8,4},{12,8},{14,12},{10,14},{6,10},{2,6},{0,2},{5,1},{9,5},... | collective-permute-start | bytes 798728 | tf_op jit(solution)/shard_map/ppermute | solution.py:375
  39.1 32.2 %copy-start.2 = (bf16[16,8320]{1,0:T(8,128)(2,1)}, bf16[16,8320]{1,0:T(8,128)(2,1)S(1)}, u32[]{:S(2)}) copy-start(bf16[16,8320]{1,0:T(8,128)(2,1)S(1)} %collective-permute-done.10.refs_1_) | copy-start | bytes 798724
  39.1 11.4 %collective-permute-start.14 = (bf16[16,8320]{1,0:T(8,128)(2,1)S(1)}, bf16[16,8320]{1,0:T(8,128)(2,1)S(1)}, u32[]{:S(2)}, u32[]{:S(2)}) collective-permute-start(bf16[16,8320]{1,0:T(8,128)(2,1)S(1)} %collective-permute-done.10.refs_1_), channel_id=1, source_target_pairs={{4,0},{8,4},{12,8},{14,12},{10,14},{6,10},{2,6},{0,2},{5,1},{9,5},... | collective-permute-start | bytes 798728 | tf_op jit(solution)/shard_map/ppermute | solution.py:375
  41.6 11.4 %collective-permute-start.11 = (bf16[16,8320]{1,0:T(8,128)(2,1)}, bf16[16,8320]{1,0:T(8,128)(2,1)S(1)}, u32[]{:S(2)}, u32[]{:S(2)}) collective-permute-start(bf16[16,8320]{1,0:T(8,128)(2,1)} %collective-permute-done.7.refs_6_), channel_id=1, source_target_pairs={{0,4},{4,8},{8,12},{12,14},{14,10},{10,6},{6,2},{2,0},{1,5},{5,9},... | collective-permute-start | bytes 798728 | tf_op jit(solution)/shard_map/ppermute | solution.py:375
  45.3 26.1 %copy-start.3 = (bf16[16,8320]{1,0:T(8,128)(2,1)}, bf16[16,8320]{1,0:T(8,128)(2,1)S(1)}, u32[]{:S(2)}) copy-start(bf16[16,8320]{1,0:T(8,128)(2,1)S(1)} %collective-permute-done.9.refs_0_) | copy-start | bytes 798724
  45.3 26.1 %collective-permute-start.13 = (bf16[16,8320]{1,0:T(8,128)(2,1)S(1)}, bf16[16,8320]{1,0:T(8,128)(2,1)S(1)}, u32[]{:S(2)}, u32[]{:S(2)}) collective-permute-start(bf16[16,8320]{1,0:T(8,128)(2,1)S(1)} %collective-permute-done.9.refs_0_), channel_id=1, source_target_pairs={{0,4},{4,8},{8,12},{12,14},{14,10},{10,6},{6,2},{2,0},{1,5},{5,9},... | collective-permute-start | bytes 798728 | tf_op jit(solution)/shard_map/ppermute | solution.py:375
  45.3 26.1 %collective-permute-start.12 = (bf16[16,8320]{1,0:T(8,128)(2,1)}, bf16[16,8320]{1,0:T(8,128)(2,1)S(1)}, u32[]{:S(2)}, u32[]{:S(2)}) collective-permute-start(bf16[16,8320]{1,0:T(8,128)(2,1)} %collective-permute-done.8.refs_7_), channel_id=1, source_target_pairs={{4,0},{8,4},{12,8},{14,12},{10,14},{6,10},{2,6},{0,2},{5,1},{9,5},... | collective-permute-start | bytes 798728 | tf_op jit(solution)/shard_map/ppermute | solution.py:375
  50.6 20.8 %copy-start.4 = (bf16[16,8320]{1,0:T(8,128)(2,1)}, bf16[16,8320]{1,0:T(8,128)(2,1)S(1)}, u32[]{:S(2)}) copy-start(bf16[16,8320]{1,0:T(8,128)(2,1)S(1)} %collective-permute-done.14.refs_5_) | copy-start | bytes 798724
  50.6 20.8 %collective-permute-start.16 = (bf16[16,8320]{1,0:T(8,128)(2,1)S(1)}, bf16[16,8320]{1,0:T(8,128)(2,1)S(1)}, u32[]{:S(2)}, u32[]{:S(2)}) collective-permute-start(bf16[16,8320]{1,0:T(8,128)(2,1)S(1)} %collective-permute-done.14.refs_5_), channel_id=1, source_target_pairs={{4,0},{8,4},{12,8},{14,12},{10,14},{6,10},{2,6},{0,2},{5,1},{9,5},... | collective-permute-start | bytes 798728 | tf_op jit(solution)/shard_map/ppermute | solution.py:375
  53.0 18.3 %copy-start.5 = (bf16[16,8320]{1,0:T(8,128)(2,1)}, bf16[16,8320]{1,0:T(8,128)(2,1)S(1)}, u32[]{:S(2)}) copy-start(bf16[16,8320]{1,0:T(8,128)(2,1)S(1)} %collective-permute-done.11.refs_2_) | copy-start | bytes 798724
  53.0 18.4 %collective-permute-start.15 = (bf16[16,8320]{1,0:T(8,128)(2,1)S(1)}, bf16[16,8320]{1,0:T(8,128)(2,1)S(1)}, u32[]{:S(2)}, u32[]{:S(2)}) collective-permute-start(bf16[16,8320]{1,0:T(8,128)(2,1)S(1)} %collective-permute-done.11.refs_2_), channel_id=1, source_target_pairs={{0,4},{4,8},{8,12},{12,14},{14,10},{10,6},{6,2},{2,0},{1,5},{5,9},... | collective-permute-start | bytes 798728 | tf_op jit(solution)/shard_map/ppermute | solution.py:375
  53.1 28.9 %copy-start = (bf16[8,16,2048]{2,1,0:T(8,128)(2,1)}, bf16[8,16,2048]{2,1,0:T(8,128)(2,1)S(1)}, u32[]{:S(2)}) copy-start(bf16[8,16,2048]{2,1,0:T(8,128)(2,1)S(1)} %all-to-all-done.refs_0_) | copy-start | bytes 1572868
  53.1 28.9 %collective-permute-start = (bf16[8,16,2048]{2,1,0:T(8,128)(2,1)S(1)}, bf16[8,16,2048]{2,1,0:T(8,128)(2,1)}, u32[]{:S(2)}, u32[]{:S(2)}) collective-permute-start(bf16[8,16,2048]{2,1,0:T(8,128)(2,1)S(1)} %all-to-all-done.refs_0_), channel_id=1, source_target_pairs={{0,16},{16,0},{1,17},{17,1},{2,18},{18,2},{3,19},{19,3},{4,20},{20... | collective-permute-start | bytes 1572872 | tf_op jit(solution)/shard_map/ppermute | solution.py:393
  71.4 0.9 copy-start.9
  77.1 20.6 %all-to-all-start.1 = ((bf16[8,256,128]{2,1,0:T(8,128)(2,1)}), bf16[8,256,128]{2,1,0:T(8,128)(2,1)S(1)}, u32[]{:S(2)}, u32[]{:S(2)}) async-start(bf16[8,256,128]{2,1,0:T(8,128)(2,1)} %shard_map.66), calls=%async_computation.1 | async-start | bytes 1048576 | tf_op jit(solution)/shard_map/all_to_all | solution.py:400
  82.0 15.7 %collective-permute-start.1 = (bf16[8,16,2048]{2,1,0:T(8,128)(2,1)S(1)}, bf16[8,16,2048]{2,1,0:T(8,128)(2,1)S(1)}, u32[]{:S(2)}, u32[]{:S(2)}) collective-permute-start(bf16[8,16,2048]{2,1,0:T(8,128)(2,1)S(1)} %all-to-all-done.refs_0_), channel_id=1, source_target_pairs={{0,1},{1,0},{2,3},{3,2},{4,5},{5,4},{6,7},{7,6},{8,9},{9,8},{10,11... | collective-permute-start | bytes 1572872 | tf_op jit(solution)/shard_map/ppermute | solution.py:393
  82.0 15.7 %collective-permute-start.2 = (bf16[8,16,2048]{2,1,0:T(8,128)(2,1)}, bf16[8,16,2048]{2,1,0:T(8,128)(2,1)S(1)}, u32[]{:S(2)}, u32[]{:S(2)}) collective-permute-start(bf16[8,16,2048]{2,1,0:T(8,128)(2,1)} %collective-permute-done.refs_1_), channel_id=1, source_target_pairs={{0,1},{1,0},{2,3},{3,2},{4,5},{5,4},{6,7},{7,6},{8,9},{9,8},{10,11... | collective-permute-start | bytes 1572872 | tf_op jit(solution)/shard_map/ppermute | solution.py:393
  97.7 1.0 copy-start.15
  97.7 1.1 copy-start.1
  103.8 7.4 %collective-permute-start.17 = (bf16[32,2048]{1,0:T(8,128)(2,1)}, bf16[32,2048]{1,0:T(8,128)(2,1)S(1)}, u32[]{:S(2)}, u32[]{:S(2)}) collective-permute-start(bf16[32,2048]{1,0:T(8,128)(2,1)} %get-tuple-element.20), channel_id=1, source_target_pairs={{0,2},{2,0},{4,6},{6,4},{8,10},{10,8},{12,14},{14,12},{1,3},{3,1},... | collective-permute-start | bytes 393224 | tf_op jit(solution)/shard_map/ppermute | solution.py:407
  105.4 8.8 %collective-permute-start.18 = (bf16[32,2048]{1,0:T(8,128)(2,1)}, bf16[32,2048]{1,0:T(8,128)(2,1)S(1)}, u32[]{:S(2)}, u32[]{:S(2)}) collective-permute-start(bf16[32,2048]{1,0:T(8,128)(2,1)} %get-tuple-element.21), channel_id=1, source_target_pairs={{0,4},{2,6},{4,0},{6,2},{8,12},{10,14},{12,8},{14,10},{1,5},{3,7},... | collective-permute-start | bytes 393224 | tf_op jit(solution)/shard_map/ppermute | solution.py:407
  106.8 9.1 %collective-permute-start.19 = (bf16[32,2048]{1,0:T(8,128)(2,1)}, bf16[32,2048]{1,0:T(8,128)(2,1)S(1)}, u32[]{:S(2)}, u32[]{:S(2)}) collective-permute-start(bf16[32,2048]{1,0:T(8,128)(2,1)} %get-tuple-element.22), channel_id=1, source_target_pairs={{0,6},{2,4},{4,2},{6,0},{8,14},{10,12},{12,10},{14,8},{1,7},{3,5},... | collective-permute-start | bytes 393224 | tf_op jit(solution)/shard_map/ppermute | solution.py:407
  107.4 10.3 %collective-permute-start.20 = (bf16[32,2048]{1,0:T(8,128)(2,1)}, bf16[32,2048]{1,0:T(8,128)(2,1)S(1)}, u32[]{:S(2)}, u32[]{:S(2)}) collective-permute-start(bf16[32,2048]{1,0:T(8,128)(2,1)} %get-tuple-element.23), channel_id=1, source_target_pairs={{0,8},{2,10},{4,12},{6,14},{8,0},{10,2},{12,4},{14,6},{1,9},{3,11}... | collective-permute-start | bytes 393224 | tf_op jit(solution)/shard_map/ppermute | solution.py:407
  107.7 18.4 %collective-permute-start.21 = (bf16[32,2048]{1,0:T(8,128)(2,1)}, bf16[32,2048]{1,0:T(8,128)(2,1)S(1)}, u32[]{:S(2)}, u32[]{:S(2)}) collective-permute-start(bf16[32,2048]{1,0:T(8,128)(2,1)} %get-tuple-element.24), channel_id=1, source_target_pairs={{0,10},{2,8},{4,14},{6,12},{8,2},{10,0},{12,6},{14,4},{1,11},{3,9}... | collective-permute-start | bytes 393224 | tf_op jit(solution)/shard_map/ppermute | solution.py:407
  111.2 22.5 %copy-start.18 = (bf16[32,2048]{1,0:T(8,128)(2,1)}, bf16[32,2048]{1,0:T(8,128)(2,1)S(1)}, u32[]{:S(2)}) copy-start(bf16[32,2048]{1,0:T(8,128)(2,1)S(1)} %collective-permute-done.17.refs_1_) | copy-start | bytes 393220
  111.2 20.2 %collective-permute-start.22 = (bf16[32,2048]{1,0:T(8,128)(2,1)}, bf16[32,2048]{1,0:T(8,128)(2,1)S(1)}, u32[]{:S(2)}, u32[]{:S(2)}) collective-permute-start(bf16[32,2048]{1,0:T(8,128)(2,1)} %get-tuple-element.25), channel_id=1, source_target_pairs={{0,12},{2,14},{4,8},{6,10},{8,4},{10,6},{12,0},{14,2},{1,13},{3,15... | collective-permute-start | bytes 393224 | tf_op jit(solution)/shard_map/ppermute | solution.py:407
  114.2 19.5 %copy-start.19 = (bf16[32,2048]{1,0:T(8,128)(2,1)}, bf16[32,2048]{1,0:T(8,128)(2,1)S(1)}, u32[]{:S(2)}) copy-start(bf16[32,2048]{1,0:T(8,128)(2,1)S(1)} %collective-permute-done.18.refs_2_) | copy-start | bytes 393220
  114.2 19.5 %collective-permute-start.23 = (bf16[32,2048]{1,0:T(8,128)(2,1)}, bf16[32,2048]{1,0:T(8,128)(2,1)S(1)}, u32[]{:S(2)}, u32[]{:S(2)}) collective-permute-start(bf16[32,2048]{1,0:T(8,128)(2,1)} %get-tuple-element.26), channel_id=1, source_target_pairs={{0,14},{2,12},{4,10},{6,8},{8,6},{10,4},{12,2},{14,0},{1,15},{3,13... | collective-permute-start | bytes 393224 | tf_op jit(solution)/shard_map/ppermute | solution.py:407
  116.0 17.8 %copy-start.20 = (bf16[32,2048]{1,0:T(8,128)(2,1)}, bf16[32,2048]{1,0:T(8,128)(2,1)S(1)}, u32[]{:S(2)}) copy-start(bf16[32,2048]{1,0:T(8,128)(2,1)S(1)} %collective-permute-done.19.refs_3_) | copy-start | bytes 393220
  117.7 16.1 %copy-start.21 = (bf16[32,2048]{1,0:T(8,128)(2,1)}, bf16[32,2048]{1,0:T(8,128)(2,1)S(1)}, u32[]{:S(2)}) copy-start(bf16[32,2048]{1,0:T(8,128)(2,1)S(1)} %collective-permute-done.20.refs_4_) | copy-start | bytes 393220
  126.2 7.6 %copy-start.22 = (bf16[32,2048]{1,0:T(8,128)(2,1)}, bf16[32,2048]{1,0:T(8,128)(2,1)S(1)}, u32[]{:S(2)}) copy-start(bf16[32,2048]{1,0:T(8,128)(2,1)S(1)} %collective-permute-done.21.refs_5_) | copy-start | bytes 393220
  131.4 2.3 %copy-start.23 = (bf16[32,2048]{1,0:T(8,128)(2,1)}, bf16[32,2048]{1,0:T(8,128)(2,1)S(1)}, u32[]{:S(2)}) copy-start(bf16[32,2048]{1,0:T(8,128)(2,1)S(1)} %collective-permute-done.22.refs_6_) | copy-start | bytes 393220
  (5 other events, 3.8 us)

commit v3 on v2

v3 whole, which is shorter than its diff:
```python
import functools

import jax
import jax.numpy as jnp
from jax import lax
from jax.experimental import pallas as pl
from jax.experimental.pallas import tpu as pltpu
from jax.sharding import PartitionSpec as P

BF16 = jnp.bfloat16
F32 = jnp.float32
HBM = pl.BlockSpec(memory_space=pltpu.HBM)
SMEM = pl.BlockSpec(memory_space=pltpu.SMEM)


def walks_back(count):
    return count % 2 == 0 and count <= 8


def ring_order(count):
    if walks_back(count):
        return list(range(0, count, 2)) + list(range(1, count, 2))[::-1]
    return list(range(count))


def owner_at(me, offset, count):
    if not walks_back(count):
        return lax.rem(me + offset + count, count)
    place = jnp.where(me % 2 == 0, me // 2, count - 1 - me // 2)
    place = lax.rem(place + offset + count, count)
    return jnp.where(place < count // 2, 2 * place, 2 * (count - 1 - place) + 1)


def starts_of(units):
    starts = [0]
    for unit in units:
        starts.append(starts[-1] + unit.shape[0])
    return starts


def fetch_rows(units, held, sem):
    starts = starts_of(units)
    return [
        pltpu.make_async_copy(unit, held.at[pl.ds(starts[j], unit.shape[0])], sem.at[j])
        for j, unit in enumerate(units)
    ]


def row_of(me, place, count, rows):
    offset, part, parts = place
    return pl.multiple_of((owner_at(me, offset, count) * parts + part) * rows, rows)


def start_all(copies):
    for copy in copies:
        copy.start()


def wait_all(copies):
    for copy in copies:
        copy.wait()


def call(kernel, outs, in_specs, scratch, flops, moved, megabytes=60):
    return pl.pallas_call(
        kernel,
        in_specs=in_specs,
        out_specs=[HBM] * len(outs),
        out_shape=[jax.ShapeDtypeStruct(out, BF16) for out in outs],
        scratch_shapes=scratch,
        compiler_params=pltpu.CompilerParams(vmem_limit_bytes=megabytes << 20),
        cost_estimate=pl.CostEstimate(flops=flops, bytes_accessed=moved, transcendentals=0),
    )


def low_ranks(held, d_held):
    low = jnp.dot(held[...], d_held[...], preferred_element_type=F32)
    return jnp.concatenate([low, jnp.zeros_like(low)], axis=1).astype(BF16)


def stream_product(held, weight, w_held, w_sem):
    bands, depth, _ = w_held.shape
    total = None
    for i in range(bands):
        band_copy(weight, w_held, w_sem, i).wait()
        part = jnp.dot(held[:, i * depth : (i + 1) * depth], w_held[i], preferred_element_type=F32)
        total = part if total is None else total + part
    return total.astype(BF16)


def start_bands(copies, weight, w_held, w_sem):
    start_all(copies)
    for i in range(w_held.shape[0]):
        if i == 2:
            wait_all(copies)
        band_copy(weight, w_held, w_sem, i).start()


def band_copy(weight, w_held, w_sem, i):
    depth = w_held.shape[1]
    return pltpu.make_async_copy(weight.at[pl.ds(i * depth, depth)], w_held.at[i], w_sem.at[i])


def early_rows(ids, units, weight, down):
    fetched, total = len(units), starts_of(units)[-1]
    wide = units[0].shape[1]
    columns = weight.shape[1]
    width, rank = down.shape
    bands = 16

    def kernel(ids, *refs):
        units, refs = refs[:fetched], refs[fetched:]
        weight, down, out, low, held, w_held, d_held, o_held, l_held, sem, w_sem, d_sem, o_sem = refs
        copies = fetch_rows(units, held, sem) + [pltpu.make_async_copy(down, d_held, d_sem)]
        o_copies = [
            pltpu.make_async_copy(l_held, low, o_sem.at[0]),
            pltpu.make_async_copy(o_held, out, o_sem.at[1]),
        ]
        start_bands(copies, weight, w_held, w_sem)
        l_held[...] = low_ranks(held, d_held)
        o_copies[0].start()
        o_held[...] = stream_product(held, weight, w_held, w_sem)
        o_copies[1].start()
        wait_all(o_copies)

    return call(
        kernel,
        [(total, columns), (total, 2 * rank)],
        [SMEM] + [HBM] * (fetched + 2),
        [
            pltpu.VMEM((total, wide), BF16),
            pltpu.VMEM((bands, width // bands, columns), BF16),
            pltpu.VMEM((width, rank), BF16),
            pltpu.VMEM((total, columns), BF16),
            pltpu.VMEM((total, 2 * rank), BF16),
            pltpu.SemaphoreType.DMA((fetched,)),
            pltpu.SemaphoreType.DMA((bands,)),
            pltpu.SemaphoreType.DMA,
            pltpu.SemaphoreType.DMA((2,)),
        ],
        2 * total * width * (columns + rank),
        2 * width * (columns + total + rank),
    )(ids, *units, weight, down)


def late_ranks(ids, units, places, down, early, early_places, slots, count):
    fetched, fresh = len(units), starts_of(units)[-1]
    wide = units[0].shape[1]
    width, rank = down.shape
    total = fresh + early.shape[0]
    rows = early.shape[0] // len(early_places)

    def kernel(ids, *refs):
        units, refs = refs[:fetched], refs[fetched:]
        down, early, slots, out, held, d_held, o_held, s_held, sem, d_sem, e_sem, s_sem, o_sem = refs
        copies = fetch_rows(units, held, sem) + [pltpu.make_async_copy(down, d_held, d_sem)]
        for j, place in enumerate(early_places):
            at = pl.ds(row_of(ids[0], place, count, rows), rows)
            part = early.at[pl.ds(j * rows, rows)]
            copies.append(pltpu.make_async_copy(part, o_held.at[at], e_sem.at[j]))
        copies.append(pltpu.make_async_copy(slots, s_held, s_sem))
        start_all(copies)
        wait_all(copies)
        low = low_ranks(held, d_held)
        starts = starts_of(units)
        for j, place in enumerate(places):
            size = units[j].shape[0]
            at = pl.ds(row_of(ids[0], place, count, size), size)
            o_held[at] = low[starts[j] : starts[j + 1]]
        own = total // count
        at = pl.ds(pl.multiple_of(ids[0] * own, own), own)
        o_held[at, rank:] = s_held[:, rank:]
        copies = [pltpu.make_async_copy(o_held, out.at[i], o_sem.at[i]) for i in range(count)]
        start_all(copies)
        wait_all(copies)

    return call(
        kernel,
        [(count, total, 2 * rank)],
        [SMEM] + [HBM] * (fetched + 3),
        [
            pltpu.VMEM((fresh, wide), BF16),
            pltpu.VMEM((width, rank), BF16),
            pltpu.VMEM((total, 2 * rank), BF16),
            pltpu.VMEM(slots.shape, BF16),
            pltpu.SemaphoreType.DMA((fetched,)),
            pltpu.SemaphoreType.DMA,
            pltpu.SemaphoreType.DMA((len(early_places),)),
            pltpu.SemaphoreType.DMA,
            pltpu.SemaphoreType.DMA((count,)),
        ],
        2 * fresh * width * rank,
        2 * width * (fresh + rank),
    )(ids, *units, down, early, slots)[0]


def base_rows(ids, units, weight):
    fetched, total = len(units), starts_of(units)[-1]
    wide = units[0].shape[1]
    width, columns = weight.shape
    bands = 16

    def kernel(ids, *refs):
        units, refs = refs[:fetched], refs[fetched:]
        weight, out, held, w_held, o_held, sem, w_sem, o_sem = refs
        start_bands(fetch_rows(units, held, sem), weight, w_held, w_sem)
        o_held[...] = stream_product(held, weight, w_held, w_sem)
        copy = pltpu.make_async_copy(o_held, out, o_sem)
        copy.start()
        copy.wait()

    return call(
        kernel,
        [(total, columns)],
        [SMEM] + [HBM] * (fetched + 1),
        [
            pltpu.VMEM((total, wide), BF16),
            pltpu.VMEM((bands, width // bands, columns), BF16),
            pltpu.VMEM((total, columns), BF16),
            pltpu.SemaphoreType.DMA((fetched,)),
            pltpu.SemaphoreType.DMA((bands,)),
            pltpu.SemaphoreType.DMA,
        ],
        2 * total * width * columns,
        2 * width * (columns + total),
    )(ids, *units, weight)[0]


def add_delta(ids, ups, crossed, pieces, low):
    bases = list({id(piece[0]): piece[0] for piece in pieces}.values())
    shares, parts = len(ups), len(bases)
    count, sub, columns = ups[0].shape
    rank = sub * shares
    total = low.shape[1]
    own = total // count
    step = min(512, columns)

    def kernel(ids, *refs):
        ups, base_refs, low = refs[:shares], refs[shares : shares + parts], refs[shares + parts]
        outs = refs[shares + parts + 1 : shares + parts + 1 + count]
        u_held, b_held, l_held, sem, b_sem, l_sem, o_sem = refs[shares + parts + 1 + count :]
        l_copy = pltpu.make_async_copy(low, l_held, l_sem)
        l_copy.start()
        u_copies, b_copies = [], []
        for j, up in enumerate(ups):
            at = pl.multiple_of((ids[1] ^ crossed[j]) * sub, sub)
            u_copies.append(pltpu.make_async_copy(up, u_held.at[:, pl.ds(at, sub)], sem.at[j]))
        for j, (base, begin, size, place) in enumerate(pieces):
            base_ref = base_refs[[b is base for b in bases].index(True)]
            at = pl.ds(row_of(ids[0], place, count, size), size)
            part = base_ref.at[pl.ds(begin, size)]
            b_copies.append(pltpu.make_async_copy(part, b_held.at[at], b_sem.at[j]))
        start_all(u_copies)
        start_all(b_copies)
        l_copy.wait()
        slots = jnp.concatenate(
            [l_held[s, s * own : (s + 1) * own, rank:] for s in range(count)], axis=0
        ).astype(F32)
        wide = jnp.concatenate(
            [jnp.where(slots == s, l_held[s][:, :rank].astype(F32), 0.0) for s in range(count)], axis=1
        ).astype(BF16)
        wait_all(u_copies)
        wait_all(b_copies)
        o_copies = []
        for n in range(0, columns, step):
            cols = slice(n, n + step)
            ups_here = u_held[:, :, cols].reshape(count * rank, step)
            delta = jnp.dot(wide, ups_here, preferred_element_type=F32).astype(BF16)
            b_held[:, cols] = (b_held[:, cols].astype(F32) + delta.astype(F32)).astype(BF16)
            for i in range(count):
                at = pl.ds(pl.multiple_of((ids[0] ^ i) * own, own), own)
                block = b_held.at[at, pl.ds(n, step)]
                o_copies.append(
                    pltpu.make_async_copy(block, outs[i].at[:, pl.ds(n, step)], o_sem.at[n // step, i])
                )
                o_copies[-1].start()
        wait_all(o_copies)

    return call(
        kernel,
        [(own, columns)] * count,
        [SMEM] + [HBM] * (shares + parts + 1),
        [
            pltpu.VMEM((count, rank, columns), BF16),
            pltpu.VMEM((total, columns), BF16),
            pltpu.VMEM(low.shape, BF16),
            pltpu.SemaphoreType.DMA((shares,)),
            pltpu.SemaphoreType.DMA((len(pieces),)),
            pltpu.SemaphoreType.DMA,
            pltpu.SemaphoreType.DMA((columns // step, count)),
        ],
        2 * total * count * rank * columns,
        2 * count * rank * columns,
    )(ids, *ups, *bases, low)


def split_share(ids, turn, up, count, sub):
    columns = up.shape[1] // count

    def kernel(ids, turn, up, out, held, sem, o_sem):
        at = pl.ds(pl.multiple_of(ids[1] * sub, sub), sub)
        copies, o_copies = [], []
        for t in range(count):
            cols = pl.ds(t * columns, columns)
            copies.append(pltpu.make_async_copy(up.at[at, cols], held.at[t], sem.at[t]))
            o_copies.append(pltpu.make_async_copy(held.at[t], out.at[t], o_sem.at[t]))
        start_all(copies)
        for t in range(count):
            copies[t].wait()
            o_copies[t].start()
        wait_all(o_copies)

    return call(
        kernel,
        [(count, sub, columns)],
        [SMEM, SMEM, HBM],
        [
            pltpu.VMEM((count, sub, columns), BF16),
            pltpu.SemaphoreType.DMA((count,)),
            pltpu.SemaphoreType.DMA((count,)),
        ],
        0,
        4 * count * sub * columns,
    )(ids, turn, up)[0]


def join_columns(ids, parts, first, whole=None):
    fetched = len(parts)
    rows, columns = parts[0].shape
    count = lax.axis_size("tensor")
    kept = [] if whole is None else [whole]

    def kernel(ids, *refs):
        parts, (out, held, sem, o_sem) = refs[:fetched], refs[fetched + len(kept) :]
        copies, o_copies = [], []
        for i, part in enumerate(parts):
            at = pl.ds(pl.multiple_of((ids[0] ^ (first + i)) * columns, columns), columns)
            copies.append(pltpu.make_async_copy(part, held.at[i], sem.at[i]))
            o_copies.append(pltpu.make_async_copy(held.at[i], out.at[:, at], o_sem.at[i]))
        start_all(copies)
        for i in range(fetched):
            copies[i].wait()
            o_copies[i].start()
        wait_all(o_copies)

    return pl.pallas_call(
        kernel,
        in_specs=[SMEM] + [HBM] * (fetched + len(kept)),
        out_specs=HBM,
        out_shape=jax.ShapeDtypeStruct((rows, count * columns), BF16),
        scratch_shapes=[
            pltpu.VMEM((fetched, rows, columns), BF16),
            pltpu.SemaphoreType.DMA((fetched,)),
            pltpu.SemaphoreType.DMA((fetched,)),
        ],
        input_output_aliases={fetched + 1: 0} if kept else {},
        compiler_params=pltpu.CompilerParams(vmem_limit_bytes=60 << 20),
    )(ids, *parts, *kept)


def after(value, *earlier):
    return lax.optimization_barrier((value, *earlier))[0]


def body(
    token_input_rows,
    base_projection_weight,
    adapter_down_maps,
    adapter_up_maps,
    token_adapter_index,
    adapter_slot_table,
):
    count = lax.axis_size("tensor")
    groups, seqs = lax.axis_size("groups"), lax.axis_size("seq")
    me = lax.axis_index("tensor")
    rows, width = token_input_rows.shape
    half = rows // 2
    rank = adapter_up_maps.shape[1]
    group_shares = max(1, min(groups, rank // (16 * seqs)))
    sub = rank // (group_shares * seqs)
    share_index = (lax.axis_index("groups") % group_shares) * seqs + lax.axis_index("seq")
    ids = jnp.stack([me, share_index]).astype(jnp.int32)

    order = ring_order(count)
    ahead = [(order[p], order[(p + 1) % count]) for p in range(count)]
    behind = [(b, a) for a, b in ahead]

    matches = token_adapter_index[:, None] == jnp.arange(count, dtype=jnp.int32)[None, :]
    slots = jnp.sum(jnp.where(matches, adapter_slot_table[None, :], 0), axis=1)
    slots = jnp.broadcast_to(slots[:, None], (rows, 2 * rank)).astype(BF16)

    far = count // 2
    down = adapter_down_maps[0]
    swapped = lax.ppermute(ids, "seq", [(i, (i + 1) % seqs) for i in range(seqs)])
    units, places = [token_input_rows], [(0, 0, 1)]
    one_way, other_way = token_input_rows, token_input_rows
    for k in range(1, far):
        one_way = lax.ppermute(one_way, "tensor", ahead)
        other_way = lax.ppermute(other_way, "tensor", behind)
        units += [one_way, other_way]
        places += [(-k, 0, 1), (k, 0, 1)]
    early = units[:far]
    early_base, early_low = early_rows(
        after(ids, *units[far - 1 : far + 1]), early, base_projection_weight, down
    )
    one_way, other_way = lax.optimization_barrier((one_way, other_way, early_low))[:2]
    units.append(lax.ppermute(one_way[:half], "tensor", ahead))
    units.append(lax.ppermute(other_way[half:], "tensor", behind))
    places += [(-far, 0, 2), (far, 1, 2)]
    late, late_places = units[far:], places[far:]

    share = split_share(ids, swapped, adapter_up_maps[0], count, sub)
    ups = [lax.all_to_all(share, "tensor", split_axis=0, concat_axis=0, tiled=True)]
    crossed = [0]
    for axis, size, shared, stride in (("groups", groups, group_shares, seqs), ("seq", seqs, seqs, 1)):
        bit = 1
        while bit < shared:
            ups += [lax.ppermute(u, axis, [(i, i ^ bit) for i in range(size)]) for u in ups]
            crossed += [c ^ (bit * stride) for c in crossed]
            bit *= 2

    low = late_ranks(ids, late, late_places, down, early_low, places[:far], slots, count)
    low_all = lax.all_to_all(low, "tensor", split_axis=0, concat_axis=0, tiled=True)
    late_base = base_rows(after(ids, low), late, base_projection_weight)
    pieces = []
    for base, held, at in ((early_base, early, places[:far]), (late_base, late, late_places)):
        starts = starts_of(held)
        for j, unit in enumerate(held):
            pieces.append((base, starts[j], unit.shape[0], at[j]))
    results = add_delta(ids, ups, crossed, pieces, low_all)
    parts = {0: results[0]}
    for i in reversed(range(1, count)):
        parts[i] = lax.ppermute(results[i], "tensor", [(t, t ^ i) for t in range(count)])
    parts = [parts[i] for i in range(count)]
    cut = 3 * count // 4
    return join_columns(ids, parts[cut:], cut, join_columns(ids, parts[:cut], 0))


def solution(mesh):
    placed = (
        P(("groups", "tensor", "seq"), None),
        P(None, "tensor"),
        P("tensor", None, None),
        P("tensor", None, None),
        P(("groups", "tensor", "seq")),
        P(),
    )
    return jax.shard_map(
        body,
        mesh=mesh,
        in_specs=placed,
        out_specs=P(("groups", "tensor", "seq"), None),
        check_vma=False,
    )
```

time: 138 us -> 125 us (0.906)
  the two profiles are of different devices: /device:TPU:16 before, /device:TPU:0 now
where the time goes in v3:
time: 125 us
  Pallas kernels  45.3 us (36%)
  waiting for transfers between devices  36.8 us (29%)
  starting transfers between devices  36 us (29%)
  local copies, waits for them, and re-layouts  6.12 us (5%)
    ppermute x3, waiting for transfers between devices, body(): other_way = lax.ppermute(other_way, 'tensor', behind)  16 us
    pallas_call x1, Pallas kernels, early_rows(): call(kernel, [(total, columns), (total, 2 * rank)], [SMEM] + [HBM] * (fet...  14.7 us
    ppermute x7, waiting for transfers between devices, body(): lax.ppermute(results[i], 'tensor', [(t, t ^ i) for t in range(count)])  14.4 us
    pallas_call x1, Pallas kernels, base_rows(): call(kernel, [(total, columns)], [SMEM] + [HBM] * (fetched + 1), [pltpu.V...  13.8 us
    ppermute x7, starting transfers between devices, body(): lax.ppermute(results[i], 'tensor', [(t, t ^ i) for t in range(count)])  11.7 us
    ppermute x3, starting transfers between devices, body(): other_way = lax.ppermute(other_way, 'tensor', behind)  6.02 us
    all_to_all x1, starting transfers between devices, body(): lax.all_to_all(share, 'tensor', split_axis=0, concat_axis=0, tiled=True)  6.01 us
    unnamed x49, local copies, waits for them, and re-layouts  5.39 us
  transfers between devices with their start and end apart: 21, of which 9 were waited for; matrix products, arithmetic and copies ran while one was open for 2% of the time, Pallas kernels for 31%

profile of v3, /device:TPU:0, one launch (start us, length us, event | category | flops | bytes accessed | tf_op | source)
XLA Modules:
  0.0 124.8 jit_solution(3572917670859785898)
XLA Ops:
  0.0 3.0 %collective-permute-start.6 = (bf16[32,8192]{1,0:T(8,128)(2,1)}, bf16[32,8192]{1,0:T(8,128)(2,1)S(1)}, u32[]{:S(2)}, u32[]{:S(2)}) collective-permute-start(bf16[32,8192]{1,0:T(8,128)(2,1)} %refs_0_.1), channel_id=1, source_target_pairs={{4,0},{8,4},{12,8},{14,12},{10,14},{6,10},{2,6},{0,2},{5,1},{9,5},... | collective-permute-start | bytes 1572872 | tf_op jit(solution)/shard_map/ppermute | solution.py:399
  3.0 0.1 collective-permute-start.4
  3.1 12.1 %collective-permute-done.6.refs_2_ = bf16[32,8192]{1,0:T(8,128)(2,1)S(1)} collective-permute-done((bf16[32,8192]{1,0:T(8,128)(2,1)}, bf16[32,8192]{1,0:T(8,128)(2,1)S(1)}, u32[]{:S(2)}, u32[]{:S(2)}) %collective-permute-start.6) | collective-permute-done | bytes 524320 | tf_op jit(solution)/shard_map/ppermute | solution.py:399
  15.2 1.7 %collective-permute-start.7 = (bf16[32,8192]{1,0:T(8,128)(2,1)S(1)}, bf16[32,8192]{1,0:T(8,128)(2,1)S(1)}, u32[]{:S(2)}, u32[]{:S(2)}) collective-permute-start(bf16[32,8192]{1,0:T(8,128)(2,1)S(1)} %collective-permute-done.6.refs_2_), channel_id=1, source_target_pairs={{4,0},{8,4},{12,8},{14,12},{10,14},{6,10},{2,6},{0,2},{5,1},{9,5},... | collective-permute-start | bytes 1572872 | tf_op jit(solution)/shard_map/ppermute | solution.py:399
  16.9 0.3 collective-permute-start.5
  17.2 0.1 pad_add_fusion.ids
  17.3 0.0 collective-permute-start
  17.3 1.1 collective-permute-done.turn
  18.4 0.5 copy-done.21
  18.9 2.5 %shard_map.64 = bf16[8,16,2048]{2,1,0:T(8,128)(2,1)} custom-call(s32[2]{0:T(128)} %copy-done.20, s32[2]{0:T(128)} %copy-done.21, bf16[64,16384]{1,0:T(8,128)(2,1)} %bitcast.6), custom_call_target="tpu_custom_call" | custom-call | bytes 1048576 | tf_op jit(solution)/shard_map/pallas_call | solution.py:313
  21.4 6.0 %all-to-all-start = ((bf16[8,16,2048]{2,1,0:T(8,128)(2,1)}), bf16[8,16,2048]{2,1,0:T(8,128)(2,1)S(1)}, u32[]{:S(2)}, u32[]{:S(2)}) async-start(bf16[8,16,2048]{2,1,0:T(8,128)(2,1)} %shard_map.64), calls=%async_computation | async-start | bytes 1048576 | tf_op jit(solution)/shard_map/all_to_all | solution.py:413
  27.5 0.8 collective-permute-done.7.refs_0_
  28.3 1.4 %collective-permute-start.9 = (bf16[32,8192]{1,0:T(8,128)(2,1)S(1)}, bf16[32,8192]{1,0:T(8,128)(2,1)S(1)}, u32[]{:S(2)}, u32[]{:S(2)}) collective-permute-start(bf16[32,8192]{1,0:T(8,128)(2,1)S(1)} %collective-permute-done.7.refs_0_), channel_id=1, source_target_pairs={{4,0},{8,4},{12,8},{14,12},{10,14},{6,10},{2,6},{0,2},{5,1},{9,5},... | collective-permute-start | bytes 1572872 | tf_op jit(solution)/shard_map/ppermute | solution.py:399
  29.6 0.7 collective-permute-start.8
  30.3 1.8 %copy.9 = bf16[1,8192,64]{2,1,0:T(8,128)(2,1)} copy(bf16[1,8192,64]{1,2,0:T(8,128)(2,1)S(1)} %copy-done.7) | data formatting | bytes 2097152 | tf_op args[2]
  32.1 14.7 %shard_map.65 = (bf16[128,2048]{1,0:T(8,128)(2,1)}, bf16[128,128]{1,0:T(8,128)(2,1)}) custom-call(s32[2]{0:T(128)} %copy-done.20, bf16[32,8192]{1,0:T(8,128)(2,1)} %refs_0_.1, bf16[32,8192]{1,0:T(8,128)(2,1)} %copy-done.9, bf16[32,8192]{1,0:T(8,128)(2,1)} %copy-done.8, bf16[32,8192]{1,0:T(8,128)(2,1)} %collective-permute-done.5.refs_3_, ...), custom_call_target="tpu_custom_call" | custom-call | flops 4429185024 | bytes 36700160 | tf_op jit(solution)/shard_map/pallas_call | solution.py:126
  46.8 3.1 %collective-permute-done.9.refs_2_ = bf16[32,8192]{1,0:T(8,128)(2,1)S(1)} collective-permute-done((bf16[32,8192]{1,0:T(8,128)(2,1)S(1)}, bf16[32,8192]{1,0:T(8,128)(2,1)S(1)}, u32[]{:S(2)}, u32[]{:S(2)}) %collective-permute-start.9) | collective-permute-done | bytes 524320 | tf_op jit(solution)/shard_map/ppermute | solution.py:399
  49.9 4.3 %collective-permute-start.10 = (bf16[16,8192]{1,0:T(8,128)(2,1)S(1)}, bf16[16,8192]{1,0:T(8,128)(2,1)S(1)}, u32[]{:S(2)}, u32[]{:S(2)}) collective-permute-start(bf16[16,8192]{1,0:T(8,128)(2,1)S(1)} %slice.6), channel_id=1, source_target_pairs={{0,4},{4,8},{8,12},{12,14},{14,10},{10,6},{6,2},{2,0},{1,5},{5,9},... | collective-permute-start | bytes 786440 | tf_op jit(solution)/shard_map/ppermute | solution.py:407
  54.2 0.1 collective-permute-start.11
  54.3 1.6 %collective-permute-start.1 = (bf16[8,16,2048]{2,1,0:T(8,128)(2,1)S(1)}, bf16[8,16,2048]{2,1,0:T(8,128)(2,1)S(1)}, u32[]{:S(2)}, u32[]{:S(2)}) collective-permute-start(bf16[8,16,2048]{2,1,0:T(8,128)(2,1)S(1)} %all-to-all-done.refs_0_), channel_id=1, source_target_pairs={{0,16},{16,0},{1,17},{17,1},{2,18},{18,2},{3,19},{19,3},{4,20},{20... | collective-permute-start | bytes 1572872 | tf_op jit(solution)/shard_map/ppermute | solution.py:418
  55.9 0.1 select_reduce_fusion
  56.0 3.0 %collective-permute-done.10.refs_3_ = bf16[16,8192]{1,0:T(8,128)(2,1)S(1)} collective-permute-done((bf16[16,8192]{1,0:T(8,128)(2,1)S(1)}, bf16[16,8192]{1,0:T(8,128)(2,1)S(1)}, u32[]{:S(2)}, u32[]{:S(2)}) %collective-permute-start.10) | collective-permute-done | bytes 262176 | tf_op jit(solution)/shard_map/ppermute | solution.py:407
  59.0 2.3 %collective-permute-done.11.refs_4_ = bf16[16,8192]{1,0:T(8,128)(2,1)S(1)} collective-permute-done((bf16[16,8192]{1,0:T(8,128)(2,1)S(1)}, bf16[16,8192]{1,0:T(8,128)(2,1)S(1)}, u32[]{:S(2)}, u32[]{:S(2)}) %collective-permute-start.11) | collective-permute-done | bytes 262176 | tf_op jit(solution)/shard_map/ppermute | solution.py:408
  61.3 0.7 broadcast_in_dim.23.refs_7_
  62.0 4.6 %shard_map.66 = bf16[8,256,128]{2,1,0:T(8,128)(2,1)} custom-call(s32[2]{0:T(128)} %copy-done.20, bf16[32,8192]{1,0:T(8,128)(2,1)} %copy-done.2, bf16[32,8192]{1,0:T(8,128)(2,1)} %copy-done.1, bf16[32,8192]{1,0:T(8,128)(2,1)} %copy-done, bf16[16,8192]{1,0:T(8,128)(2,1)} %copy-done.5, bf16[16,8192]{1,0:T(8,128)(2,1)} %copy-done.6, bf16[8192,64]{1,0:T(8,128)(2,1)} %bitcast.5, ...), custom_call_target="tpu_custom_call" | custom-call | flops 134217728 | bytes 3145728 | tf_op jit(solution)/shard_map/pallas_call | solution.py:177
  66.6 4.6 %all-to-all-start.1 = ((bf16[8,256,128]{2,1,0:T(8,128)(2,1)}), bf16[8,256,128]{2,1,0:T(8,128)(2,1)S(1)}, u32[]{:S(2)}, u32[]{:S(2)}) async-start(bf16[8,256,128]{2,1,0:T(8,128)(2,1)} %shard_map.66), calls=%async_computation.1 | async-start | bytes 1048576 | tf_op jit(solution)/shard_map/all_to_all | solution.py:423
  71.2 0.1 collective-permute-start.2
  71.3 0.5 collective-permute-start.3
  71.8 13.8 %shard_map.67.refs_5_ = bf16[128,2048]{1,0:T(8,128)(2,1)} custom-call(s32[2]{0:T(128)} %copy-done.20, bf16[32,8192]{1,0:T(8,128)(2,1)} %copy-done.2, bf16[32,8192]{1,0:T(8,128)(2,1)} %copy-done.1, bf16[32,8192]{1,0:T(8,128)(2,1)} %copy-done, bf16[16,8192]{1,0:T(8,128)(2,1)} %copy-done.5, bf16[16,8192]{1,0:T(8,128)(2,1)} %copy-done.6, bf16[8192,2048]{1,0:T(8,128)(2,1)} %refs_5_.1), custom_call_target="tpu_custom_call" | custom-call | flops 4294967296 | bytes 35651584 | tf_op jit(solution)/shard_map/pallas_call | solution.py:212
  85.7 0.7 copy-done.11
  86.4 0.2 copy-done.12
  86.6 0.2 copy-done.4
  86.8 4.8 %shard_map.68 = (bf16[32,2048]{1,0:T(8,128)(2,1)}, bf16[32,2048]{1,0:T(8,128)(2,1)}, bf16[32,2048]{1,0:T(8,128)(2,1)}, bf16[32,2048]{1,0:T(8,128)(2,1)}, bf16[32...) custom-call(s32[2]{0:T(128)} %copy-done.20, ...), custom_call_target="tpu_custom_call" | custom-call | flops 536870912 | bytes 2097152 | tf_op jit(solution)/shard_map/pallas_call | solution.py:279
  91.5 2.0 %collective-permute-start.14 = (bf16[32,2048]{1,0:T(8,128)(2,1)}, bf16[32,2048]{1,0:T(8,128)(2,1)S(1)}, u32[]{:S(2)}, u32[]{:S(2)}) collective-permute-start(bf16[32,2048]{1,0:T(8,128)(2,1)} %get-tuple-element.28), channel_id=1, source_target_pairs={{0,2},{2,0},{4,6},{6,4},{8,10},{10,8},{12,14},{14,12},{1,3},{3,1},... | collective-permute-start | bytes 393224 | tf_op jit(solution)/shard_map/ppermute | solution.py:433
  93.6 1.5 %collective-permute-start.15 = (bf16[32,2048]{1,0:T(8,128)(2,1)}, bf16[32,2048]{1,0:T(8,128)(2,1)S(1)}, u32[]{:S(2)}, u32[]{:S(2)}) collective-permute-start(bf16[32,2048]{1,0:T(8,128)(2,1)} %get-tuple-element.29), channel_id=1, source_target_pairs={{0,4},{2,6},{4,0},{6,2},{8,12},{10,14},{12,8},{14,10},{1,5},{3,7},... | collective-permute-start | bytes 393224 | tf_op jit(solution)/shard_map/ppermute | solution.py:433
  95.0 0.1 collective-permute-start.16
  95.1 2.8 %collective-permute-start.17 = (bf16[32,2048]{1,0:T(8,128)(2,1)}, bf16[32,2048]{1,0:T(8,128)(2,1)S(1)}, u32[]{:S(2)}, u32[]{:S(2)}) collective-permute-start(bf16[32,2048]{1,0:T(8,128)(2,1)} %get-tuple-element.31), channel_id=1, source_target_pairs={{0,8},{2,10},{4,12},{6,14},{8,0},{10,2},{12,4},{14,6},{1,9},{3,11}... | collective-permute-start | bytes 393224 | tf_op jit(solution)/shard_map/ppermute | solution.py:433
  98.0 1.5 %collective-permute-start.18 = (bf16[32,2048]{1,0:T(8,128)(2,1)}, bf16[32,2048]{1,0:T(8,128)(2,1)S(1)}, u32[]{:S(2)}, u32[]{:S(2)}) collective-permute-start(bf16[32,2048]{1,0:T(8,128)(2,1)} %get-tuple-element.32), channel_id=1, source_target_pairs={{0,10},{2,8},{4,14},{6,12},{8,2},{10,0},{12,6},{14,4},{1,11},{3,9}... | collective-permute-start | bytes 393224 | tf_op jit(solution)/shard_map/ppermute | solution.py:433
  99.4 3.3 %collective-permute-start.12 = (bf16[32,2048]{1,0:T(8,128)(2,1)}, bf16[32,2048]{1,0:T(8,128)(2,1)S(1)}, u32[]{:S(2)}, u32[]{:S(2)}) collective-permute-start(bf16[32,2048]{1,0:T(8,128)(2,1)} %get-tuple-element.25), channel_id=1, source_target_pairs={{0,12},{2,14},{4,8},{6,10},{8,4},{10,6},{12,0},{14,2},{1,13},{3,15... | collective-permute-start | bytes 393224 | tf_op jit(solution)/shard_map/ppermute | solution.py:433
  102.7 1.9 %collective-permute-done.15.refs_2_ = bf16[32,2048]{1,0:T(8,128)(2,1)S(1)} collective-permute-done((bf16[32,2048]{1,0:T(8,128)(2,1)}, bf16[32,2048]{1,0:T(8,128)(2,1)S(1)}, u32[]{:S(2)}, u32[]{:S(2)}) %collective-permute-start.15) | collective-permute-done | bytes 131104 | tf_op jit(solution)/shard_map/ppermute | solution.py:433
  104.6 0.6 collective-permute-start.13
  105.2 0.3 collective-permute-done.16.refs_3_
  105.5 12.2 %collective-permute-done.18.refs_5_ = bf16[32,2048]{1,0:T(8,128)(2,1)S(1)} collective-permute-done((bf16[32,2048]{1,0:T(8,128)(2,1)}, bf16[32,2048]{1,0:T(8,128)(2,1)S(1)}, u32[]{:S(2)}, u32[]{:S(2)}) %collective-permute-start.18) | collective-permute-done | bytes 131104 | tf_op jit(solution)/shard_map/ppermute | solution.py:433
  117.8 0.6 copy-done.19
  118.4 2.6 %shard_map.69.refs_2_ = bf16[32,16384]{1,0:T(8,128)(2,1)} custom-call(s32[2]{0:T(128)} %copy-done.20, bf16[32,2048]{1,0:T(8,128)(2,1)} %get-tuple-element.27.refs_0_, bf16[32,2048]{1,0:T(8,128)(2,1)} %copy-done.15, bf16[32,2048]{1,0:T(8,128)(2,1)} %copy-done.16, bf16[32,2048]{1,0:T(8,128)(2,1)} %copy-done.17, bf16[32,2048]{1,0:T(8,128)(2,1)} %copy-done.18, ...), custom_call_target="tpu_custom_call" | custom-call | tf_op jit(solution)/shard_map/pallas_call | solution.py:346
  121.1 0.6 copy-done.13
  121.7 0.7 copy-done.14
  122.4 2.3 %shard_map.70 = bf16[32,16384]{1,0:T(8,128)(2,1)} custom-call(s32[2]{0:T(128)} %copy-done.20, bf16[32,2048]{1,0:T(8,128)(2,1)} %copy-done.13, bf16[32,2048]{1,0:T(8,128)(2,1)} %copy-done.14, bf16[32,16384]{1,0:T(8,128)(2,1)} %shard_map.69.refs_2_), custom_call_target="tpu_custom_call", output_to_operand_aliasing={{}: (3, {})} | custom-call | tf_op jit(solution)/shard_map/pallas_call | solution.py:346
  (56 shorter events, 0.2 us)
Async XLA Ops:
  0.0 30.3 %copy-start.7 = (bf16[1,8192,64]{1,2,0:T(8,128)(2,1)S(1)}, bf16[1,8192,64]{1,2,0:T(8,128)(2,1)}, u32[]{:S(2)}) copy-start(bf16[1,8192,64]{1,2,0:T(8,128)(2,1)} %param.8) | copy-start | bytes 3145732
  0.0 15.2 %collective-permute-start.6 = (bf16[32,8192]{1,0:T(8,128)(2,1)}, bf16[32,8192]{1,0:T(8,128)(2,1)S(1)}, u32[]{:S(2)}, u32[]{:S(2)}) collective-permute-start(bf16[32,8192]{1,0:T(8,128)(2,1)} %refs_0_.1), channel_id=1, source_target_pairs={{4,0},{8,4},{12,8},{14,12},{10,14},{6,10},{2,6},{0,2},{5,1},{9,5},... | collective-permute-start | bytes 1572872 | tf_op jit(solution)/shard_map/ppermute | solution.py:399
  3.0 13.9 %collective-permute-start.4 = (bf16[32,8192]{1,0:T(8,128)(2,1)}, bf16[32,8192]{1,0:T(8,128)(2,1)S(1)}, u32[]{:S(2)}, u32[]{:S(2)}) collective-permute-start(bf16[32,8192]{1,0:T(8,128)(2,1)} %refs_0_.1), channel_id=1, source_target_pairs={{0,4},{4,8},{8,12},{12,14},{14,10},{10,6},{6,2},{2,0},{1,5},{5,9},... | collective-permute-start | bytes 1572872 | tf_op jit(solution)/shard_map/ppermute | solution.py:398
  15.2 12.3 %copy-start.8 = (bf16[32,8192]{1,0:T(8,128)(2,1)}, bf16[32,8192]{1,0:T(8,128)(2,1)S(1)}, u32[]{:S(2)}) copy-start(bf16[32,8192]{1,0:T(8,128)(2,1)S(1)} %collective-permute-done.6.refs_2_) | copy-start | bytes 1572868
  15.2 13.1 %collective-permute-start.7 = (bf16[32,8192]{1,0:T(8,128)(2,1)S(1)}, bf16[32,8192]{1,0:T(8,128)(2,1)S(1)}, u32[]{:S(2)}, u32[]{:S(2)}) collective-permute-start(bf16[32,8192]{1,0:T(8,128)(2,1)S(1)} %collective-permute-done.6.refs_2_), channel_id=1, source_target_pairs={{4,0},{8,4},{12,8},{14,12},{10,14},{6,10},{2,6},{0,2},{5,1},{9,5},... | collective-permute-start | bytes 1572872 | tf_op jit(solution)/shard_map/ppermute | solution.py:399
  16.9 12.8 %copy-start.9 = (bf16[32,8192]{1,0:T(8,128)(2,1)}, bf16[32,8192]{1,0:T(8,128)(2,1)S(1)}, u32[]{:S(2)}) copy-start(bf16[32,8192]{1,0:T(8,128)(2,1)S(1)} %collective-permute-done.4.refs_1_) | copy-start | bytes 1572868
  16.9 12.8 %collective-permute-start.5 = (bf16[32,8192]{1,0:T(8,128)(2,1)S(1)}, bf16[32,8192]{1,0:T(8,128)(2,1)}, u32[]{:S(2)}, u32[]{:S(2)}) collective-permute-start(bf16[32,8192]{1,0:T(8,128)(2,1)S(1)} %collective-permute-done.4.refs_1_), channel_id=1, source_target_pairs={{0,4},{4,8},{8,12},{12,14},{14,10},{10,6},{6,2},{2,0},{1,5},{5,9},... | collective-permute-start | bytes 1572872 | tf_op jit(solution)/shard_map/ppermute | solution.py:398
  17.3 1.1 copy-start.20
  17.3 1.1 collective-permute-start
  18.4 0.5 copy-start.21
  21.4 32.8 %all-to-all-start = ((bf16[8,16,2048]{2,1,0:T(8,128)(2,1)}), bf16[8,16,2048]{2,1,0:T(8,128)(2,1)S(1)}, u32[]{:S(2)}, u32[]{:S(2)}) async-start(bf16[8,16,2048]{2,1,0:T(8,128)(2,1)} %shard_map.64), calls=%async_computation | async-start | bytes 1048576 | tf_op jit(solution)/shard_map/all_to_all | solution.py:413
  28.3 18.5 %copy-start.2 = (bf16[32,8192]{1,0:T(8,128)(2,1)}, bf16[32,8192]{1,0:T(8,128)(2,1)S(1)}, u32[]{:S(2)}) copy-start(bf16[32,8192]{1,0:T(8,128)(2,1)S(1)} %collective-permute-done.7.refs_0_) | copy-start | bytes 1572868
  28.3 21.6 %collective-permute-start.9 = (bf16[32,8192]{1,0:T(8,128)(2,1)S(1)}, bf16[32,8192]{1,0:T(8,128)(2,1)S(1)}, u32[]{:S(2)}, u32[]{:S(2)}) collective-permute-start(bf16[32,8192]{1,0:T(8,128)(2,1)S(1)} %collective-permute-done.7.refs_0_), channel_id=1, source_target_pairs={{4,0},{8,4},{12,8},{14,12},{10,14},{6,10},{2,6},{0,2},{5,1},{9,5},... | collective-permute-start | bytes 1572872 | tf_op jit(solution)/shard_map/ppermute | solution.py:399
  29.6 20.2 %collective-permute-start.8 = (bf16[32,8192]{1,0:T(8,128)(2,1)}, bf16[32,8192]{1,0:T(8,128)(2,1)S(1)}, u32[]{:S(2)}, u32[]{:S(2)}) collective-permute-start(bf16[32,8192]{1,0:T(8,128)(2,1)} %collective-permute-done.5.refs_3_), channel_id=1, source_target_pairs={{0,4},{4,8},{8,12},{12,14},{14,10},{10,6},{6,2},{2,0},{1,5},{5,9},... | collective-permute-start | bytes 1572872 | tf_op jit(solution)/shard_map/ppermute | solution.py:398
  32.1 23.8 %copy-start.22 = (s32[8]{0:T(128)S(1)}, s32[8]{0:T(128)}, u32[]{:S(2)}) copy-start(s32[8]{0:T(128)} %param.11) | copy-start | bytes 100
  32.1 23.8 %copy-start.23 = (s32[32]{0:T(128)S(1)}, s32[32]{0:T(128)}, u32[]{:S(2)}) copy-start(s32[32]{0:T(128)} %param.10) | copy-start | bytes 388
  49.8 12.1 %copy-start = (bf16[32,8192]{1,0:T(8,128)(2,1)}, bf16[32,8192]{1,0:T(8,128)(2,1)S(1)}, u32[]{:S(2)}) copy-start(bf16[32,8192]{1,0:T(8,128)(2,1)S(1)} %collective-permute-done.9.refs_2_) | copy-start | bytes 1572868
  49.8 12.1 %copy-start.1 = (bf16[32,8192]{1,0:T(8,128)(2,1)}, bf16[32,8192]{1,0:T(8,128)(2,1)S(1)}, u32[]{:S(2)}) copy-start(bf16[32,8192]{1,0:T(8,128)(2,1)S(1)} %collective-permute-done.8.refs_1_) | copy-start | bytes 1572868
  49.9 9.1 %collective-permute-start.10 = (bf16[16,8192]{1,0:T(8,128)(2,1)S(1)}, bf16[16,8192]{1,0:T(8,128)(2,1)S(1)}, u32[]{:S(2)}, u32[]{:S(2)}) collective-permute-start(bf16[16,8192]{1,0:T(8,128)(2,1)S(1)} %slice.6), channel_id=1, source_target_pairs={{0,4},{4,8},{8,12},{12,14},{14,10},{10,6},{6,2},{2,0},{1,5},{5,9},... | collective-permute-start | bytes 786440 | tf_op jit(solution)/shard_map/ppermute | solution.py:407
  54.2 7.0 %collective-permute-start.11 = (bf16[16,8192]{1,0:T(8,128)(2,1)S(1)}, bf16[16,8192]{1,0:T(8,128)(2,1)S(1)}, u32[]{:S(2)}, u32[]{:S(2)}) collective-permute-start(bf16[16,8192]{1,0:T(8,128)(2,1)S(1)} %slice.7), channel_id=1, source_target_pairs={{4,0},{8,4},{12,8},{14,12},{10,14},{6,10},{2,6},{0,2},{5,1},{9,5},... | collective-permute-start | bytes 786440 | tf_op jit(solution)/shard_map/ppermute | solution.py:408
  54.3 16.9 %copy-start.3 = (bf16[8,16,2048]{2,1,0:T(8,128)(2,1)}, bf16[8,16,2048]{2,1,0:T(8,128)(2,1)S(1)}, u32[]{:S(2)}) copy-start(bf16[8,16,2048]{2,1,0:T(8,128)(2,1)S(1)} %all-to-all-done.refs_0_) | copy-start | bytes 1572868
  54.3 17.0 %collective-permute-start.1 = (bf16[8,16,2048]{2,1,0:T(8,128)(2,1)S(1)}, bf16[8,16,2048]{2,1,0:T(8,128)(2,1)S(1)}, u32[]{:S(2)}, u32[]{:S(2)}) collective-permute-start(bf16[8,16,2048]{2,1,0:T(8,128)(2,1)S(1)} %all-to-all-done.refs_0_), channel_id=1, source_target_pairs={{0,16},{16,0},{1,17},{17,1},{2,18},{18,2},{3,19},{19,3},{4,20},{20... | collective-permute-start | bytes 1572872 | tf_op jit(solution)/shard_map/ppermute | solution.py:418
  59.0 3.0 %copy-start.5 = (bf16[16,8192]{1,0:T(8,128)(2,1)}, bf16[16,8192]{1,0:T(8,128)(2,1)S(1)}, u32[]{:S(2)}) copy-start(bf16[16,8192]{1,0:T(8,128)(2,1)S(1)} %collective-permute-done.10.refs_3_) | copy-start | bytes 786436
  61.3 0.7 copy-start.6
  66.6 19.1 %all-to-all-start.1 = ((bf16[8,256,128]{2,1,0:T(8,128)(2,1)}), bf16[8,256,128]{2,1,0:T(8,128)(2,1)S(1)}, u32[]{:S(2)}, u32[]{:S(2)}) async-start(bf16[8,256,128]{2,1,0:T(8,128)(2,1)} %shard_map.66), calls=%async_computation.1 | async-start | bytes 1048576 | tf_op jit(solution)/shard_map/all_to_all | solution.py:423
  71.2 14.4 %collective-permute-start.2 = (bf16[8,16,2048]{2,1,0:T(8,128)(2,1)S(1)}, bf16[8,16,2048]{2,1,0:T(8,128)(2,1)S(1)}, u32[]{:S(2)}, u32[]{:S(2)}) collective-permute-start(bf16[8,16,2048]{2,1,0:T(8,128)(2,1)S(1)} %all-to-all-done.refs_0_), channel_id=1, source_target_pairs={{0,1},{1,0},{2,3},{3,2},{4,5},{5,4},{6,7},{7,6},{8,9},{9,8},{10,11... | collective-permute-start | bytes 1572872 | tf_op jit(solution)/shard_map/ppermute | solution.py:418
  71.3 14.3 %copy-start.10 = (bf16[8,16,2048]{2,1,0:T(8,128)(2,1)}, bf16[8,16,2048]{2,1,0:T(8,128)(2,1)S(1)}, u32[]{:S(2)}) copy-start(bf16[8,16,2048]{2,1,0:T(8,128)(2,1)S(1)} %collective-permute-done.1.refs_1_) | copy-start | bytes 1572868
  71.3 14.3 %collective-permute-start.3 = (bf16[8,16,2048]{2,1,0:T(8,128)(2,1)S(1)}, bf16[8,16,2048]{2,1,0:T(8,128)(2,1)S(1)}, u32[]{:S(2)}, u32[]{:S(2)}) collective-permute-start(bf16[8,16,2048]{2,1,0:T(8,128)(2,1)S(1)} %collective-permute-done.1.refs_1_), channel_id=1, source_target_pairs={{0,1},{1,0},{2,3},{3,2},{4,5},{5,4},{6,7},{7,6},{8,9},{9,8},{10,11... | collective-permute-start | bytes 1572872 | tf_op jit(solution)/shard_map/ppermute | solution.py:418
  85.6 0.8 copy-start.11
  85.7 1.0 copy-start.12
  85.7 1.1 copy-start.4
  91.5 7.9 %collective-permute-start.14 = (bf16[32,2048]{1,0:T(8,128)(2,1)}, bf16[32,2048]{1,0:T(8,128)(2,1)S(1)}, u32[]{:S(2)}, u32[]{:S(2)}) collective-permute-start(bf16[32,2048]{1,0:T(8,128)(2,1)} %get-tuple-element.28), channel_id=1, source_target_pairs={{0,2},{2,0},{4,6},{6,4},{8,10},{10,8},{12,14},{14,12},{1,3},{3,1},... | collective-permute-start | bytes 393224 | tf_op jit(solution)/shard_map/ppermute | solution.py:433
  93.6 11.0 %collective-permute-start.15 = (bf16[32,2048]{1,0:T(8,128)(2,1)}, bf16[32,2048]{1,0:T(8,128)(2,1)S(1)}, u32[]{:S(2)}, u32[]{:S(2)}) collective-permute-start(bf16[32,2048]{1,0:T(8,128)(2,1)} %get-tuple-element.29), channel_id=1, source_target_pairs={{0,4},{2,6},{4,0},{6,2},{8,12},{10,14},{12,8},{14,10},{1,5},{3,7},... | collective-permute-start | bytes 393224 | tf_op jit(solution)/shard_map/ppermute | solution.py:433
  95.0 10.5 %collective-permute-start.16 = (bf16[32,2048]{1,0:T(8,128)(2,1)}, bf16[32,2048]{1,0:T(8,128)(2,1)S(1)}, u32[]{:S(2)}, u32[]{:S(2)}) collective-permute-start(bf16[32,2048]{1,0:T(8,128)(2,1)} %get-tuple-element.30), channel_id=1, source_target_pairs={{0,6},{2,4},{4,2},{6,0},{8,14},{10,12},{12,10},{14,8},{1,7},{3,5},... | collective-permute-start | bytes 393224 | tf_op jit(solution)/shard_map/ppermute | solution.py:433
  95.1 10.4 %collective-permute-start.17 = (bf16[32,2048]{1,0:T(8,128)(2,1)}, bf16[32,2048]{1,0:T(8,128)(2,1)S(1)}, u32[]{:S(2)}, u32[]{:S(2)}) collective-permute-start(bf16[32,2048]{1,0:T(8,128)(2,1)} %get-tuple-element.31), channel_id=1, source_target_pairs={{0,8},{2,10},{4,12},{6,14},{8,0},{10,2},{12,4},{14,6},{1,9},{3,11}... | collective-permute-start | bytes 393224 | tf_op jit(solution)/shard_map/ppermute | solution.py:433
  98.0 19.8 %collective-permute-start.18 = (bf16[32,2048]{1,0:T(8,128)(2,1)}, bf16[32,2048]{1,0:T(8,128)(2,1)S(1)}, u32[]{:S(2)}, u32[]{:S(2)}) collective-permute-start(bf16[32,2048]{1,0:T(8,128)(2,1)} %get-tuple-element.32), channel_id=1, source_target_pairs={{0,10},{2,8},{4,14},{6,12},{8,2},{10,0},{12,6},{14,4},{1,11},{3,9}... | collective-permute-start | bytes 393224 | tf_op jit(solution)/shard_map/ppermute | solution.py:433
  99.4 18.3 %copy-start.15 = (bf16[32,2048]{1,0:T(8,128)(2,1)}, bf16[32,2048]{1,0:T(8,128)(2,1)S(1)}, u32[]{:S(2)}) copy-start(bf16[32,2048]{1,0:T(8,128)(2,1)S(1)} %collective-permute-done.14.refs_1_) | copy-start | bytes 393220
  99.4 21.6 %collective-permute-start.12 = (bf16[32,2048]{1,0:T(8,128)(2,1)}, bf16[32,2048]{1,0:T(8,128)(2,1)S(1)}, u32[]{:S(2)}, u32[]{:S(2)}) collective-permute-start(bf16[32,2048]{1,0:T(8,128)(2,1)} %get-tuple-element.25), channel_id=1, source_target_pairs={{0,12},{2,14},{4,8},{6,10},{8,4},{10,6},{12,0},{14,2},{1,13},{3,15... | collective-permute-start | bytes 393224 | tf_op jit(solution)/shard_map/ppermute | solution.py:433
  104.6 13.1 %copy-start.16 = (bf16[32,2048]{1,0:T(8,128)(2,1)}, bf16[32,2048]{1,0:T(8,128)(2,1)S(1)}, u32[]{:S(2)}) copy-start(bf16[32,2048]{1,0:T(8,128)(2,1)S(1)} %collective-permute-done.15.refs_2_) | copy-start | bytes 393220
  104.6 16.4 %collective-permute-start.13 = (bf16[32,2048]{1,0:T(8,128)(2,1)}, bf16[32,2048]{1,0:T(8,128)(2,1)S(1)}, u32[]{:S(2)}, u32[]{:S(2)}) collective-permute-start(bf16[32,2048]{1,0:T(8,128)(2,1)} %get-tuple-element.26), channel_id=1, source_target_pairs={{0,14},{2,12},{4,10},{6,8},{8,6},{10,4},{12,2},{14,0},{1,15},{3,13... | collective-permute-start | bytes 393224 | tf_op jit(solution)/shard_map/ppermute | solution.py:433
  105.5 12.2 %copy-start.17 = (bf16[32,2048]{1,0:T(8,128)(2,1)}, bf16[32,2048]{1,0:T(8,128)(2,1)S(1)}, u32[]{:S(2)}) copy-start(bf16[32,2048]{1,0:T(8,128)(2,1)S(1)} %collective-permute-done.16.refs_3_) | copy-start | bytes 393220
  105.5 12.2 %copy-start.18 = (bf16[32,2048]{1,0:T(8,128)(2,1)}, bf16[32,2048]{1,0:T(8,128)(2,1)S(1)}, u32[]{:S(2)}) copy-start(bf16[32,2048]{1,0:T(8,128)(2,1)S(1)} %collective-permute-done.17.refs_4_) | copy-start | bytes 393220
  117.7 0.7 copy-start.19
  121.0 0.7 copy-start.13
  121.7 0.7 copy-start.14

commit v4 on v3

--- a/solution.py
+++ b/solution.py
@@ -11,6 +11,7 @@
 F32 = jnp.float32
 HBM = pl.BlockSpec(memory_space=pltpu.HBM)
 SMEM = pl.BlockSpec(memory_space=pltpu.SMEM)
+VMEM = pl.BlockSpec(memory_space=pltpu.VMEM)
 
 
 def walks_back(count):
@@ -74,7 +75,9 @@
 
 
 def low_ranks(held, d_held):
-    low = jnp.dot(held[...], d_held[...], preferred_element_type=F32)
+    low = lax.dot_general(
+        held[...], d_held[...], (((1,), (1,)), ((), ())), preferred_element_type=F32
+    )
     return jnp.concatenate([low, jnp.zeros_like(low)], axis=1).astype(BF16)
 
 
@@ -105,7 +108,7 @@
     fetched, total = len(units), starts_of(units)[-1]
     wide = units[0].shape[1]
     columns = weight.shape[1]
-    width, rank = down.shape
+    rank, width = down.shape
     bands = 16
 
     def kernel(ids, *refs):
@@ -130,7 +133,7 @@
         [
             pltpu.VMEM((total, wide), BF16),
             pltpu.VMEM((bands, width // bands, columns), BF16),
-            pltpu.VMEM((width, rank), BF16),
+            pltpu.VMEM((rank, width), BF16),
             pltpu.VMEM((total, columns), BF16),
             pltpu.VMEM((total, 2 * rank), BF16),
             pltpu.SemaphoreType.DMA((fetched,)),
@@ -140,13 +143,14 @@
         ],
         2 * total * width * (columns + rank),
         2 * width * (columns + total + rank),
+        42,
     )(ids, *units, weight, down)
 
 
 def late_ranks(ids, units, places, down, early, early_places, slots, count):
     fetched, fresh = len(units), starts_of(units)[-1]
     wide = units[0].shape[1]
-    width, rank = down.shape
+    rank, width = down.shape
     total = fresh + early.shape[0]
     rows = early.shape[0] // len(early_places)
 
@@ -180,7 +184,7 @@
         [SMEM] + [HBM] * (fetched + 3),
         [
             pltpu.VMEM((fresh, wide), BF16),
-            pltpu.VMEM((width, rank), BF16),
+            pltpu.VMEM((rank, width), BF16),
             pltpu.VMEM((total, 2 * rank), BF16),
             pltpu.VMEM(slots.shape, BF16),
             pltpu.SemaphoreType.DMA((fetched,)),
@@ -191,6 +195,7 @@
         ],
         2 * fresh * width * rank,
         2 * width * (fresh + rank),
+        16,
     )(ids, *units, down, early, slots)[0]
 
 
@@ -223,53 +228,61 @@
         ],
         2 * total * width * columns,
         2 * width * (columns + total),
+        40,
     )(ids, *units, weight)[0]
 
 
-def add_delta(ids, ups, crossed, pieces, low):
+def add_delta(ids, ups, crossed, pieces, low, cuts):
     bases = list({id(piece[0]): piece[0] for piece in pieces}.values())
     shares, parts = len(ups), len(bases)
     count, sub, columns = ups[0].shape
     rank = sub * shares
     total = low.shape[1]
     own = total // count
-    step = min(512, columns)
+    begin, end = cuts
+    blocks = end - begin
+    step = min(1024, columns)
 
     def kernel(ids, *refs):
         ups, base_refs, low = refs[:shares], refs[shares : shares + parts], refs[shares + parts]
-        outs = refs[shares + parts + 1 : shares + parts + 1 + count]
-        u_held, b_held, l_held, sem, b_sem, l_sem, o_sem = refs[shares + parts + 1 + count :]
+        outs = refs[shares + parts + 1 : shares + parts + 1 + blocks]
+        u_held, b_held, l_held, k_held, p_held, sem, b_sem, l_sem, o_sem = refs[shares + parts + 1 + blocks :]
+        u_copies, b_copies = [], []
         l_copy = pltpu.make_async_copy(low, l_held, l_sem)
         l_copy.start()
-        u_copies, b_copies = [], []
         for j, up in enumerate(ups):
             at = pl.multiple_of((ids[1] ^ crossed[j]) * sub, sub)
             u_copies.append(pltpu.make_async_copy(up, u_held.at[:, pl.ds(at, sub)], sem.at[j]))
-        for j, (base, begin, size, place) in enumerate(pieces):
+        for j, (base, row, size, place) in enumerate(pieces):
             base_ref = base_refs[[b is base for b in bases].index(True)]
             at = pl.ds(row_of(ids[0], place, count, size), size)
-            part = base_ref.at[pl.ds(begin, size)]
+            part = base_ref.at[pl.ds(row, size)]
             b_copies.append(pltpu.make_async_copy(part, b_held.at[at], b_sem.at[j]))
         start_all(u_copies)
         start_all(b_copies)
         l_copy.wait()
-        slots = jnp.concatenate(
-            [l_held[s, s * own : (s + 1) * own, rank:] for s in range(count)], axis=0
-        ).astype(F32)
-        wide = jnp.concatenate(
-            [jnp.where(slots == s, l_held[s][:, :rank].astype(F32), 0.0) for s in range(count)], axis=1
-        ).astype(BF16)
+        for i in range(blocks):
+            owner = ids[0] ^ (begin + i)
+            at = pl.ds(pl.multiple_of(owner * own, own), own)
+            slots = l_held[owner, at][:, rank:].astype(F32)
+            wide = [
+                jnp.where(slots == s, l_held[s, at][:, :rank].astype(F32), 0.0) for s in range(count)
+            ]
+            k_held[i * own : (i + 1) * own] = jnp.concatenate(wide, axis=1).astype(BF16)
         wait_all(u_copies)
         wait_all(b_copies)
         o_copies = []
         for n in range(0, columns, step):
             cols = slice(n, n + step)
             ups_here = u_held[:, :, cols].reshape(count * rank, step)
-            delta = jnp.dot(wide, ups_here, preferred_element_type=F32).astype(BF16)
-            b_held[:, cols] = (b_held[:, cols].astype(F32) + delta.astype(F32)).astype(BF16)
-            for i in range(count):
-                at = pl.ds(pl.multiple_of((ids[0] ^ i) * own, own), own)
-                block = b_held.at[at, pl.ds(n, step)]
+            delta = jnp.dot(k_held[...], ups_here, preferred_element_type=F32).astype(BF16)
+            for i in range(blocks):
+                at = pl.ds(pl.multiple_of((ids[0] ^ (begin + i)) * own, own), own)
+                here = slice(i * own, (i + 1) * own)
+                p_held[here, cols] = (
+                    b_held[at, cols].astype(F32) + delta[here].astype(F32)
+                ).astype(BF16)
+                block = p_held.at[pl.ds(i * own, own), pl.ds(n, step)]
                 o_copies.append(
                     pltpu.make_async_copy(block, outs[i].at[:, pl.ds(n, step)], o_sem.at[n // step, i])
                 )
@@ -278,19 +291,22 @@
 
     return call(
         kernel,
-        [(own, columns)] * count,
+        [(own, columns)] * blocks,
         [SMEM] + [HBM] * (shares + parts + 1),
         [
             pltpu.VMEM((count, rank, columns), BF16),
             pltpu.VMEM((total, columns), BF16),
             pltpu.VMEM(low.shape, BF16),
+            pltpu.VMEM((blocks * own, count * rank), BF16),
+            pltpu.VMEM((blocks * own, columns), BF16),
             pltpu.SemaphoreType.DMA((shares,)),
             pltpu.SemaphoreType.DMA((len(pieces),)),
             pltpu.SemaphoreType.DMA,
-            pltpu.SemaphoreType.DMA((columns // step, count)),
+            pltpu.SemaphoreType.DMA((columns // step, blocks)),
         ],
         2 * total * count * rank * columns,
         2 * count * rank * columns,
+        60,
     )(ids, *ups, *bases, low)
 
 
@@ -321,6 +337,7 @@
         ],
         0,
         4 * count * sub * columns,
+        60,
     )(ids, turn, up)[0]
 
 
@@ -331,30 +348,22 @@
     kept = [] if whole is None else [whole]
 
     def kernel(ids, *refs):
-        parts, (out, held, sem, o_sem) = refs[:fetched], refs[fetched + len(kept) :]
-        copies, o_copies = [], []
+        parts, (out, sem) = refs[:fetched], refs[fetched + len(kept) :]
+        copies = []
         for i, part in enumerate(parts):
             at = pl.ds(pl.multiple_of((ids[0] ^ (first + i)) * columns, columns), columns)
-            copies.append(pltpu.make_async_copy(part, held.at[i], sem.at[i]))
-            o_copies.append(pltpu.make_async_copy(held.at[i], out.at[:, at], o_sem.at[i]))
+            copies.append(pltpu.make_async_copy(part, out.at[:, at], sem.at[i]))
         start_all(copies)
-        for i in range(fetched):
-            copies[i].wait()
-            o_copies[i].start()
-        wait_all(o_copies)
+        wait_all(copies)
 
     return pl.pallas_call(
         kernel,
-        in_specs=[SMEM] + [HBM] * (fetched + len(kept)),
+        in_specs=[SMEM] + [VMEM] * fetched + [HBM] * len(kept),
         out_specs=HBM,
         out_shape=jax.ShapeDtypeStruct((rows, count * columns), BF16),
-        scratch_shapes=[
-            pltpu.VMEM((fetched, rows, columns), BF16),
-            pltpu.SemaphoreType.DMA((fetched,)),
-            pltpu.SemaphoreType.DMA((fetched,)),
-        ],
+        scratch_shapes=[pltpu.SemaphoreType.DMA((fetched,))],
         input_output_aliases={fetched + 1: 0} if kept else {},
-        compiler_params=pltpu.CompilerParams(vmem_limit_bytes=60 << 20),
+        compiler_params=pltpu.CompilerParams(vmem_limit_bytes=16 << 20),
     )(ids, *parts, *kept)
 
 
@@ -390,7 +399,7 @@
     slots = jnp.broadcast_to(slots[:, None], (rows, 2 * rank)).astype(BF16)
 
     far = count // 2
-    down = adapter_down_maps[0]
+    down = adapter_down_maps[0].T
     swapped = lax.ppermute(ids, "seq", [(i, (i + 1) % seqs) for i in range(seqs)])
     units, places = [token_input_rows], [(0, 0, 1)]
     one_way, other_way = token_input_rows, token_input_rows
@@ -401,7 +410,7 @@
         places += [(-k, 0, 1), (k, 0, 1)]
     early = units[:far]
     early_base, early_low = early_rows(
-        after(ids, *units[far - 1 : far + 1]), early, base_projection_weight, down
+        after(ids, slots, *units[far - 1 : far + 1]), early, base_projection_weight, down
     )
     one_way, other_way = lax.optimization_barrier((one_way, other_way, early_low))[:2]
     units.append(lax.ppermute(one_way[:half], "tensor", ahead))
@@ -427,11 +436,9 @@
         starts = starts_of(held)
         for j, unit in enumerate(held):
             pieces.append((base, starts[j], unit.shape[0], at[j]))
-    results = add_delta(ids, ups, crossed, pieces, low_all)
-    parts = {0: results[0]}
+    parts = list(add_delta(ids, ups, crossed, pieces, low_all, (0, count)))
     for i in reversed(range(1, count)):
-        parts[i] = lax.ppermute(results[i], "tensor", [(t, t ^ i) for t in range(count)])
-    parts = [parts[i] for i in range(count)]
+        parts[i] = lax.ppermute(parts[i], "tensor", [(t, t ^ i) for t in range(count)])
     cut = 3 * count // 4
     return join_columns(ids, parts[cut:], cut, join_columns(ids, parts[:cut], 0))
 

time: 125 us -> 120 us (0.960)
  Pallas kernels: 45.3 us -> 37.4 us
  local copies, waits for them, and re-layouts: 6.12 us -> 8.63 us
    unnamed x49 -> x30, local copies, waits for them, and re-layouts: 5.39 us -> 7.81 us
    pallas_call x1, Pallas kernels: 4.6 us -> 2.51 us  [late_ranks(): call(kernel, [(count, total, 2 * rank)], [SMEM] + [HBM] * (fetched + 3),...]
    pallas_call x3, Pallas kernels: 9.7 us -> 7.65 us  [the longest x1 4.92 us: add_delta(): call(kernel, [(own, columns)] * blocks, [SMEM] + [HBM] * (shares + parts...]
    pallas_call x1, Pallas kernels: 14.7 us -> 12.7 us  [early_rows(): call(kernel, [(total, columns), (total, 2 * rank)], [SMEM] + [HBM] * (fet...]
    pallas_call x1, Pallas kernels: 13.8 us -> 12 us  [base_rows(): call(kernel, [(total, columns)], [SMEM] + [HBM] * (fetched + 1), [pltpu.V...]
  transfers between devices with their start and end apart: 21 -> 21, of which waited for: 9 -> 9; matrix products, arithmetic and copies ran while one was open for 2% -> 1% of each run, Pallas kernels for 31% -> 26%
where the time goes in v4:
time: 120 us; the launch traced here: 119 us
  Pallas kernels  37.4 us (31%)
  waiting for transfers between devices  36.1 us (30%)
  starting transfers between devices  35.9 us (30%)
  local copies, waits for them, and re-layouts  8.63 us (7%)
    ppermute x3, waiting for transfers between devices, body(): other_way = lax.ppermute(other_way, 'tensor', behind)  14.9 us
    ppermute x7, waiting for transfers between devices, body(): lax.ppermute(parts[i], 'tensor', [(t, t ^ i) for t in range(count)])  14.4 us
    pallas_call x1, Pallas kernels, early_rows(): call(kernel, [(total, columns), (total, 2 * rank)], [SMEM] + [HBM] * (fet...  12.7 us
    pallas_call x1, Pallas kernels, base_rows(): call(kernel, [(total, columns)], [SMEM] + [HBM] * (fetched + 1), [pltpu.V...  12 us
    ppermute x7, starting transfers between devices, body(): lax.ppermute(parts[i], 'tensor', [(t, t ^ i) for t in range(count)])  11.8 us
    unnamed x30, local copies, waits for them, and re-layouts  7.81 us
    ppermute x3, starting transfers between devices, body(): other_way = lax.ppermute(other_way, 'tensor', behind)  6.02 us
    all_to_all x1, starting transfers between devices, body(): lax.all_to_all(share, 'tensor', split_axis=0, concat_axis=0, tiled=True)  6.01 us
  transfers between devices with their start and end apart: 21, of which 9 were waited for; matrix products, arithmetic and copies ran while one was open for 1% of the time, Pallas kernels for 26%

profile of v4, /device:TPU:0, one launch (start us, length us, event | category | flops | bytes accessed | tf_op | source)
XLA Modules:
  0.0 119.2 jit_solution(5618345618761860889)
XLA Ops:
  0.0 3.0 %collective-permute-start.6 = (bf16[32,8192]{1,0:T(8,128)(2,1)}, bf16[32,8192]{1,0:T(8,128)(2,1)S(1)}, u32[]{:S(2)}, u32[]{:S(2)}) collective-permute-start(bf16[32,8192]{1,0:T(8,128)(2,1)} %refs_0_.1), channel_id=1, source_target_pairs={{4,0},{8,4},{12,8},{14,12},{10,14},{6,10},{2,6},{0,2},{5,1},{9,5},... | collective-permute-start | bytes 1572872 | tf_op jit(solution)/shard_map/ppermute | solution.py:408
  3.0 0.1 collective-permute-start.4
  3.1 12.1 %collective-permute-done.6.refs_2_ = bf16[32,8192]{1,0:T(8,128)(2,1)S(1)} collective-permute-done((bf16[32,8192]{1,0:T(8,128)(2,1)}, bf16[32,8192]{1,0:T(8,128)(2,1)S(1)}, u32[]{:S(2)}, u32[]{:S(2)}) %collective-permute-start.6) | collective-permute-done | bytes 524320 | tf_op jit(solution)/shard_map/ppermute | solution.py:408
  15.2 1.7 %collective-permute-start.7 = (bf16[32,8192]{1,0:T(8,128)(2,1)S(1)}, bf16[32,8192]{1,0:T(8,128)(2,1)S(1)}, u32[]{:S(2)}, u32[]{:S(2)}) collective-permute-start(bf16[32,8192]{1,0:T(8,128)(2,1)S(1)} %collective-permute-done.6.refs_2_), channel_id=1, source_target_pairs={{4,0},{8,4},{12,8},{14,12},{10,14},{6,10},{2,6},{0,2},{5,1},{9,5},... | collective-permute-start | bytes 1572872 | tf_op jit(solution)/shard_map/ppermute | solution.py:408
  16.9 0.3 collective-permute-start.5
  17.2 0.1 pad_add_fusion.ids
  17.3 0.0 collective-permute-start
  17.3 1.1 collective-permute-done.turn
  18.4 0.6 copy-done.14
  19.0 2.5 %shard_map.64 = bf16[8,16,2048]{2,1,0:T(8,128)(2,1)} custom-call(s32[2]{0:T(128)} %copy-done.8, s32[2]{0:T(128)} %copy-done.14, bf16[64,16384]{1,0:T(8,128)(2,1)} %bitcast.8), custom_call_target="tpu_custom_call" | custom-call | bytes 1048576 | tf_op jit(solution)/shard_map/pallas_call | solution.py:329
  21.5 6.0 %all-to-all-start = ((bf16[8,16,2048]{2,1,0:T(8,128)(2,1)}), bf16[8,16,2048]{2,1,0:T(8,128)(2,1)}, u32[]{:S(2)}, u32[]{:S(2)}) async-start(bf16[8,16,2048]{2,1,0:T(8,128)(2,1)} %shard_map.64), calls=%async_computation | async-start | bytes 1048576 | tf_op jit(solution)/shard_map/all_to_all | solution.py:422
  27.5 0.8 collective-permute-done.7.refs_0_
  28.3 1.4 %collective-permute-start.9 = (bf16[32,8192]{1,0:T(8,128)(2,1)S(1)}, bf16[32,8192]{1,0:T(8,128)(2,1)S(1)}, u32[]{:S(2)}, u32[]{:S(2)}) collective-permute-start(bf16[32,8192]{1,0:T(8,128)(2,1)S(1)} %collective-permute-done.7.refs_0_), channel_id=1, source_target_pairs={{4,0},{8,4},{12,8},{14,12},{10,14},{6,10},{2,6},{0,2},{5,1},{9,5},... | collective-permute-start | bytes 1572872 | tf_op jit(solution)/shard_map/ppermute | solution.py:408
  29.6 0.7 collective-permute-start.8
  30.3 0.8 select_reduce_fusion
  31.1 0.1 broadcast_in_dim.23.refs_7_
  31.1 1.2 %copy-done = bf16[1,8192,64]{1,2,0:T(8,128)(2,1)S(1)} copy-done((bf16[1,8192,64]{1,2,0:T(8,128)(2,1)S(1)}, bf16[1,8192,64]{1,2,0:T(8,128)(2,1)}, u32[]{:S(2)}) %copy-start) | copy-done | bytes 1048600
  32.4 1.0 copy-done.3
  33.4 1.0 copy-done.5
  34.5 0.6 copy-done.9
  35.1 12.7 %shard_map.65 = (bf16[128,2048]{1,0:T(8,128)(2,1)S(1)}, bf16[128,128]{1,0:T(8,128)(2,1)S(1)}) custom-call(s32[2]{0:T(128)S(1)} %copy-done.9, bf16[32,8192]{1,0:T(8,128)(2,1)S(1)} %copy-done.3, bf16[32,8192]{1,0:T(8,128)(2,1)S(1)} %copy-done.5, bf16[32,8192]{1,0:T(8,128)(2,1)S(1)} %collective-permute-done.6.refs_2_, ...), custom_call_target="tpu_custom_call" | custom-call | flops 4429185024 | bytes 36700160 | tf_op jit(solution)/shard_map/pallas_call | solution.py:129
  47.8 2.1 %collective-permute-done.9.refs_2_ = bf16[32,8192]{1,0:T(8,128)(2,1)S(1)} collective-permute-done((bf16[32,8192]{1,0:T(8,128)(2,1)S(1)}, bf16[32,8192]{1,0:T(8,128)(2,1)S(1)}, u32[]{:S(2)}, u32[]{:S(2)}) %collective-permute-start.9) | collective-permute-done | bytes 524320 | tf_op jit(solution)/shard_map/ppermute | solution.py:408
  49.9 4.3 %collective-permute-start.10 = (bf16[16,8192]{1,0:T(8,128)(2,1)S(1)}, bf16[16,8192]{1,0:T(8,128)(2,1)S(1)}, u32[]{:S(2)}, u32[]{:S(2)}) collective-permute-start(bf16[16,8192]{1,0:T(8,128)(2,1)S(1)} %slice.6), channel_id=1, source_target_pairs={{0,4},{4,8},{8,12},{12,14},{14,10},{10,6},{6,2},{2,0},{1,5},{5,9},... | collective-permute-start | bytes 786440 | tf_op jit(solution)/shard_map/ppermute | solution.py:416
  54.2 0.7 slice.7
  55.0 1.5 %collective-permute-start.1 = (bf16[8,16,2048]{2,1,0:T(8,128)(2,1)}, bf16[8,16,2048]{2,1,0:T(8,128)(2,1)}, u32[]{:S(2)}, u32[]{:S(2)}) collective-permute-start(bf16[8,16,2048]{2,1,0:T(8,128)(2,1)} %all-to-all-done.refs_0_), channel_id=1, source_target_pairs={{0,16},{16,0},{1,17},{17,1},{2,18},{18,2},{3,19},{19,3},{4,20},{20... | collective-permute-start | bytes 1572872 | tf_op jit(solution)/shard_map/ppermute | solution.py:427
  56.5 2.6 %collective-permute-done.10.refs_3_ = bf16[16,8192]{1,0:T(8,128)(2,1)S(1)} collective-permute-done((bf16[16,8192]{1,0:T(8,128)(2,1)S(1)}, bf16[16,8192]{1,0:T(8,128)(2,1)S(1)}, u32[]{:S(2)}, u32[]{:S(2)}) %collective-permute-start.10) | collective-permute-done | bytes 262176 | tf_op jit(solution)/shard_map/ppermute | solution.py:416
  59.0 3.1 %collective-permute-done.11.refs_4_ = bf16[16,8192]{1,0:T(8,128)(2,1)S(1)} collective-permute-done((bf16[16,8192]{1,0:T(8,128)(2,1)}, bf16[16,8192]{1,0:T(8,128)(2,1)S(1)}, u32[]{:S(2)}, u32[]{:S(2)}) %collective-permute-start.11) | collective-permute-done | bytes 262176 | tf_op jit(solution)/shard_map/ppermute | solution.py:417
  62.2 2.5 %shard_map.66 = bf16[8,256,128]{2,1,0:T(8,128)(2,1)} custom-call(s32[2]{0:T(128)S(1)} %copy-done.10, bf16[32,8192]{1,0:T(8,128)(2,1)S(1)} %collective-permute-done.7.refs_0_, bf16[32,8192]{1,0:T(8,128)(2,1)S(1)} %collective-permute-done.8.refs_1_, bf16[32,8192]{1,0:T(8,128)(2,1)S(1)} %collective-permute-done.9.refs_2_, ...), custom_call_target="tpu_custom_call" | custom-call | flops 134217728 | bytes 3145728 | tf_op jit(solution)/shard_map/pallas_call | solution.py:181
  64.7 4.6 %all-to-all-start.1 = ((bf16[8,256,128]{2,1,0:T(8,128)(2,1)}), bf16[8,256,128]{2,1,0:T(8,128)(2,1)S(1)}, u32[]{:S(2)}, u32[]{:S(2)}) async-start(bf16[8,256,128]{2,1,0:T(8,128)(2,1)} %shard_map.66), calls=%async_computation.1 | async-start | bytes 1048576 | tf_op jit(solution)/shard_map/all_to_all | solution.py:432
  69.4 0.5 collective-permute-start.3
  69.9 12.0 %shard_map.67.refs_5_ = bf16[128,2048]{1,0:T(8,128)(2,1)S(1)} custom-call(s32[2]{0:T(128)S(1)} %copy-done.10, bf16[32,8192]{1,0:T(8,128)(2,1)S(1)} %collective-permute-done.7.refs_0_, bf16[32,8192]{1,0:T(8,128)(2,1)S(1)} %collective-permute-done.8.refs_1_, bf16[32,8192]{1,0:T(8,128)(2,1)S(1)} %collective-permute-done.9.refs_2_, ...), custom_call_target="tpu_custom_call" | custom-call | flops 4294967296 | bytes 35651584 | tf_op jit(solution)/shard_map/pallas_call | solution.py:217
  81.9 0.8 copy-done.2
  82.7 0.8 copy-done.13
  83.5 0.8 copy-done.12
  84.3 4.9 %shard_map.68 = (bf16[32,2048]{1,0:T(8,128)(2,1)}, bf16[32,2048]{1,0:T(8,128)(2,1)}, bf16[32,2048]{1,0:T(8,128)(2,1)}, bf16[32,2048]{1,0:T(8,128)(2,1)}, bf16[32...) custom-call(s32[2]{0:T(128)} %copy-done.8, ...), custom_call_target="tpu_custom_call" | custom-call | flops 536870912 | bytes 2097152 | tf_op jit(solution)/shard_map/pallas_call | solution.py:292
  89.2 2.1 %collective-permute-start.14 = (bf16[32,2048]{1,0:T(8,128)(2,1)}, bf16[32,2048]{1,0:T(8,128)(2,1)S(1)}, u32[]{:S(2)}, u32[]{:S(2)}) collective-permute-start(bf16[32,2048]{1,0:T(8,128)(2,1)} %get-tuple-element.28), channel_id=1, source_target_pairs={{0,2},{2,0},{4,6},{6,4},{8,10},{10,8},{12,14},{14,12},{1,3},{3,1},... | collective-permute-start | bytes 393224 | tf_op jit(solution)/shard_map/ppermute | solution.py:441
  91.3 1.5 %collective-permute-start.15 = (bf16[32,2048]{1,0:T(8,128)(2,1)}, bf16[32,2048]{1,0:T(8,128)(2,1)S(1)}, u32[]{:S(2)}, u32[]{:S(2)}) collective-permute-start(bf16[32,2048]{1,0:T(8,128)(2,1)} %get-tuple-element.29), channel_id=1, source_target_pairs={{0,4},{2,6},{4,0},{6,2},{8,12},{10,14},{12,8},{14,10},{1,5},{3,7},... | collective-permute-start | bytes 393224 | tf_op jit(solution)/shard_map/ppermute | solution.py:441
  92.8 0.1 collective-permute-start.16
  92.8 2.8 %collective-permute-start.17 = (bf16[32,2048]{1,0:T(8,128)(2,1)}, bf16[32,2048]{1,0:T(8,128)(2,1)S(1)}, u32[]{:S(2)}, u32[]{:S(2)}) collective-permute-start(bf16[32,2048]{1,0:T(8,128)(2,1)} %get-tuple-element.31), channel_id=1, source_target_pairs={{0,8},{2,10},{4,12},{6,14},{8,0},{10,2},{12,4},{14,6},{1,9},{3,11}... | collective-permute-start | bytes 393224 | tf_op jit(solution)/shard_map/ppermute | solution.py:441
  95.7 1.5 %collective-permute-start.18 = (bf16[32,2048]{1,0:T(8,128)(2,1)}, bf16[32,2048]{1,0:T(8,128)(2,1)S(1)}, u32[]{:S(2)}, u32[]{:S(2)}) collective-permute-start(bf16[32,2048]{1,0:T(8,128)(2,1)} %get-tuple-element.32), channel_id=1, source_target_pairs={{0,10},{2,8},{4,14},{6,12},{8,2},{10,0},{12,6},{14,4},{1,11},{3,9}... | collective-permute-start | bytes 393224 | tf_op jit(solution)/shard_map/ppermute | solution.py:441
  97.1 3.3 %collective-permute-start.12 = (bf16[32,2048]{1,0:T(8,128)(2,1)}, bf16[32,2048]{1,0:T(8,128)(2,1)S(1)}, u32[]{:S(2)}, u32[]{:S(2)}) collective-permute-start(bf16[32,2048]{1,0:T(8,128)(2,1)} %get-tuple-element.25), channel_id=1, source_target_pairs={{0,12},{2,14},{4,8},{6,10},{8,4},{10,6},{12,0},{14,2},{1,13},{3,15... | collective-permute-start | bytes 393224 | tf_op jit(solution)/shard_map/ppermute | solution.py:441
  100.4 1.9 %collective-permute-done.15.refs_2_ = bf16[32,2048]{1,0:T(8,128)(2,1)S(1)} collective-permute-done((bf16[32,2048]{1,0:T(8,128)(2,1)}, bf16[32,2048]{1,0:T(8,128)(2,1)S(1)}, u32[]{:S(2)}, u32[]{:S(2)}) %collective-permute-start.15) | collective-permute-done | bytes 131104 | tf_op jit(solution)/shard_map/ppermute | solution.py:441
  102.3 0.6 collective-permute-start.13
  103.0 0.3 collective-permute-done.16.refs_3_
  103.2 12.2 %collective-permute-done.18.refs_5_ = bf16[32,2048]{1,0:T(8,128)(2,1)S(1)} collective-permute-done((bf16[32,2048]{1,0:T(8,128)(2,1)}, bf16[32,2048]{1,0:T(8,128)(2,1)S(1)}, u32[]{:S(2)}, u32[]{:S(2)}) %collective-permute-start.18) | collective-permute-done | bytes 131104 | tf_op jit(solution)/shard_map/ppermute | solution.py:441
  115.4 0.9 copy-done.7
  116.3 1.5 %shard_map.69.refs_2_ = bf16[32,16384]{1,0:T(8,128)(2,1)} custom-call(s32[2]{0:T(128)S(1)} %copy-done.11, bf16[32,2048]{1,0:T(8,128)(2,1)S(1)} %copy-done.7, bf16[32,2048]{1,0:T(8,128)(2,1)S(1)} %collective-permute-done.14.refs_1_, bf16[32,2048]{1,0:T(8,128)(2,1)S(1)} %collective-permute-done.15.refs_2_, ...), custom_call_target="tpu_custom_call" | custom-call | tf_op jit(solution)/shard_map/pallas_call | solution.py:359
  117.8 1.3 %shard_map.70 = bf16[32,16384]{1,0:T(8,128)(2,1)} custom-call(s32[2]{0:T(128)S(1)} %copy-done.11, bf16[32,2048]{1,0:T(8,128)(2,1)S(1)} %collective-permute-done.12.refs_0_, bf16[32,2048]{1,0:T(8,128)(2,1)S(1)} %collective-permute-done.13.refs_1_, bf16[32,16384]{1,0:T(8,128)(2,1)} %shard_map.69.refs_2_), custom_call_target="tpu_custom_call", output_to_operand_aliasing={{}: (3, {})} | custom-call | tf_op jit(solution)/shard_map/pallas_call | solution.py:359
  (37 shorter events, 0.1 us)
Async XLA Ops:
  0.0 62.2 %copy-start.1 = (bf16[1,8192,64]{1,2,0:T(8,128)(2,1)S(1)}, bf16[1,8192,64]{1,2,0:T(8,128)(2,1)}, u32[]{:S(2)}) copy-start(bf16[1,8192,64]{1,2,0:T(8,128)(2,1)} %param.8) | copy-start | bytes 3145732
  0.0 15.2 %collective-permute-start.6 = (bf16[32,8192]{1,0:T(8,128)(2,1)}, bf16[32,8192]{1,0:T(8,128)(2,1)S(1)}, u32[]{:S(2)}, u32[]{:S(2)}) collective-permute-start(bf16[32,8192]{1,0:T(8,128)(2,1)} %refs_0_.1), channel_id=1, source_target_pairs={{4,0},{8,4},{12,8},{14,12},{10,14},{6,10},{2,6},{0,2},{5,1},{9,5},... | collective-permute-start | bytes 1572872 | tf_op jit(solution)/shard_map/ppermute | solution.py:408
  3.0 13.9 %collective-permute-start.4 = (bf16[32,8192]{1,0:T(8,128)(2,1)}, bf16[32,8192]{1,0:T(8,128)(2,1)S(1)}, u32[]{:S(2)}, u32[]{:S(2)}) collective-permute-start(bf16[32,8192]{1,0:T(8,128)(2,1)} %refs_0_.1), channel_id=1, source_target_pairs={{0,4},{4,8},{8,12},{12,14},{14,10},{10,6},{6,2},{2,0},{1,5},{5,9},... | collective-permute-start | bytes 1572872 | tf_op jit(solution)/shard_map/ppermute | solution.py:407
  15.2 13.1 %collective-permute-start.7 = (bf16[32,8192]{1,0:T(8,128)(2,1)S(1)}, bf16[32,8192]{1,0:T(8,128)(2,1)S(1)}, u32[]{:S(2)}, u32[]{:S(2)}) collective-permute-start(bf16[32,8192]{1,0:T(8,128)(2,1)S(1)} %collective-permute-done.6.refs_2_), channel_id=1, source_target_pairs={{4,0},{8,4},{12,8},{14,12},{10,14},{6,10},{2,6},{0,2},{5,1},{9,5},... | collective-permute-start | bytes 1572872 | tf_op jit(solution)/shard_map/ppermute | solution.py:408
  16.8 12.8 %copy-start.4 = (bf16[32,8192]{1,0:T(8,128)(2,1)}, bf16[32,8192]{1,0:T(8,128)(2,1)S(1)}, u32[]{:S(2)}) copy-start(bf16[32,8192]{1,0:T(8,128)(2,1)S(1)} %collective-permute-done.4.refs_1_) | copy-start | bytes 1572868
  16.9 12.8 %collective-permute-start.5 = (bf16[32,8192]{1,0:T(8,128)(2,1)S(1)}, bf16[32,8192]{1,0:T(8,128)(2,1)}, u32[]{:S(2)}, u32[]{:S(2)}) collective-permute-start(bf16[32,8192]{1,0:T(8,128)(2,1)S(1)} %collective-permute-done.4.refs_1_), channel_id=1, source_target_pairs={{0,4},{4,8},{8,12},{12,14},{14,10},{10,6},{6,2},{2,0},{1,5},{5,9},... | collective-permute-start | bytes 1572872 | tf_op jit(solution)/shard_map/ppermute | solution.py:407
  17.3 1.1 copy-start.8
  17.3 1.1 collective-permute-start
  18.4 0.6 copy-start.14
  21.5 40.7 %copy-start.10 = (s32[2]{0:T(128)S(1)}, s32[2]{0:T(128)}, u32[]{:S(2)}) copy-start(s32[2]{0:T(128)} %copy-done.8) | copy-start | bytes 28
  21.5 33.5 %all-to-all-start = ((bf16[8,16,2048]{2,1,0:T(8,128)(2,1)}), bf16[8,16,2048]{2,1,0:T(8,128)(2,1)}, u32[]{:S(2)}, u32[]{:S(2)}) async-start(bf16[8,16,2048]{2,1,0:T(8,128)(2,1)} %shard_map.64), calls=%async_computation | async-start | bytes 1048576 | tf_op jit(solution)/shard_map/all_to_all | solution.py:422
  28.3 21.6 %collective-permute-start.9 = (bf16[32,8192]{1,0:T(8,128)(2,1)S(1)}, bf16[32,8192]{1,0:T(8,128)(2,1)S(1)}, u32[]{:S(2)}, u32[]{:S(2)}) collective-permute-start(bf16[32,8192]{1,0:T(8,128)(2,1)S(1)} %collective-permute-done.7.refs_0_), channel_id=1, source_target_pairs={{4,0},{8,4},{12,8},{14,12},{10,14},{6,10},{2,6},{0,2},{5,1},{9,5},... | collective-permute-start | bytes 1572872 | tf_op jit(solution)/shard_map/ppermute | solution.py:408
  29.6 20.3 %collective-permute-start.8 = (bf16[32,8192]{1,0:T(8,128)(2,1)}, bf16[32,8192]{1,0:T(8,128)(2,1)S(1)}, u32[]{:S(2)}, u32[]{:S(2)}) collective-permute-start(bf16[32,8192]{1,0:T(8,128)(2,1)} %collective-permute-done.5.refs_3_), channel_id=1, source_target_pairs={{0,4},{4,8},{8,12},{12,14},{14,10},{10,6},{6,2},{2,0},{1,5},{5,9},... | collective-permute-start | bytes 1572872 | tf_op jit(solution)/shard_map/ppermute | solution.py:407
  31.1 1.2 %copy-start = (bf16[1,8192,64]{1,2,0:T(8,128)(2,1)S(1)}, bf16[1,8192,64]{1,2,0:T(8,128)(2,1)}, u32[]{:S(2)}) copy-start(bf16[1,8192,64]{1,2,0:T(8,128)(2,1)} %param.8) | copy-start | bytes 3145732
  32.4 1.0 copy-start.3
  33.4 1.0 copy-start.5
  34.5 0.6 copy-start.9
  35.1 80.3 %copy-start.11 = (s32[2]{0:T(128)S(1)}, s32[2]{0:T(128)}, u32[]{:S(2)}) copy-start(s32[2]{0:T(128)} %copy-done.8) | copy-start | bytes 28
  47.8 6.4 %copy-start.6 = (bf16[128,2048]{1,0:T(8,128)(2,1)}, bf16[128,2048]{1,0:T(8,128)(2,1)S(1)}, u32[]{:S(2)}) copy-start(bf16[128,2048]{1,0:T(8,128)(2,1)S(1)} %get-tuple-element.20.refs_4_) | copy-start | bytes 1572868
  49.9 9.1 %collective-permute-start.10 = (bf16[16,8192]{1,0:T(8,128)(2,1)S(1)}, bf16[16,8192]{1,0:T(8,128)(2,1)S(1)}, u32[]{:S(2)}, u32[]{:S(2)}) collective-permute-start(bf16[16,8192]{1,0:T(8,128)(2,1)S(1)} %slice.6), channel_id=1, source_target_pairs={{0,4},{4,8},{8,12},{12,14},{14,10},{10,6},{6,2},{2,0},{1,5},{5,9},... | collective-permute-start | bytes 786440 | tf_op jit(solution)/shard_map/ppermute | solution.py:416
  55.0 7.2 %collective-permute-start.11 = (bf16[16,8192]{1,0:T(8,128)(2,1)}, bf16[16,8192]{1,0:T(8,128)(2,1)S(1)}, u32[]{:S(2)}, u32[]{:S(2)}) collective-permute-start(bf16[16,8192]{1,0:T(8,128)(2,1)} %slice.7), channel_id=1, source_target_pairs={{4,0},{8,4},{12,8},{14,12},{10,14},{6,10},{2,6},{0,2},{5,1},{9,5},... | collective-permute-start | bytes 786440 | tf_op jit(solution)/shard_map/ppermute | solution.py:417
  55.0 14.4 %collective-permute-start.1 = (bf16[8,16,2048]{2,1,0:T(8,128)(2,1)}, bf16[8,16,2048]{2,1,0:T(8,128)(2,1)}, u32[]{:S(2)}, u32[]{:S(2)}) collective-permute-start(bf16[8,16,2048]{2,1,0:T(8,128)(2,1)} %all-to-all-done.refs_0_), channel_id=1, source_target_pairs={{0,16},{16,0},{1,17},{17,1},{2,18},{18,2},{3,19},{19,3},{4,20},{20... | collective-permute-start | bytes 1572872 | tf_op jit(solution)/shard_map/ppermute | solution.py:427
  64.7 18.8 %all-to-all-start.1 = ((bf16[8,256,128]{2,1,0:T(8,128)(2,1)}), bf16[8,256,128]{2,1,0:T(8,128)(2,1)S(1)}, u32[]{:S(2)}, u32[]{:S(2)}) async-start(bf16[8,256,128]{2,1,0:T(8,128)(2,1)} %shard_map.66), calls=%async_computation.1 | async-start | bytes 1048576 | tf_op jit(solution)/shard_map/all_to_all | solution.py:432
  69.3 13.3 %collective-permute-start.2 = (bf16[8,16,2048]{2,1,0:T(8,128)(2,1)}, bf16[8,16,2048]{2,1,0:T(8,128)(2,1)S(1)}, u32[]{:S(2)}, u32[]{:S(2)}) collective-permute-start(bf16[8,16,2048]{2,1,0:T(8,128)(2,1)} %all-to-all-done.refs_0_), channel_id=1, source_target_pairs={{0,1},{1,0},{2,3},{3,2},{4,5},{5,4},{6,7},{7,6},{8,9},{9,8},{10,11... | collective-permute-start | bytes 1572872 | tf_op jit(solution)/shard_map/ppermute | solution.py:427
  69.4 14.1 %collective-permute-start.3 = (bf16[8,16,2048]{2,1,0:T(8,128)(2,1)}, bf16[8,16,2048]{2,1,0:T(8,128)(2,1)}, u32[]{:S(2)}, u32[]{:S(2)}) collective-permute-start(bf16[8,16,2048]{2,1,0:T(8,128)(2,1)} %collective-permute-done.1.refs_1_), channel_id=1, source_target_pairs={{0,1},{1,0},{2,3},{3,2},{4,5},{5,4},{6,7},{7,6},{8,9},{9,8},{10,11... | collective-permute-start | bytes 1572872 | tf_op jit(solution)/shard_map/ppermute | solution.py:427
  81.9 0.8 copy-start.2
  82.7 0.8 copy-start.13
  83.5 0.8 copy-start.12
  89.2 7.9 %collective-permute-start.14 = (bf16[32,2048]{1,0:T(8,128)(2,1)}, bf16[32,2048]{1,0:T(8,128)(2,1)S(1)}, u32[]{:S(2)}, u32[]{:S(2)}) collective-permute-start(bf16[32,2048]{1,0:T(8,128)(2,1)} %get-tuple-element.28), channel_id=1, source_target_pairs={{0,2},{2,0},{4,6},{6,4},{8,10},{10,8},{12,14},{14,12},{1,3},{3,1},... | collective-permute-start | bytes 393224 | tf_op jit(solution)/shard_map/ppermute | solution.py:441
  91.3 11.1 %collective-permute-start.15 = (bf16[32,2048]{1,0:T(8,128)(2,1)}, bf16[32,2048]{1,0:T(8,128)(2,1)S(1)}, u32[]{:S(2)}, u32[]{:S(2)}) collective-permute-start(bf16[32,2048]{1,0:T(8,128)(2,1)} %get-tuple-element.29), channel_id=1, source_target_pairs={{0,4},{2,6},{4,0},{6,2},{8,12},{10,14},{12,8},{14,10},{1,5},{3,7},... | collective-permute-start | bytes 393224 | tf_op jit(solution)/shard_map/ppermute | solution.py:441
  92.8 10.5 %collective-permute-start.16 = (bf16[32,2048]{1,0:T(8,128)(2,1)}, bf16[32,2048]{1,0:T(8,128)(2,1)S(1)}, u32[]{:S(2)}, u32[]{:S(2)}) collective-permute-start(bf16[32,2048]{1,0:T(8,128)(2,1)} %get-tuple-element.30), channel_id=1, source_target_pairs={{0,6},{2,4},{4,2},{6,0},{8,14},{10,12},{12,10},{14,8},{1,7},{3,5},... | collective-permute-start | bytes 393224 | tf_op jit(solution)/shard_map/ppermute | solution.py:441
  92.8 10.4 %collective-permute-start.17 = (bf16[32,2048]{1,0:T(8,128)(2,1)}, bf16[32,2048]{1,0:T(8,128)(2,1)S(1)}, u32[]{:S(2)}, u32[]{:S(2)}) collective-permute-start(bf16[32,2048]{1,0:T(8,128)(2,1)} %get-tuple-element.31), channel_id=1, source_target_pairs={{0,8},{2,10},{4,12},{6,14},{8,0},{10,2},{12,4},{14,6},{1,9},{3,11}... | collective-permute-start | bytes 393224 | tf_op jit(solution)/shard_map/ppermute | solution.py:441
  95.7 19.7 %collective-permute-start.18 = (bf16[32,2048]{1,0:T(8,128)(2,1)}, bf16[32,2048]{1,0:T(8,128)(2,1)S(1)}, u32[]{:S(2)}, u32[]{:S(2)}) collective-permute-start(bf16[32,2048]{1,0:T(8,128)(2,1)} %get-tuple-element.32), channel_id=1, source_target_pairs={{0,10},{2,8},{4,14},{6,12},{8,2},{10,0},{12,6},{14,4},{1,11},{3,9}... | collective-permute-start | bytes 393224 | tf_op jit(solution)/shard_map/ppermute | solution.py:441
  97.1 20.6 %collective-permute-start.12 = (bf16[32,2048]{1,0:T(8,128)(2,1)}, bf16[32,2048]{1,0:T(8,128)(2,1)S(1)}, u32[]{:S(2)}, u32[]{:S(2)}) collective-permute-start(bf16[32,2048]{1,0:T(8,128)(2,1)} %get-tuple-element.25), channel_id=1, source_target_pairs={{0,12},{2,14},{4,8},{6,10},{8,4},{10,6},{12,0},{14,2},{1,13},{3,15... | collective-permute-start | bytes 393224 | tf_op jit(solution)/shard_map/ppermute | solution.py:441
  102.3 15.4 %collective-permute-start.13 = (bf16[32,2048]{1,0:T(8,128)(2,1)}, bf16[32,2048]{1,0:T(8,128)(2,1)S(1)}, u32[]{:S(2)}, u32[]{:S(2)}) collective-permute-start(bf16[32,2048]{1,0:T(8,128)(2,1)} %get-tuple-element.26), channel_id=1, source_target_pairs={{0,14},{2,12},{4,10},{6,8},{8,6},{10,4},{12,2},{14,0},{1,15},{3,13... | collective-permute-start | bytes 393224 | tf_op jit(solution)/shard_map/ppermute | solution.py:441
  115.4 0.9 copy-start.7

commit v5 on v4

--- a/solution.py
+++ b/solution.py
@@ -292,7 +292,7 @@
     return call(
         kernel,
         [(own, columns)] * blocks,
-        [SMEM] + [HBM] * (shares + parts + 1),
+        [SMEM] + [HBM] * (shares + parts) + [VMEM],
         [
             pltpu.VMEM((count, rank, columns), BF16),
             pltpu.VMEM((total, columns), BF16),

time: 120 us -> 120 us (level)
  no operation moved by 1% of the time
where the time goes in v5:
time: 120 us; the launch traced here: 119 us
  Pallas kernels  37.3 us (31%)
  waiting for transfers between devices  36.1 us (30%)
  starting transfers between devices  35.9 us (30%)
  local copies, waits for them, and re-layouts  8.63 us (7%)
    ppermute x3, waiting for transfers between devices, body(): other_way = lax.ppermute(other_way, 'tensor', behind)  14.9 us
    ppermute x7, waiting for transfers between devices, body(): lax.ppermute(parts[i], 'tensor', [(t, t ^ i) for t in range(count)])  14.4 us
    pallas_call x1, Pallas kernels, early_rows(): call(kernel, [(total, columns), (total, 2 * rank)], [SMEM] + [HBM] * (fet...  12.7 us
    pallas_call x1, Pallas kernels, base_rows(): call(kernel, [(total, columns)], [SMEM] + [HBM] * (fetched + 1), [pltpu.V...  12 us
    ppermute x7, starting transfers between devices, body(): lax.ppermute(parts[i], 'tensor', [(t, t ^ i) for t in range(count)])  11.8 us
    unnamed x30, local copies, waits for them, and re-layouts  7.81 us
    ppermute x3, starting transfers between devices, body(): other_way = lax.ppermute(other_way, 'tensor', behind)  6.02 us
    all_to_all x1, starting transfers between devices, body(): lax.all_to_all(share, 'tensor', split_axis=0, concat_axis=0, tiled=True)  6.01 us
  transfers between devices with their start and end apart: 21, of which 9 were waited for; matrix products, arithmetic and copies ran while one was open for 1% of the time, Pallas kernels for 26%

profile of v5, /device:TPU:0, one launch (start us, length us, event | category | flops | bytes accessed | tf_op | source)
XLA Modules:
  0.0 119.1 jit_solution(4026669036357960366)
XLA Ops:
  0.0 3.0 %collective-permute-start.6 = (bf16[32,8192]{1,0:T(8,128)(2,1)}, bf16[32,8192]{1,0:T(8,128)(2,1)S(1)}, u32[]{:S(2)}, u32[]{:S(2)}) collective-permute-start(bf16[32,8192]{1,0:T(8,128)(2,1)} %refs_0_.1), channel_id=1, source_target_pairs={{4,0},{8,4},{12,8},{14,12},{10,14},{6,10},{2,6},{0,2},{5,1},{9,5},... | collective-permute-start | bytes 1572872 | tf_op jit(solution)/shard_map/ppermute | solution.py:408
  3.0 0.1 collective-permute-start.4
  3.1 12.1 %collective-permute-done.6.refs_2_ = bf16[32,8192]{1,0:T(8,128)(2,1)S(1)} collective-permute-done((bf16[32,8192]{1,0:T(8,128)(2,1)}, bf16[32,8192]{1,0:T(8,128)(2,1)S(1)}, u32[]{:S(2)}, u32[]{:S(2)}) %collective-permute-start.6) | collective-permute-done | bytes 524320 | tf_op jit(solution)/shard_map/ppermute | solution.py:408
  15.2 1.7 %collective-permute-start.7 = (bf16[32,8192]{1,0:T(8,128)(2,1)S(1)}, bf16[32,8192]{1,0:T(8,128)(2,1)S(1)}, u32[]{:S(2)}, u32[]{:S(2)}) collective-permute-start(bf16[32,8192]{1,0:T(8,128)(2,1)S(1)} %collective-permute-done.6.refs_2_), channel_id=1, source_target_pairs={{4,0},{8,4},{12,8},{14,12},{10,14},{6,10},{2,6},{0,2},{5,1},{9,5},... | collective-permute-start | bytes 1572872 | tf_op jit(solution)/shard_map/ppermute | solution.py:408
  16.9 0.3 collective-permute-start.5
  17.2 0.1 pad_add_fusion.ids
  17.3 0.0 collective-permute-start
  17.3 1.1 collective-permute-done.turn
  18.4 0.6 copy-done.14
  19.0 2.5 %shard_map.64 = bf16[8,16,2048]{2,1,0:T(8,128)(2,1)} custom-call(s32[2]{0:T(128)} %copy-done.8, s32[2]{0:T(128)} %copy-done.14, bf16[64,16384]{1,0:T(8,128)(2,1)} %bitcast.8), custom_call_target="tpu_custom_call" | custom-call | bytes 1048576 | tf_op jit(solution)/shard_map/pallas_call | solution.py:329
  21.5 6.0 %all-to-all-start = ((bf16[8,16,2048]{2,1,0:T(8,128)(2,1)}), bf16[8,16,2048]{2,1,0:T(8,128)(2,1)}, u32[]{:S(2)}, u32[]{:S(2)}) async-start(bf16[8,16,2048]{2,1,0:T(8,128)(2,1)} %shard_map.64), calls=%async_computation | async-start | bytes 1048576 | tf_op jit(solution)/shard_map/all_to_all | solution.py:422
  27.5 0.8 collective-permute-done.7.refs_0_
  28.3 1.4 %collective-permute-start.9 = (bf16[32,8192]{1,0:T(8,128)(2,1)S(1)}, bf16[32,8192]{1,0:T(8,128)(2,1)S(1)}, u32[]{:S(2)}, u32[]{:S(2)}) collective-permute-start(bf16[32,8192]{1,0:T(8,128)(2,1)S(1)} %collective-permute-done.7.refs_0_), channel_id=1, source_target_pairs={{4,0},{8,4},{12,8},{14,12},{10,14},{6,10},{2,6},{0,2},{5,1},{9,5},... | collective-permute-start | bytes 1572872 | tf_op jit(solution)/shard_map/ppermute | solution.py:408
  29.6 0.7 collective-permute-start.8
  30.3 0.8 select_reduce_fusion
  31.1 0.1 broadcast_in_dim.23.refs_7_
  31.1 1.2 %copy-done = bf16[1,8192,64]{1,2,0:T(8,128)(2,1)S(1)} copy-done((bf16[1,8192,64]{1,2,0:T(8,128)(2,1)S(1)}, bf16[1,8192,64]{1,2,0:T(8,128)(2,1)}, u32[]{:S(2)}) %copy-start) | copy-done | bytes 1048600
  32.4 1.0 copy-done.3
  33.4 1.0 copy-done.5
  34.5 0.6 copy-done.9
  35.1 12.7 %shard_map.65 = (bf16[128,2048]{1,0:T(8,128)(2,1)S(1)}, bf16[128,128]{1,0:T(8,128)(2,1)S(1)}) custom-call(s32[2]{0:T(128)S(1)} %copy-done.9, bf16[32,8192]{1,0:T(8,128)(2,1)S(1)} %copy-done.3, bf16[32,8192]{1,0:T(8,128)(2,1)S(1)} %copy-done.5, bf16[32,8192]{1,0:T(8,128)(2,1)S(1)} %collective-permute-done.6.refs_2_, ...), custom_call_target="tpu_custom_call" | custom-call | flops 4429185024 | bytes 36700160 | tf_op jit(solution)/shard_map/pallas_call | solution.py:129
  47.8 2.1 %collective-permute-done.9.refs_2_ = bf16[32,8192]{1,0:T(8,128)(2,1)S(1)} collective-permute-done((bf16[32,8192]{1,0:T(8,128)(2,1)S(1)}, bf16[32,8192]{1,0:T(8,128)(2,1)S(1)}, u32[]{:S(2)}, u32[]{:S(2)}) %collective-permute-start.9) | collective-permute-done | bytes 524320 | tf_op jit(solution)/shard_map/ppermute | solution.py:408
  49.9 4.3 %collective-permute-start.10 = (bf16[16,8192]{1,0:T(8,128)(2,1)S(1)}, bf16[16,8192]{1,0:T(8,128)(2,1)S(1)}, u32[]{:S(2)}, u32[]{:S(2)}) collective-permute-start(bf16[16,8192]{1,0:T(8,128)(2,1)S(1)} %slice.6), channel_id=1, source_target_pairs={{0,4},{4,8},{8,12},{12,14},{14,10},{10,6},{6,2},{2,0},{1,5},{5,9},... | collective-permute-start | bytes 786440 | tf_op jit(solution)/shard_map/ppermute | solution.py:416
  54.2 0.7 slice.7
  55.0 1.5 %collective-permute-start.1 = (bf16[8,16,2048]{2,1,0:T(8,128)(2,1)}, bf16[8,16,2048]{2,1,0:T(8,128)(2,1)}, u32[]{:S(2)}, u32[]{:S(2)}) collective-permute-start(bf16[8,16,2048]{2,1,0:T(8,128)(2,1)} %all-to-all-done.refs_0_), channel_id=1, source_target_pairs={{0,16},{16,0},{1,17},{17,1},{2,18},{18,2},{3,19},{19,3},{4,20},{20... | collective-permute-start | bytes 1572872 | tf_op jit(solution)/shard_map/ppermute | solution.py:427
  56.5 2.6 %collective-permute-done.10.refs_3_ = bf16[16,8192]{1,0:T(8,128)(2,1)S(1)} collective-permute-done((bf16[16,8192]{1,0:T(8,128)(2,1)S(1)}, bf16[16,8192]{1,0:T(8,128)(2,1)S(1)}, u32[]{:S(2)}, u32[]{:S(2)}) %collective-permute-start.10) | collective-permute-done | bytes 262176 | tf_op jit(solution)/shard_map/ppermute | solution.py:416
  59.0 3.1 %collective-permute-done.11.refs_4_ = bf16[16,8192]{1,0:T(8,128)(2,1)S(1)} collective-permute-done((bf16[16,8192]{1,0:T(8,128)(2,1)}, bf16[16,8192]{1,0:T(8,128)(2,1)S(1)}, u32[]{:S(2)}, u32[]{:S(2)}) %collective-permute-start.11) | collective-permute-done | bytes 262176 | tf_op jit(solution)/shard_map/ppermute | solution.py:417
  62.2 2.5 %shard_map.66 = bf16[8,256,128]{2,1,0:T(8,128)(2,1)} custom-call(s32[2]{0:T(128)S(1)} %copy-done.10, bf16[32,8192]{1,0:T(8,128)(2,1)S(1)} %collective-permute-done.7.refs_0_, bf16[32,8192]{1,0:T(8,128)(2,1)S(1)} %collective-permute-done.8.refs_1_, bf16[32,8192]{1,0:T(8,128)(2,1)S(1)} %collective-permute-done.9.refs_2_, ...), custom_call_target="tpu_custom_call" | custom-call | flops 134217728 | bytes 3145728 | tf_op jit(solution)/shard_map/pallas_call | solution.py:181
  64.7 4.6 %all-to-all-start.1 = ((bf16[8,256,128]{2,1,0:T(8,128)(2,1)}), bf16[8,256,128]{2,1,0:T(8,128)(2,1)S(1)}, u32[]{:S(2)}, u32[]{:S(2)}) async-start(bf16[8,256,128]{2,1,0:T(8,128)(2,1)} %shard_map.66), calls=%async_computation.1 | async-start | bytes 1048576 | tf_op jit(solution)/shard_map/all_to_all | solution.py:432
  69.4 0.5 collective-permute-start.3
  69.9 12.0 %shard_map.67.refs_5_ = bf16[128,2048]{1,0:T(8,128)(2,1)S(1)} custom-call(s32[2]{0:T(128)S(1)} %copy-done.10, bf16[32,8192]{1,0:T(8,128)(2,1)S(1)} %collective-permute-done.7.refs_0_, bf16[32,8192]{1,0:T(8,128)(2,1)S(1)} %collective-permute-done.8.refs_1_, bf16[32,8192]{1,0:T(8,128)(2,1)S(1)} %collective-permute-done.9.refs_2_, ...), custom_call_target="tpu_custom_call" | custom-call | flops 4294967296 | bytes 35651584 | tf_op jit(solution)/shard_map/pallas_call | solution.py:217
  81.9 0.8 copy-done.2
  82.7 0.8 copy-done.13
  83.5 0.8 copy-done.12
  84.3 4.8 %shard_map.68 = (bf16[32,2048]{1,0:T(8,128)(2,1)}, bf16[32,2048]{1,0:T(8,128)(2,1)}, bf16[32,2048]{1,0:T(8,128)(2,1)}, bf16[32,2048]{1,0:T(8,128)(2,1)}, bf16[32...) custom-call(s32[2]{0:T(128)} %copy-done.8, ...), custom_call_target="tpu_custom_call" | custom-call | flops 536870912 | bytes 2097152 | tf_op jit(solution)/shard_map/pallas_call | solution.py:292
  89.1 2.1 %collective-permute-start.14 = (bf16[32,2048]{1,0:T(8,128)(2,1)}, bf16[32,2048]{1,0:T(8,128)(2,1)S(1)}, u32[]{:S(2)}, u32[]{:S(2)}) collective-permute-start(bf16[32,2048]{1,0:T(8,128)(2,1)} %get-tuple-element.28), channel_id=1, source_target_pairs={{0,2},{2,0},{4,6},{6,4},{8,10},{10,8},{12,14},{14,12},{1,3},{3,1},... | collective-permute-start | bytes 393224 | tf_op jit(solution)/shard_map/ppermute | solution.py:441
  91.2 1.5 %collective-permute-start.15 = (bf16[32,2048]{1,0:T(8,128)(2,1)}, bf16[32,2048]{1,0:T(8,128)(2,1)S(1)}, u32[]{:S(2)}, u32[]{:S(2)}) collective-permute-start(bf16[32,2048]{1,0:T(8,128)(2,1)} %get-tuple-element.29), channel_id=1, source_target_pairs={{0,4},{2,6},{4,0},{6,2},{8,12},{10,14},{12,8},{14,10},{1,5},{3,7},... | collective-permute-start | bytes 393224 | tf_op jit(solution)/shard_map/ppermute | solution.py:441
  92.6 0.1 collective-permute-start.16
  92.7 2.8 %collective-permute-start.17 = (bf16[32,2048]{1,0:T(8,128)(2,1)}, bf16[32,2048]{1,0:T(8,128)(2,1)S(1)}, u32[]{:S(2)}, u32[]{:S(2)}) collective-permute-start(bf16[32,2048]{1,0:T(8,128)(2,1)} %get-tuple-element.31), channel_id=1, source_target_pairs={{0,8},{2,10},{4,12},{6,14},{8,0},{10,2},{12,4},{14,6},{1,9},{3,11}... | collective-permute-start | bytes 393224 | tf_op jit(solution)/shard_map/ppermute | solution.py:441
  95.6 1.5 %collective-permute-start.18 = (bf16[32,2048]{1,0:T(8,128)(2,1)}, bf16[32,2048]{1,0:T(8,128)(2,1)S(1)}, u32[]{:S(2)}, u32[]{:S(2)}) collective-permute-start(bf16[32,2048]{1,0:T(8,128)(2,1)} %get-tuple-element.32), channel_id=1, source_target_pairs={{0,10},{2,8},{4,14},{6,12},{8,2},{10,0},{12,6},{14,4},{1,11},{3,9}... | collective-permute-start | bytes 393224 | tf_op jit(solution)/shard_map/ppermute | solution.py:441
  97.0 3.3 %collective-permute-start.12 = (bf16[32,2048]{1,0:T(8,128)(2,1)}, bf16[32,2048]{1,0:T(8,128)(2,1)S(1)}, u32[]{:S(2)}, u32[]{:S(2)}) collective-permute-start(bf16[32,2048]{1,0:T(8,128)(2,1)} %get-tuple-element.25), channel_id=1, source_target_pairs={{0,12},{2,14},{4,8},{6,10},{8,4},{10,6},{12,0},{14,2},{1,13},{3,15... | collective-permute-start | bytes 393224 | tf_op jit(solution)/shard_map/ppermute | solution.py:441
  100.3 1.9 %collective-permute-done.15.refs_2_ = bf16[32,2048]{1,0:T(8,128)(2,1)S(1)} collective-permute-done((bf16[32,2048]{1,0:T(8,128)(2,1)}, bf16[32,2048]{1,0:T(8,128)(2,1)S(1)}, u32[]{:S(2)}, u32[]{:S(2)}) %collective-permute-start.15) | collective-permute-done | bytes 131104 | tf_op jit(solution)/shard_map/ppermute | solution.py:441
  102.2 0.6 collective-permute-start.13
  102.8 0.3 collective-permute-done.16.refs_3_
  103.1 12.2 %collective-permute-done.18.refs_5_ = bf16[32,2048]{1,0:T(8,128)(2,1)S(1)} collective-permute-done((bf16[32,2048]{1,0:T(8,128)(2,1)}, bf16[32,2048]{1,0:T(8,128)(2,1)S(1)}, u32[]{:S(2)}, u32[]{:S(2)}) %collective-permute-start.18) | collective-permute-done | bytes 131104 | tf_op jit(solution)/shard_map/ppermute | solution.py:441
  115.3 0.9 copy-done.7
  116.2 1.5 %shard_map.69.refs_2_ = bf16[32,16384]{1,0:T(8,128)(2,1)} custom-call(s32[2]{0:T(128)S(1)} %copy-done.11, bf16[32,2048]{1,0:T(8,128)(2,1)S(1)} %copy-done.7, bf16[32,2048]{1,0:T(8,128)(2,1)S(1)} %collective-permute-done.14.refs_1_, bf16[32,2048]{1,0:T(8,128)(2,1)S(1)} %collective-permute-done.15.refs_2_, ...), custom_call_target="tpu_custom_call" | custom-call | tf_op jit(solution)/shard_map/pallas_call | solution.py:359
  117.7 1.3 %shard_map.70 = bf16[32,16384]{1,0:T(8,128)(2,1)} custom-call(s32[2]{0:T(128)S(1)} %copy-done.11, bf16[32,2048]{1,0:T(8,128)(2,1)S(1)} %collective-permute-done.12.refs_0_, bf16[32,2048]{1,0:T(8,128)(2,1)S(1)} %collective-permute-done.13.refs_1_, bf16[32,16384]{1,0:T(8,128)(2,1)} %shard_map.69.refs_2_), custom_call_target="tpu_custom_call", output_to_operand_aliasing={{}: (3, {})} | custom-call | tf_op jit(solution)/shard_map/pallas_call | solution.py:359
  (37 shorter events, 0.1 us)
Async XLA Ops:
  0.0 62.2 %copy-start.1 = (bf16[1,8192,64]{1,2,0:T(8,128)(2,1)S(1)}, bf16[1,8192,64]{1,2,0:T(8,128)(2,1)}, u32[]{:S(2)}) copy-start(bf16[1,8192,64]{1,2,0:T(8,128)(2,1)} %param.8) | copy-start | bytes 3145732
  0.0 15.2 %collective-permute-start.6 = (bf16[32,8192]{1,0:T(8,128)(2,1)}, bf16[32,8192]{1,0:T(8,128)(2,1)S(1)}, u32[]{:S(2)}, u32[]{:S(2)}) collective-permute-start(bf16[32,8192]{1,0:T(8,128)(2,1)} %refs_0_.1), channel_id=1, source_target_pairs={{4,0},{8,4},{12,8},{14,12},{10,14},{6,10},{2,6},{0,2},{5,1},{9,5},... | collective-permute-start | bytes 1572872 | tf_op jit(solution)/shard_map/ppermute | solution.py:408
  3.0 13.9 %collective-permute-start.4 = (bf16[32,8192]{1,0:T(8,128)(2,1)}, bf16[32,8192]{1,0:T(8,128)(2,1)S(1)}, u32[]{:S(2)}, u32[]{:S(2)}) collective-permute-start(bf16[32,8192]{1,0:T(8,128)(2,1)} %refs_0_.1), channel_id=1, source_target_pairs={{0,4},{4,8},{8,12},{12,14},{14,10},{10,6},{6,2},{2,0},{1,5},{5,9},... | collective-permute-start | bytes 1572872 | tf_op jit(solution)/shard_map/ppermute | solution.py:407
  15.2 13.1 %collective-permute-start.7 = (bf16[32,8192]{1,0:T(8,128)(2,1)S(1)}, bf16[32,8192]{1,0:T(8,128)(2,1)S(1)}, u32[]{:S(2)}, u32[]{:S(2)}) collective-permute-start(bf16[32,8192]{1,0:T(8,128)(2,1)S(1)} %collective-permute-done.6.refs_2_), channel_id=1, source_target_pairs={{4,0},{8,4},{12,8},{14,12},{10,14},{6,10},{2,6},{0,2},{5,1},{9,5},... | collective-permute-start | bytes 1572872 | tf_op jit(solution)/shard_map/ppermute | solution.py:408
  16.8 12.8 %copy-start.4 = (bf16[32,8192]{1,0:T(8,128)(2,1)}, bf16[32,8192]{1,0:T(8,128)(2,1)S(1)}, u32[]{:S(2)}) copy-start(bf16[32,8192]{1,0:T(8,128)(2,1)S(1)} %collective-permute-done.4.refs_1_) | copy-start | bytes 1572868
  16.9 12.8 %collective-permute-start.5 = (bf16[32,8192]{1,0:T(8,128)(2,1)S(1)}, bf16[32,8192]{1,0:T(8,128)(2,1)}, u32[]{:S(2)}, u32[]{:S(2)}) collective-permute-start(bf16[32,8192]{1,0:T(8,128)(2,1)S(1)} %collective-permute-done.4.refs_1_), channel_id=1, source_target_pairs={{0,4},{4,8},{8,12},{12,14},{14,10},{10,6},{6,2},{2,0},{1,5},{5,9},... | collective-permute-start | bytes 1572872 | tf_op jit(solution)/shard_map/ppermute | solution.py:407
  17.3 1.1 copy-start.8
  17.3 1.1 collective-permute-start
  18.4 0.6 copy-start.14
  21.5 40.7 %copy-start.10 = (s32[2]{0:T(128)S(1)}, s32[2]{0:T(128)}, u32[]{:S(2)}) copy-start(s32[2]{0:T(128)} %copy-done.8) | copy-start | bytes 28
  21.5 33.5 %all-to-all-start = ((bf16[8,16,2048]{2,1,0:T(8,128)(2,1)}), bf16[8,16,2048]{2,1,0:T(8,128)(2,1)}, u32[]{:S(2)}, u32[]{:S(2)}) async-start(bf16[8,16,2048]{2,1,0:T(8,128)(2,1)} %shard_map.64), calls=%async_computation | async-start | bytes 1048576 | tf_op jit(solution)/shard_map/all_to_all | solution.py:422
  28.3 21.6 %collective-permute-start.9 = (bf16[32,8192]{1,0:T(8,128)(2,1)S(1)}, bf16[32,8192]{1,0:T(8,128)(2,1)S(1)}, u32[]{:S(2)}, u32[]{:S(2)}) collective-permute-start(bf16[32,8192]{1,0:T(8,128)(2,1)S(1)} %collective-permute-done.7.refs_0_), channel_id=1, source_target_pairs={{4,0},{8,4},{12,8},{14,12},{10,14},{6,10},{2,6},{0,2},{5,1},{9,5},... | collective-permute-start | bytes 1572872 | tf_op jit(solution)/shard_map/ppermute | solution.py:408
  29.6 20.3 %collective-permute-start.8 = (bf16[32,8192]{1,0:T(8,128)(2,1)}, bf16[32,8192]{1,0:T(8,128)(2,1)S(1)}, u32[]{:S(2)}, u32[]{:S(2)}) collective-permute-start(bf16[32,8192]{1,0:T(8,128)(2,1)} %collective-permute-done.5.refs_3_), channel_id=1, source_target_pairs={{0,4},{4,8},{8,12},{12,14},{14,10},{10,6},{6,2},{2,0},{1,5},{5,9},... | collective-permute-start | bytes 1572872 | tf_op jit(solution)/shard_map/ppermute | solution.py:407
  31.1 1.2 %copy-start = (bf16[1,8192,64]{1,2,0:T(8,128)(2,1)S(1)}, bf16[1,8192,64]{1,2,0:T(8,128)(2,1)}, u32[]{:S(2)}) copy-start(bf16[1,8192,64]{1,2,0:T(8,128)(2,1)} %param.8) | copy-start | bytes 3145732
  32.4 1.0 copy-start.3
  33.4 1.0 copy-start.5
  34.5 0.6 copy-start.9
  35.1 80.2 %copy-start.11 = (s32[2]{0:T(128)S(1)}, s32[2]{0:T(128)}, u32[]{:S(2)}) copy-start(s32[2]{0:T(128)} %copy-done.8) | copy-start | bytes 28
  47.8 6.4 %copy-start.6 = (bf16[128,2048]{1,0:T(8,128)(2,1)}, bf16[128,2048]{1,0:T(8,128)(2,1)S(1)}, u32[]{:S(2)}) copy-start(bf16[128,2048]{1,0:T(8,128)(2,1)S(1)} %get-tuple-element.20.refs_4_) | copy-start | bytes 1572868
  49.9 9.1 %collective-permute-start.10 = (bf16[16,8192]{1,0:T(8,128)(2,1)S(1)}, bf16[16,8192]{1,0:T(8,128)(2,1)S(1)}, u32[]{:S(2)}, u32[]{:S(2)}) collective-permute-start(bf16[16,8192]{1,0:T(8,128)(2,1)S(1)} %slice.6), channel_id=1, source_target_pairs={{0,4},{4,8},{8,12},{12,14},{14,10},{10,6},{6,2},{2,0},{1,5},{5,9},... | collective-permute-start | bytes 786440 | tf_op jit(solution)/shard_map/ppermute | solution.py:416
  55.0 7.2 %collective-permute-start.11 = (bf16[16,8192]{1,0:T(8,128)(2,1)}, bf16[16,8192]{1,0:T(8,128)(2,1)S(1)}, u32[]{:S(2)}, u32[]{:S(2)}) collective-permute-start(bf16[16,8192]{1,0:T(8,128)(2,1)} %slice.7), channel_id=1, source_target_pairs={{4,0},{8,4},{12,8},{14,12},{10,14},{6,10},{2,6},{0,2},{5,1},{9,5},... | collective-permute-start | bytes 786440 | tf_op jit(solution)/shard_map/ppermute | solution.py:417
  55.0 14.4 %collective-permute-start.1 = (bf16[8,16,2048]{2,1,0:T(8,128)(2,1)}, bf16[8,16,2048]{2,1,0:T(8,128)(2,1)}, u32[]{:S(2)}, u32[]{:S(2)}) collective-permute-start(bf16[8,16,2048]{2,1,0:T(8,128)(2,1)} %all-to-all-done.refs_0_), channel_id=1, source_target_pairs={{0,16},{16,0},{1,17},{17,1},{2,18},{18,2},{3,19},{19,3},{4,20},{20... | collective-permute-start | bytes 1572872 | tf_op jit(solution)/shard_map/ppermute | solution.py:427
  64.7 18.8 %all-to-all-start.1 = ((bf16[8,256,128]{2,1,0:T(8,128)(2,1)}), bf16[8,256,128]{2,1,0:T(8,128)(2,1)S(1)}, u32[]{:S(2)}, u32[]{:S(2)}) async-start(bf16[8,256,128]{2,1,0:T(8,128)(2,1)} %shard_map.66), calls=%async_computation.1 | async-start | bytes 1048576 | tf_op jit(solution)/shard_map/all_to_all | solution.py:432
  69.3 13.3 %collective-permute-start.2 = (bf16[8,16,2048]{2,1,0:T(8,128)(2,1)}, bf16[8,16,2048]{2,1,0:T(8,128)(2,1)S(1)}, u32[]{:S(2)}, u32[]{:S(2)}) collective-permute-start(bf16[8,16,2048]{2,1,0:T(8,128)(2,1)} %all-to-all-done.refs_0_), channel_id=1, source_target_pairs={{0,1},{1,0},{2,3},{3,2},{4,5},{5,4},{6,7},{7,6},{8,9},{9,8},{10,11... | collective-permute-start | bytes 1572872 | tf_op jit(solution)/shard_map/ppermute | solution.py:427
  69.4 14.1 %collective-permute-start.3 = (bf16[8,16,2048]{2,1,0:T(8,128)(2,1)}, bf16[8,16,2048]{2,1,0:T(8,128)(2,1)}, u32[]{:S(2)}, u32[]{:S(2)}) collective-permute-start(bf16[8,16,2048]{2,1,0:T(8,128)(2,1)} %collective-permute-done.1.refs_1_), channel_id=1, source_target_pairs={{0,1},{1,0},{2,3},{3,2},{4,5},{5,4},{6,7},{7,6},{8,9},{9,8},{10,11... | collective-permute-start | bytes 1572872 | tf_op jit(solution)/shard_map/ppermute | solution.py:427
  81.9 0.8 copy-start.2
  82.7 0.8 copy-start.13
  83.5 0.8 copy-start.12
  89.1 7.9 %collective-permute-start.14 = (bf16[32,2048]{1,0:T(8,128)(2,1)}, bf16[32,2048]{1,0:T(8,128)(2,1)S(1)}, u32[]{:S(2)}, u32[]{:S(2)}) collective-permute-start(bf16[32,2048]{1,0:T(8,128)(2,1)} %get-tuple-element.28), channel_id=1, source_target_pairs={{0,2},{2,0},{4,6},{6,4},{8,10},{10,8},{12,14},{14,12},{1,3},{3,1},... | collective-permute-start | bytes 393224 | tf_op jit(solution)/shard_map/ppermute | solution.py:441
  91.2 11.1 %collective-permute-start.15 = (bf16[32,2048]{1,0:T(8,128)(2,1)}, bf16[32,2048]{1,0:T(8,128)(2,1)S(1)}, u32[]{:S(2)}, u32[]{:S(2)}) collective-permute-start(bf16[32,2048]{1,0:T(8,128)(2,1)} %get-tuple-element.29), channel_id=1, source_target_pairs={{0,4},{2,6},{4,0},{6,2},{8,12},{10,14},{12,8},{14,10},{1,5},{3,7},... | collective-permute-start | bytes 393224 | tf_op jit(solution)/shard_map/ppermute | solution.py:441
  92.6 10.5 %collective-permute-start.16 = (bf16[32,2048]{1,0:T(8,128)(2,1)}, bf16[32,2048]{1,0:T(8,128)(2,1)S(1)}, u32[]{:S(2)}, u32[]{:S(2)}) collective-permute-start(bf16[32,2048]{1,0:T(8,128)(2,1)} %get-tuple-element.30), channel_id=1, source_target_pairs={{0,6},{2,4},{4,2},{6,0},{8,14},{10,12},{12,10},{14,8},{1,7},{3,5},... | collective-permute-start | bytes 393224 | tf_op jit(solution)/shard_map/ppermute | solution.py:441
  92.7 10.4 %collective-permute-start.17 = (bf16[32,2048]{1,0:T(8,128)(2,1)}, bf16[32,2048]{1,0:T(8,128)(2,1)S(1)}, u32[]{:S(2)}, u32[]{:S(2)}) collective-permute-start(bf16[32,2048]{1,0:T(8,128)(2,1)} %get-tuple-element.31), channel_id=1, source_target_pairs={{0,8},{2,10},{4,12},{6,14},{8,0},{10,2},{12,4},{14,6},{1,9},{3,11}... | collective-permute-start | bytes 393224 | tf_op jit(solution)/shard_map/ppermute | solution.py:441
  95.6 19.7 %collective-permute-start.18 = (bf16[32,2048]{1,0:T(8,128)(2,1)}, bf16[32,2048]{1,0:T(8,128)(2,1)S(1)}, u32[]{:S(2)}, u32[]{:S(2)}) collective-permute-start(bf16[32,2048]{1,0:T(8,128)(2,1)} %get-tuple-element.32), channel_id=1, source_target_pairs={{0,10},{2,8},{4,14},{6,12},{8,2},{10,0},{12,6},{14,4},{1,11},{3,9}... | collective-permute-start | bytes 393224 | tf_op jit(solution)/shard_map/ppermute | solution.py:441
  97.0 20.6 %collective-permute-start.12 = (bf16[32,2048]{1,0:T(8,128)(2,1)}, bf16[32,2048]{1,0:T(8,128)(2,1)S(1)}, u32[]{:S(2)}, u32[]{:S(2)}) collective-permute-start(bf16[32,2048]{1,0:T(8,128)(2,1)} %get-tuple-element.25), channel_id=1, source_target_pairs={{0,12},{2,14},{4,8},{6,10},{8,4},{10,6},{12,0},{14,2},{1,13},{3,15... | collective-permute-start | bytes 393224 | tf_op jit(solution)/shard_map/ppermute | solution.py:441
  102.2 15.4 %collective-permute-start.13 = (bf16[32,2048]{1,0:T(8,128)(2,1)}, bf16[32,2048]{1,0:T(8,128)(2,1)S(1)}, u32[]{:S(2)}, u32[]{:S(2)}) collective-permute-start(bf16[32,2048]{1,0:T(8,128)(2,1)} %get-tuple-element.26), channel_id=1, source_target_pairs={{0,14},{2,12},{4,10},{6,8},{8,6},{10,4},{12,2},{14,0},{1,15},{3,13... | collective-permute-start | bytes 393224 | tf_op jit(solution)/shard_map/ppermute | solution.py:441
  115.3 0.9 copy-start.7
